TPU v7x, 32 devices: a whole 2x2x4 slice. The times are simulated.
32 devices in a mesh: section: 2 (over core), expert: 16 (over z, y, x).
Axes of the slice: x: 2, y: 2, z: 4, core: 2. Of those that a mesh axis runs over, the one named last changes fastest.
Arguments:
- hidden_in: bfloat16 [2, 2048, 2048], P('section', 'expert'), may hold values from -6 to 6
- target_rows: bfloat16 [2, 2048, 2048], P('section', 'expert'), may hold values from -6 to 6
- norm_gain: float32 [2048], replicated, may hold values from 0.25 to 1.75
- router_weight: bfloat16 [2048, 8], replicated, may hold values from -0.125 to 0.125
- w_up: bfloat16 [16, 2048, 2048], P('expert', None, 'section'), may hold values from -0.125 to 0.125
- w_down: bfloat16 [16, 2048, 2048], P('expert', 'section'), may hold values from -0.09375 to 0.09375
- routes: int32 [2, 2048, 2], P('section', 'expert'), may hold values from 0 to 7, all different within a row; in each aligned block of 128 rows (0 to 127, 128 to 255, ..., all dimensions but the last counted through in order) at most 48 rows name the same one
- pair_ids: int32 [2, 2048], P('section', 'expert'), may hold values from 0 to 63, never falling along the last dimension, each value on 1 to 96 neighbouring positions
Outputs:
- layer_out: bfloat16 [2, 2048, 2048], P('section', 'expert')
- dual_score: float32 [64], P(('section', 'expert'))
Inputs may be any that keep to these rules, and one draw needn't show every extreme that they name: `routes`: within each aligned block of 128 rows of one direction no expert is named more than 48 times; the two experts of a row differ. `pair_ids`: never falling along each direction; every pair from 0 to 63 has 1 to 96 tokens in each direction.
All inputs are finite; a program needn't handle non-finite values.
Results may differ from a plain program's by a relative error of at most 0.014.
Values may be sent and summed in bfloat16 or wider, within the bound.
No kernel may reach another device: no remote copies, remote signals or barrier semaphores. Data moves between devices by JAX's collectives and lax.ppermute only.
A program may use at most 128 MiB of HBM per device.

v0:
```python
import math

import jax
import jax.numpy as jnp
from jax import lax
from jax.sharding import PartitionSpec as P

PAIR_DEV = 2


def partner_2(value, axis, stride):
    mask = 2**stride
    pairs = [(source, source ^ mask) for source in range(lax.axis_size(axis))]
    return lax.ppermute(value, axis, pairs)


def normalize(values, norm_gain):
    center = jnp.mean(values, axis=-1, keepdims=True)
    shifted = values - center
    spread = jnp.mean(shifted * shifted, axis=-1, keepdims=True)
    return shifted * lax.rsqrt(spread + 1e-05) * norm_gain


def apply_units(rows_in, up_part, down_part):
    features = rows_in.shape[-1]
    flat_rows = rows_in.reshape(-1, features)
    hidden = jnp.maximum(
        jnp.dot(flat_rows, up_part, preferred_element_type=jnp.float32), 0.0
    ).astype(jnp.bfloat16)
    result = jnp.dot(hidden, down_part, preferred_element_type=jnp.float32)
    return result.reshape(rows_in.shape[:-1] + (down_part.shape[-1],))


def expert_work(rows_in, up_part, down_part, partner):
    result = apply_units(rows_in, up_part, down_part) + apply_units(rows_in, partner[0], partner[1])
    return result


def local(hidden_in, target_rows, norm_gain, router_weight, w_up, w_down, routes, pair_ids):
    tok_rows = hidden_in.shape[1]
    features = hidden_in.shape[2]
    experts = router_weight.shape[1]
    capacity = 3 * tok_rows // experts
    residual = hidden_in[0].astype(jnp.float32)
    normed = normalize(residual, norm_gain).astype(jnp.bfloat16)
    logits = jnp.dot(normed, router_weight, preferred_element_type=jnp.float32)
    chosen = routes[0]
    picked = jnp.take_along_axis(logits, chosen, axis=1)
    gate_one = 1.0 / (1.0 + jnp.exp(picked[:, 1] - picked[:, 0]))
    gate_two = 1.0 / (1.0 + jnp.exp(picked[:, 0] - picked[:, 1]))
    flat_routes = chosen.reshape(-1)
    member = (flat_routes[:, None] == jnp.arange(experts, dtype=jnp.int32)[None, :]).astype(
        jnp.int32
    )
    earlier = jnp.cumsum(member, axis=0) - member
    slot_pos = jnp.sum(earlier * member, axis=1)
    targets = (flat_routes * capacity + slot_pos).reshape(tok_rows, 2)
    positions = jnp.arange(experts * capacity, dtype=jnp.int32)[:, None]
    placing = ((positions == targets[None, :, 0]) | (positions == targets[None, :, 1])).astype(
        jnp.bfloat16
    )
    buffer_rows = jnp.dot(placing, normed, preferred_element_type=jnp.float32).astype(jnp.bfloat16)
    partner = partner_2((w_up[0], w_down[0]), "section", 0)
    sending = jnp.repeat(buffer_rows.reshape(experts, capacity, features), 2, axis=0)
    partials = expert_work(
        lax.all_to_all(sending, "expert", split_axis=0, concat_axis=0, tiled=True)[None],
        w_up[0],
        w_down[0],
        partner,
    )[0]
    returned = lax.all_to_all(partials, "expert", split_axis=0, concat_axis=0, tiled=True)
    expert_rows = (
        jnp.sum(returned.reshape(experts, 2, capacity, features), axis=1)
        .astype(jnp.bfloat16)
        .reshape(experts * capacity, features)
    )
    routed_one = expert_rows[targets[:, 0]].astype(jnp.float32)
    routed_two = expert_rows[targets[:, 1]].astype(jnp.float32)
    combined = residual + gate_one[:, None] * routed_one + gate_two[:, None] * routed_two
    layer_out = combined.astype(jnp.bfloat16)
    token_score = jnp.sum(
        layer_out.astype(jnp.float32) * target_rows[0].astype(jnp.float32), axis=1
    ) / math.sqrt(features)
    pair_count = PAIR_DEV * lax.axis_size("section") * lax.axis_size("expert")
    belongs = (pair_ids[0][:, None] == jnp.arange(pair_count, dtype=jnp.int32)[None, :]).astype(
        jnp.float32
    )
    totals = jnp.dot(token_score, belongs, precision=lax.Precision.HIGHEST)
    counts = jnp.sum(belongs, axis=0)
    own_column = (jnp.arange(2, dtype=jnp.int32) == lax.axis_index("section")).astype(jnp.float32)
    summed, counted = (
        lax.psum_scatter(
            totals[:, None] * own_column[None, :],
            ("section", "expert"),
            scatter_dimension=0,
            tiled=True,
        ),
        lax.psum_scatter(
            counts[:, None] * own_column[None, :],
            ("section", "expert"),
            scatter_dimension=0,
            tiled=True,
        ),
    )
    entropy = -summed / counted
    dual_score = jnp.abs(entropy[:, 0] - entropy[:, 1]) + 0.5 * (entropy[:, 0] + entropy[:, 1])
    return (layer_out[None], dual_score)


def solution(mesh):
    in_specs = (
        P("section", "expert", None),
        P("section", "expert", None),
        P(),
        P(),
        P("expert", None, "section"),
        P("expert", "section", None),
        P("section", "expert", None),
        P("section", "expert"),
    )
    out_specs = (P("section", "expert", None), P(("section", "expert")))
    return jax.shard_map(local, mesh=mesh, in_specs=in_specs, out_specs=out_specs, check_vma=False)
```

profile of v0, /device:TPU:0, one launch (start us, length us, event | category | flops | bytes accessed | tf_op | source)
XLA Modules:
  0.0 317.0 jit_solution(3559049377357560463)
XLA Ops:
  0.6 0.0 copy-start
  0.6 0.8 copy.28
  1.4 0.1 eq.85
  1.6 0.1 eq.81
  1.7 0.6 reduce-window.6
  2.3 0.2 slice_reduce_fusion
  2.6 0.1 fusion.23
  2.7 0.1 reduce_sum.59
  2.8 0.1 copy.30
  2.9 0.7 fusion.28
  3.6 1.2 convert_reduce_fusion
  4.8 1.3 fusion.6
  6.1 1.7 convolution_convert_fusion
  7.9 2.1 broadcast_in_dim.7
  9.9 8.3 %all-to-all-start = ((bf16[16,48,2048]{2,1,0:T(8,128)(2,1)}), bf16[16,48,2048]{2,1,0:T(8,128)(2,1)S(1)}, u32[]{:S(2)}, u32[]{:S(2)}) async-start(bf16[16,48,2048]{2,1,0:T(8,128)(2,1)} %bitcast.9), calls=%async_computation | async-start | bytes 6291456 | tf_op jit(solution)/shard_map/all_to_all | solution.py:66
  18.3 0.1 collective-permute-start
  18.3 0.5 collective-permute-start.1
  18.8 60.4 %all-to-all-done = bf16[16,48,2048]{2,1,0:T(8,128)(2,1)S(1)} async-done(((bf16[16,48,2048]{2,1,0:T(8,128)(2,1)}), bf16[16,48,2048]{2,1,0:T(8,128)(2,1)S(1)}, u32[]{:S(2)}, u32[]{:S(2)}) %all-to-all-start) | async-done | bytes 3145760 | tf_op jit(solution)/shard_map/all_to_all | solution.py:66
  79.2 5.7 %maximum_convert_fusion.1 = bf16[768,1024]{1,0:T(8,128)(2,1)S(1)} fusion(bf16[768,2048]{1,0:T(8,128)(2,1)S(1)} %bitcast.107, bf16[1,2048,1024]{2,1,0:T(8,128)(2,1)} %param.12), kind=kOutput, calls=%fused_computation.7 | convolution fusion | flops 3222798336 | bytes 8912896 | tf_op jit(solution)/shard_map/dot_general | solution.py:28
  84.9 0.0 copy-done.4
  84.9 5.4 %fusion = f32[16,48,2048]{2,1,0:T(8,128)} fusion(bf16[16,48,1024]{2,1,0:T(8,128)(2,1)S(1)} %bitcast.113, bf16[1,1024,2048]{2,1,0:T(8,128)(2,1)S(1)} %copy-done.4), kind=kOutput, calls=%fused_computation.4 | convolution fusion | flops 3221225472 | bytes 12058624 | tf_op jit(solution)/shard_map/dot_general | solution.py:30
  90.3 0.0 collective-permute-done
  90.4 0.0 collective-permute-done.1
  90.4 12.8 %fusion.16 = f32[768,2048]{1,0:T(8,128)} fusion(bf16[1024,2048]{1,0:T(8,128)(2,1)} %collective-permute-done.1, bf16[768,2048]{1,0:T(8,128)(2,1)S(1)} %bitcast.108, bf16[2048,1024]{1,0:T(8,128)(2,1)} %collective-permute-done), kind=kOutput, calls=%fused_computation.32 | convolution fusion | flops 6444023808 | bytes 17825792 | tf_op jit(solution)/shard_map/dot_general | solution.py:30
  103.1 9.2 %add.90 = f32[16,48,2048]{2,1,0:T(8,128)} add(f32[16,48,2048]{2,1,0:T(8,128)} %fusion, f32[16,48,2048]{2,1,0:T(8,128)} %bitcast.106) | non-fusion elementwise | flops 1572864 | bytes 18874368 | tf_op jit(solution)/shard_map/add | solution.py:35
  112.3 15.2 %all-to-all-start.1 = ((f32[16,48,2048]{2,1,0:T(8,128)}), f32[16,48,2048]{2,1,0:T(8,128)}, u32[]{:S(2)}, u32[]{:S(2)}) async-start(f32[16,48,2048]{2,1,0:T(8,128)} %add.90), calls=%async_computation.1 | async-start | bytes 12582912 | tf_op jit(solution)/shard_map/all_to_all | solution.py:71
  127.5 0.0 copy-done.2
  127.5 0.1 copy.26
  127.6 0.1 reshape.217
  127.8 0.0 copy-done
  127.8 0.0 copy-done.1
  127.8 0.0 copy-done.3
  127.8 0.3 fusion.36
  128.1 1.4 gather_fusion.2
  129.5 0.1 reshape.220
  129.7 0.1 copy.27
  129.8 0.1 convert_reduce_fusion.1
  129.9 113.8 %all-to-all-done.1 = f32[16,48,2048]{2,1,0:T(8,128)} async-done(((f32[16,48,2048]{2,1,0:T(8,128)}), f32[16,48,2048]{2,1,0:T(8,128)}, u32[]{:S(2)}, u32[]{:S(2)}) %all-to-all-start.1) | async-done | bytes 6291488 | tf_op jit(solution)/shard_map/all_to_all | solution.py:71
  243.8 3.7 %bitcast_reduce_fusion = bf16[8,48,2048]{2,1,0:T(8,128)(2,1)S(1)} fusion(f32[16,48,2048]{2,1,0:T(8,128)} %all-to-all-done.1), kind=kLoop, calls=%fused_computation.3 | loop fusion | flops 786432 | bytes 7864320 | tf_op jit(solution)/shard_map/reduce_sum | solution.py:73
  247.4 0.9 gather_fusion
  248.4 0.9 gather_fusion.1
  249.3 1.2 fusion.12
  250.5 1.5 fusion.15
  252.0 0.1 convolution_bitcast_fusion
  252.2 0.1 broadcast_multiply_fusion.1
  252.2 64.1 %all-reduce.2 = (f32[64,2]{0,1:T(2,128)S(1)}, f32[64,2]{0,1:T(2,128)S(1)}) all-reduce(f32[64,2]{0,1:T(2,128)S(1)} %get-tuple-element.11, f32[64,2]{0,1:T(2,128)S(1)} %get-tuple-element.10), channel_id=3, replica_groups=mesh['section'=2,'expert'=16] {'section','expert'}, use_global_device_ids=true, to_apply=%region_9.10.clone | all-reduce | flops 256 | bytes 2048
  316.4 0.1 dynamic-slice_divide_fusion
  316.4 0.5 add_bitcast_fusion
  (17 shorter events, 0.1 us)
Async XLA Ops:
  0.6 127.1 %copy-start = (bf16[2048,8]{0,1:T(8,128)(2,1)S(1)}, bf16[2048,8]{0,1:T(8,128)(2,1)}, u32[]{:S(2)}) copy-start(bf16[2048,8]{0,1:T(8,128)(2,1)} %param.11) | copy-start | bytes 98308
  9.9 69.3 %all-to-all-start = ((bf16[16,48,2048]{2,1,0:T(8,128)(2,1)}), bf16[16,48,2048]{2,1,0:T(8,128)(2,1)S(1)}, u32[]{:S(2)}, u32[]{:S(2)}) async-start(bf16[16,48,2048]{2,1,0:T(8,128)(2,1)} %bitcast.9), calls=%async_computation | async-start | bytes 6291456 | tf_op jit(solution)/shard_map/all_to_all | solution.py:66
  18.3 72.1 %collective-permute-start = (bf16[2048,1024]{1,0:T(8,128)(2,1)}, bf16[2048,1024]{1,0:T(8,128)(2,1)}, u32[]{:S(2)}, u32[]{:S(2)}) collective-permute-start(bf16[2048,1024]{1,0:T(8,128)(2,1)} %bitcast.109), channel_id=1, source_target_pairs={{0,16},{16,0},{1,17},{17,1},{2,18},{18,2},{3,19},{19,3},{4,20},{20... | collective-permute-start | bytes 12582920 | tf_op jit(solution)/shard_map/ppermute | solution.py:14
  18.3 72.0 %collective-permute-start.1 = (bf16[1024,2048]{1,0:T(8,128)(2,1)}, bf16[1024,2048]{1,0:T(8,128)(2,1)}, u32[]{:S(2)}, u32[]{:S(2)}) collective-permute-start(bf16[1024,2048]{1,0:T(8,128)(2,1)} %bitcast.110), channel_id=1, source_target_pairs={{0,16},{16,0},{1,17},{17,1},{2,18},{18,2},{3,19},{19,3},{4,20},{20... | collective-permute-start | bytes 12582920 | tf_op jit(solution)/shard_map/ppermute | solution.py:14
  79.2 5.8 %copy-start.4 = (bf16[1,1024,2048]{2,1,0:T(8,128)(2,1)S(1)}, bf16[1,1024,2048]{2,1,0:T(8,128)(2,1)}, u32[]{:S(2)}) copy-start(bf16[1,1024,2048]{2,1,0:T(8,128)(2,1)} %param.13) | copy-start | bytes 12582916
  112.3 15.2 %copy-start.2 = (s32[1,128,2]{1,2,0:T(2,128)S(1)}, s32[1,128,2]{1,2,0:T(2,128)}, u32[]{:S(2)}) copy-start(s32[1,128,2]{1,2,0:T(2,128)} %param.14) | copy-start | bytes 3076
  112.3 15.5 %copy-start.1 = (bf16[1,128,2048]{2,1,0:T(8,128)(2,1)S(1)}, bf16[1,128,2048]{2,1,0:T(8,128)(2,1)}, u32[]{:S(2)}) copy-start(bf16[1,128,2048]{2,1,0:T(8,128)(2,1)} %param.8) | copy-start | bytes 1572868
  112.3 15.5 %copy-start.3 = (f32[2048]{0:T(1024)S(1)}, f32[2048]{0:T(1024)}, u32[]{:S(2)}) copy-start(f32[2048]{0:T(1024)} %param.10) | copy-start | bytes 24580
  112.3 131.4 %all-to-all-start.1 = ((f32[16,48,2048]{2,1,0:T(8,128)}), f32[16,48,2048]{2,1,0:T(8,128)}, u32[]{:S(2)}, u32[]{:S(2)}) async-start(f32[16,48,2048]{2,1,0:T(8,128)} %add.90), calls=%async_computation.1 | async-start | bytes 12582912 | tf_op jit(solution)/shard_map/all_to_all | solution.py:71
  128.1 1.6 copy-start.5
where the time goes:
time: 318 us; the launch traced here: 317 us
  waiting for transfers between devices  174 us (55%)
  blocking collectives  64.1 us (20%)
  matrix products  26.1 us (8%)
  starting transfers between devices  24.1 us (8%)
  other arithmetic  20.4 us (6%)
  local copies, waits for them, and re-layouts  7.28 us (2%)
    all_to_all x1, waiting for transfers between devices, local(): lax.all_to_all(partials, 'expert', split_axis=0, concat_axis=0, tiled=True)  114 us
    unnamed x1, blocking collectives  64.1 us
    all_to_all x1, waiting for transfers between devices, local(): lax.all_to_all(sending, 'expert', split_axis=0, concat_axis=0, tiled=True)  60.4 us
    dot_general x2, matrix products, apply_units(): result = jnp.dot(hidden, down_part, preferred_element_type=jnp.float32)  18.2 us
    all_to_all x1, starting transfers between devices, local(): lax.all_to_all(partials, 'expert', split_axis=0, concat_axis=0, tiled=True)  15.2 us
    add x1, other arithmetic, expert_work(): apply_units(rows_in, up_part, down_part)  9.16 us
    all_to_all x1, starting transfers between devices, local(): lax.all_to_all(sending, 'expert', split_axis=0, concat_axis=0, tiled=True)  8.31 us
  transfers between devices with their start and end apart: 4, of which 2 were waited for; matrix products, arithmetic and copies ran while one was open for 4% of the time, Pallas kernels for 0%

commit v1 on v0

v1 whole, which is shorter than its diff:
```python
import math

import jax
import jax.numpy as jnp
from jax import lax
from jax.experimental import pallas as pl
from jax.experimental.pallas import tpu as pltpu
from jax.sharding import PartitionSpec as P

PAIR_DEV = 2
LANES = 128
MIB = 1 << 20
VMEM = pl.BlockSpec(memory_space=pltpu.VMEM)


def normalize(values, norm_gain):
    center = jnp.mean(values, axis=-1, keepdims=True)
    shifted = values - center
    spread = jnp.mean(shifted * shifted, axis=-1, keepdims=True)
    return shifted * lax.rsqrt(spread + 1e-05) * norm_gain


def row_sum(values):
    return jnp.sum(values, axis=1, keepdims=True)


def place_body(capacity, hidden, other, gain, router, routes, other_routes, *outs):
    sends, weights = outs[:-1], outs[-1]
    experts = router.shape[1]
    tok_rows = hidden.shape[0]
    couples = experts // 2
    slots = experts * capacity
    side = lax.axis_index("section")
    group = lax.axis_index("expert") // 2
    expert_ids = lax.broadcasted_iota(jnp.int32, (tok_rows, experts), 1)
    before = (
        lax.broadcasted_iota(jnp.int32, (tok_rows, tok_rows), 0)
        > lax.broadcasted_iota(jnp.int32, (tok_rows, tok_rows), 1)
    ).astype(jnp.bfloat16)
    columns = lax.broadcasted_iota(jnp.int32, (tok_rows, slots), 1)
    rows, placing = [], []
    for turn, (values, chosen) in enumerate(((hidden, routes), (other, other_routes))):
        normed = normalize(values[...].astype(jnp.float32), gain[...]).astype(jnp.bfloat16)
        chosen = chosen[...]
        named = [chosen[:, k : k + 1] == expert_ids for k in range(2)]
        member = jnp.where(named[0] | named[1], 1.0, 0.0).astype(jnp.bfloat16)
        earlier = jnp.dot(before, member, preferred_element_type=jnp.float32)
        place = [row_sum(jnp.where(n, earlier, 0.0)).astype(jnp.int32) for n in named]
        step = [chosen[:, k : k + 1] ^ group for k in range(2)]
        mine = [(k & 1) == side for k in step]
        full = [(k >> 1) * (2 * capacity) + p for k, p in zip(step, place)]
        target = [jnp.where(m, f + turn * capacity, -1) for m, f in zip(mine, full)]
        placing.append(
            jnp.where((columns == target[0]) | (columns == target[1]), 1.0, 0.0).astype(jnp.bfloat16)
        )
        rows.append(normed)
        if turn == 0:
            logits = jnp.dot(normed, router[...], preferred_element_type=jnp.float32)
            picked = [row_sum(jnp.where(n, logits, 0.0)) for n in named]
            gates = (
                1.0 / (1.0 + jnp.exp(picked[1] - picked[0])),
                1.0 / (1.0 + jnp.exp(picked[0] - picked[1])),
            )
            wide = lax.broadcasted_iota(jnp.int32, weights.shape, 1)
            back = [
                jnp.where(m, f, slots + (k >> 1) * capacity + p)
                for m, f, k, p in zip(mine, full, step, place)
            ]
            weights[...] = jnp.where(wide == back[0], gates[0], 0.0) + jnp.where(
                wide == back[1], gates[1], 0.0
            )
    sent = lax.dot_general(
        jnp.concatenate(placing, axis=0),
        jnp.concatenate(rows, axis=0),
        (((0,), (0,)), ((), ())),
        preferred_element_type=jnp.float32,
    ).astype(jnp.bfloat16)
    span = sends[0].shape[0]
    for k, ref in enumerate(sends):
        ref[...] = sent[k * span : (k + 1) * span]


def expert_body(own, across, up, down, up_other, down_other, kept, sent, rows, total):
    step = pl.program_id(0)
    span = own.shape[0]

    @pl.when(step == 0)
    def _():
        rows[:span] = own[...]
        rows[span:] = across[...]

    part = None
    for up_part, down_part in ((up, down), (up_other, down_other)):
        hidden = jnp.maximum(
            jnp.dot(rows[...], up_part[...], preferred_element_type=jnp.float32), 0.0
        ).astype(jnp.bfloat16)
        product = jnp.dot(hidden, down_part[...], preferred_element_type=jnp.float32)
        part = product if part is None else part + product

    @pl.when(step == 0)
    def _():
        total[...] = part

    @pl.when(step > 0)
    def _():
        total[...] += part

    @pl.when(step == pl.num_programs(0) - 1)
    def _():
        kept[...] = total[:span]
        sent[...] = total[span:].astype(jnp.bfloat16)


def expert_work(own, across, up, down, up_other, down_other):
    span, features = own.shape
    units = up.shape[1]
    block = min(256, units)
    rows_spec = pl.BlockSpec((span, features), lambda i: (0, 0))
    up_spec = pl.BlockSpec((features, block), lambda i: (0, i))
    down_spec = pl.BlockSpec((block, features), lambda i: (i, 0))
    return pl.pallas_call(
        expert_body,
        grid=(units // block,),
        in_specs=[rows_spec, rows_spec, up_spec, down_spec, up_spec, down_spec],
        out_specs=[rows_spec, rows_spec],
        out_shape=[
            jax.ShapeDtypeStruct((span, features), jnp.float32),
            jax.ShapeDtypeStruct((span, features), jnp.bfloat16),
        ],
        scratch_shapes=[
            pltpu.VMEM((2 * span, features), jnp.bfloat16),
            pltpu.VMEM((2 * span, features), jnp.float32),
        ],
        compiler_params=pltpu.CompilerParams(vmem_limit_bytes=32 * MIB),
        cost_estimate=pl.CostEstimate(
            flops=16 * span * features * units,
            bytes_accessed=8 * features * units,
            transcendentals=0,
        ),
    )(own, across, up, down, up_other, down_other)


def combine_body(rounds, pair_rows, *refs):
    returned, crossed = refs[:rounds], refs[rounds : 2 * rounds]
    weights, hidden, target, pairs, layer_out, sums = refs[2 * rounds :]
    features = hidden.shape[1]
    span, half = returned[0].shape[0], crossed[0].shape[0]
    gate = weights[...]
    high = gate.astype(jnp.bfloat16)
    low = (gate - high.astype(jnp.float32)).astype(jnp.bfloat16)
    total = hidden[...].astype(jnp.float32)
    rows = jnp.concatenate([r[...] for r in returned + crossed], axis=0)
    total = total + (
        jnp.dot(high, rows, preferred_element_type=jnp.float32)
        + jnp.dot(low, rows, preferred_element_type=jnp.float32)
    )
    result = total.astype(jnp.bfloat16)
    layer_out[...] = result
    score = row_sum(result.astype(jnp.float32) * target[...].astype(jnp.float32)) / math.sqrt(features)
    lane = lax.broadcasted_iota(jnp.int32, (score.shape[0], LANES), 1)
    owner = lax.broadcasted_iota(jnp.int32, (pair_rows, score.shape[0]), 0) * PAIR_DEV
    gathered = None
    for k in range(PAIR_DEV):
        belongs = jnp.where(pairs[...] == owner + k, 1.0, 0.0)
        column = jnp.where(lane == k, score, 0.0) + jnp.where(lane == PAIR_DEV + k, 1.0, 0.0)
        one = jnp.dot(
            belongs, column, preferred_element_type=jnp.float32, precision=lax.Precision.HIGHEST
        )
        gathered = one if gathered is None else gathered + one
    sums[...] = gathered


def local(hidden_in, target_rows, norm_gain, router_weight, w_up, w_down, routes, pair_ids):
    tok_rows = hidden_in.shape[1]
    features = hidden_in.shape[2]
    experts = router_weight.shape[1]
    capacity = 3 * tok_rows // experts
    sections, chips = lax.axis_size("section"), lax.axis_size("expert")
    couples = experts // 2
    rounds = min(4, couples)
    each = couples // rounds
    span = each * 2 * capacity
    both = ("section", "expert")

    def over_section(value):
        return lax.ppermute(value, "section", [(0, 1), (1, 0)])

    def over_x(value):
        return lax.ppermute(value, "expert", [(i, i ^ 1) for i in range(chips)])

    def over_groups(value, index):
        parts = []
        for k in range(each):
            couple = index * each + k
            pairs = [
                (side * chips + i, side * chips + (i ^ (2 * (2 * couple + side))))
                for side in range(sections)
                for i in range(chips)
            ]
            part = value[k * 2 * capacity : (k + 1) * 2 * capacity]
            parts.append(lax.ppermute(part, both, pairs))
        return parts[0] if each == 1 else jnp.concatenate(parts, axis=0)

    other_hidden = over_section(hidden_in[0])
    other_routes = over_section(routes[0])
    sends = pl.pallas_call(
        lambda *refs: place_body(capacity, *refs),
        in_specs=[VMEM] * 6,
        out_specs=[VMEM] * (rounds + 1),
        out_shape=[jax.ShapeDtypeStruct((span, features), jnp.bfloat16)] * rounds
        + [jax.ShapeDtypeStruct((tok_rows, experts * capacity * 3 // 2), jnp.float32)],
        compiler_params=pltpu.CompilerParams(vmem_limit_bytes=32 * MIB),
    )(hidden_in[0], other_hidden, norm_gain[None], router_weight, routes[0], other_routes)
    sends, weights = sends[:-1], sends[-1]
    up, down = w_up[0], w_down[0]
    up_other, down_other = over_section(up), over_section(down)

    order = list(range(rounds))
    order = [order[k] for k in (2, 3, 1, 0)] if rounds == 4 else order[::-1]
    arrived = {k: over_groups(sends[k], k) for k in order}
    returned, crossed = {}, {}
    for k in (0, 2, 1, 3) if rounds == 4 else order:
        across = over_x(arrived[k])
        kept, sent = expert_work(arrived[k], across, up, down, up_other, down_other)
        summed = (kept + over_x(sent).astype(jnp.float32)).astype(jnp.bfloat16)
        returned[k] = over_groups(summed, k)
        crossed[k] = over_section(
            returned[k].reshape(each, 2, capacity, features)[:, 1].reshape(each * capacity, features)
        )
    layer_out, sums = pl.pallas_call(
        lambda *refs: combine_body(rounds, sections * chips, *refs),
        in_specs=[VMEM] * (2 * rounds + 4),
        out_specs=[VMEM] * 2,
        out_shape=[
            jax.ShapeDtypeStruct((tok_rows, features), jnp.bfloat16),
            jax.ShapeDtypeStruct((sections * chips, LANES), jnp.float32),
        ],
        compiler_params=pltpu.CompilerParams(vmem_limit_bytes=32 * MIB),
    )(
        *[returned[k] for k in range(rounds)],
        *[crossed[k] for k in range(rounds)],
        weights,
        hidden_in[0],
        target_rows[0],
        pair_ids,
    )
    owned = lax.all_to_all(sums, both, split_axis=0, concat_axis=0, tiled=True)
    owned = jnp.sum(owned.reshape(sections, chips, LANES), axis=1)
    entropy = -owned[:, :PAIR_DEV] / owned[:, PAIR_DEV : 2 * PAIR_DEV]
    dual_score = jnp.abs(entropy[0] - entropy[1]) + 0.5 * (entropy[0] + entropy[1])
    return (layer_out[None], dual_score)


def solution(mesh):
    in_specs = (
        P("section", "expert", None),
        P("section", "expert", None),
        P(),
        P(),
        P("expert", None, "section"),
        P("expert", "section", None),
        P("section", "expert", None),
        P("section", "expert"),
    )
    out_specs = (P("section", "expert", None), P(("section", "expert")))
    return jax.shard_map(local, mesh=mesh, in_specs=in_specs, out_specs=out_specs, check_vma=False)
```

time: 318 us -> 149 us (0.47)
  waiting for transfers between devices: 174 us -> 28.9 us
  blocking collectives: 64.1 us -> 16.7 us
  starting transfers between devices: 24.1 us -> 59.7 us
  Pallas kernels: 0 us -> 33.7 us
  matrix products: 26.1 us -> 0 us
  other arithmetic: 20.4 us -> 0.92 us
    all_to_all x2 -> x0, waiting for transfers between devices: 174 us -> none  [the longest x1 114 us: local(): lax.all_to_all(partials, 'expert', split_axis=0, concat_axis=0, tiled=True)]
    unnamed x1 -> x0, blocking collectives: 64.1 us -> none
    ppermute x2 -> x24, starting transfers between devices: 0.57 us -> 59.7 us  [the longest x8 29.1 us: over_section(): return lax.ppermute(value, 'section', [(0, 1), (1, 0)])]
    pallas_call x0 -> x6, Pallas kernels: none -> 33.7 us  [the longest x4 30.1 us: expert_work(): pl.pallas_call(expert_body, grid=(units // block,), in_specs=[rows_spec,...]
    ppermute x2 -> x24, waiting for transfers between devices: 0.01 us -> 28.9 us  [the longest x8 22.1 us: over_groups(): parts.append(lax.ppermute(part, both, pairs))]
    dot_general x6 -> x0, matrix products: 26.1 us -> none  [the longest x2 18.2 us: apply_units(): result = jnp.dot(hidden, down_part, preferred_element_type=jnp.float32)]
    all_to_all x2 -> x0, starting transfers between devices: 23.5 us -> none  [the longest x1 15.2 us: local(): lax.all_to_all(partials, 'expert', split_axis=0, concat_axis=0, tiled=True)]
    all_to_all x0 -> x1, blocking collectives: none -> 16.7 us  [local(): owned = lax.all_to_all(sums, both, split_axis=0, concat_axis=0, tiled=True)]
  transfers between devices with their start and end apart: 4 -> 24, of which waited for: 2 -> 6; matrix products, arithmetic and copies ran while one was open for 4% -> 1% of each run, Pallas kernels for 0% -> 21%
where the time goes in v1:
time: 149 us
  starting transfers between devices  59.7 us (40%)
  Pallas kernels  33.7 us (23%)
  waiting for transfers between devices  28.9 us (19%)
  blocking collectives  16.7 us (11%)
  local copies, waits for them, and re-layouts  8 us (5%)
    pallas_call x4, Pallas kernels, expert_work(): pl.pallas_call(expert_body, grid=(units // block,), in_specs=[rows_spec,...  30.1 us
    ppermute x8, starting transfers between devices, over_section(): return lax.ppermute(value, 'section', [(0, 1), (1, 0)])  29.1 us
    ppermute x8, waiting for transfers between devices, over_groups(): parts.append(lax.ppermute(part, both, pairs))  22.1 us
    ppermute x8, starting transfers between devices, over_groups(): parts.append(lax.ppermute(part, both, pairs))  21.4 us
    all_to_all x1, blocking collectives, local(): owned = lax.all_to_all(sums, both, split_axis=0, concat_axis=0, tiled=True)  16.7 us
    ppermute x8, starting transfers between devices, over_x(): return lax.ppermute(value, 'expert', [(i, i ^ 1) for i in range(chips)])  9.2 us
    unnamed x20, local copies, waits for them, and re-layouts  7.95 us
    ppermute x8, waiting for transfers between devices, over_section(): return lax.ppermute(value, 'section', [(0, 1), (1, 0)])  6.81 us
  transfers between devices with their start and end apart: 24, of which 6 were waited for; matrix products, arithmetic and copies ran while one was open for 1% of the time, Pallas kernels for 21%

profile of v1, /device:TPU:0, one launch (start us, length us, event | category | flops | bytes accessed | tf_op | source)
XLA Modules:
  0.0 148.8 jit_solution(5263478860509276315)
XLA Ops:
  0.6 0.5 collective-permute-start.4
  1.1 0.1 collective-permute-start.5
  1.2 0.4 collective-permute-start
  1.7 0.8 copy.12
  2.4 0.1 collective-permute-start.1
  2.6 1.0 copy.13.refs_3_
  3.6 5.2 %collective-permute-done.1.refs_5_ = s32[128,2]{1,0:T(8,128)S(1)} collective-permute-done((s32[128,2]{1,0:T(8,128)S(1)}, s32[128,2]{1,0:T(8,128)S(1)}, u32[]{:S(2)}, u32[]{:S(2)}) %collective-permute-start.1) | collective-permute-done | bytes 1056 | tf_op jit(solution)/shard_map/ppermute | solution.py:186
  8.8 0.2 collective-permute-done.refs_1_
  9.0 1.0 copy-done.4
  10.1 0.7 copy-done.7
  10.8 1.7 %shard_map.95 = (bf16[96,2048]{1,0:T(8,128)(2,1)S(1)}, bf16[96,2048]{1,0:T(8,128)(2,1)S(1)}, bf16[96,2048]{1,0:T(8,128)(2,1)S(1)}, bf16[96,2048]{1,0:T(8,128)(2,1)S(1)}, f32[128,576]{1,0:T(8,128)S(1)}) custom-call(bf16[128,2048]{1,0:T(8,128)(2,1)S(1)} %bitcast.38, bf16[128,2048]{1,0:T(8,128)(2,1)S(1)} %collective-permute-done.refs_1_, ...), custom_call_target="tpu_custom_call" | custom-call | tf_op jit(solution)/shard_map/pallas_call | solution.py:206
  12.5 0.7 collective-permute-start.2
  13.2 3.2 %collective-permute-start.8 = (bf16[96,2048]{1,0:T(8,128)(2,1)S(1)}, bf16[96,2048]{1,0:T(8,128)(2,1)S(1)}, u32[]{:S(2)}, u32[]{:S(2)}) collective-permute-start(bf16[96,2048]{1,0:T(8,128)(2,1)S(1)} %get-tuple-element.20), channel_id=1, source_target_pairs={{0,4},{1,5},{2,6},{3,7},{4,0},{5,1},{6,2},{7,3},{8,12},{9,13},{10,... | collective-permute-start | bytes 1179656 | tf_op jit(solution)/shard_map/ppermute | solution.py:201
  16.4 2.6 %collective-permute-start.12 = (bf16[96,2048]{1,0:T(8,128)(2,1)S(1)}, bf16[96,2048]{1,0:T(8,128)(2,1)S(1)}, u32[]{:S(2)}, u32[]{:S(2)}) collective-permute-start(bf16[96,2048]{1,0:T(8,128)(2,1)S(1)} %get-tuple-element.23), channel_id=1, source_target_pairs={{0,8},{1,9},{2,10},{3,11},{4,12},{5,13},{6,14},{7,15},{8,0},{9,1},... | collective-permute-start | bytes 1179656 | tf_op jit(solution)/shard_map/ppermute | solution.py:201
  19.0 12.1 %collective-permute-done.8.own = bf16[96,2048]{1,0:T(8,128)(2,1)S(1)} collective-permute-done((bf16[96,2048]{1,0:T(8,128)(2,1)S(1)}, bf16[96,2048]{1,0:T(8,128)(2,1)S(1)}, u32[]{:S(2)}, u32[]{:S(2)}) %collective-permute-start.8) | collective-permute-done | bytes 393248 | tf_op jit(solution)/shard_map/ppermute | solution.py:201
  31.1 2.3 %collective-permute-start.3 = (bf16[96,2048]{1,0:T(8,128)(2,1)S(1)}, bf16[96,2048]{1,0:T(8,128)(2,1)S(1)}, u32[]{:S(2)}, u32[]{:S(2)}) collective-permute-start(bf16[96,2048]{1,0:T(8,128)(2,1)S(1)} %collective-permute-done.2.own), channel_id=1, source_target_pairs={{0,1},{1,0},{2,3},{3,2},{4,5},{5,4},{6,7},{7,6},{8,9},{9,8},{10,11... | collective-permute-start | bytes 1179656 | tf_op jit(solution)/shard_map/ppermute | solution.py:189
  33.4 0.6 collective-permute-start.9
  34.0 9.9 %collective-permute-done.16.own = bf16[96,2048]{1,0:T(8,128)(2,1)S(1)} collective-permute-done((bf16[96,2048]{1,0:T(8,128)(2,1)S(1)}, bf16[96,2048]{1,0:T(8,128)(2,1)S(1)}, u32[]{:S(2)}, u32[]{:S(2)}) %collective-permute-start.16) | collective-permute-done | bytes 393248 | tf_op jit(solution)/shard_map/ppermute | solution.py:201
  43.9 1.5 collective-permute-start.13
  45.4 0.5 collective-permute-start.17
  45.9 2.2 %copy-done = bf16[1,2048,1024]{2,1,0:T(8,128)(2,1)S(1)} copy-done((bf16[1,2048,1024]{2,1,0:T(8,128)(2,1)S(1)}, bf16[1,2048,1024]{2,1,0:T(8,128)(2,1)}, u32[]{:S(2)}) %copy-start) | copy-done | bytes 4194328
  48.1 2.2 %copy-done.2 = bf16[1,1024,2048]{2,1,0:T(8,128)(2,1)S(1)} copy-done((bf16[1,1024,2048]{2,1,0:T(8,128)(2,1)S(1)}, bf16[1,1024,2048]{2,1,0:T(8,128)(2,1)}, u32[]{:S(2)}) %copy-start.2) | copy-done | bytes 4194328
  50.3 7.9 %shard_map.96 = (f32[96,2048]{1,0:T(8,128)S(1)}, bf16[96,2048]{1,0:T(8,128)(2,1)S(1)}) custom-call(bf16[96,2048]{1,0:T(8,128)(2,1)S(1)} %collective-permute-done.2.own, bf16[96,2048]{1,0:T(8,128)(2,1)S(1)} %collective-permute-done.3.across, bf16[2048,1024]{1,0:T(8,128)(2,1)S(1)} %bitcast.28, bf16[1024,2048]{1,0:T(8,128)(2,1)S(1)} %bitcast.33, ...), custom_call_target="tpu_custom_call" | custom-call | flops 3221225472 | bytes 16777216 | tf_op jit(solution)/shard_map/pallas_call | solution.py:121
  58.2 1.6 %collective-permute-start.6 = (bf16[96,2048]{1,0:T(8,128)(2,1)S(1)}, bf16[96,2048]{1,0:T(8,128)(2,1)S(1)}, u32[]{:S(2)}, u32[]{:S(2)}) collective-permute-start(bf16[96,2048]{1,0:T(8,128)(2,1)S(1)} %get-tuple-element.19), channel_id=1, source_target_pairs={{0,1},{1,0},{2,3},{3,2},{4,5},{5,4},{6,7},{7,6},{8,9},{9,8},{10,11... | collective-permute-start | bytes 1179656 | tf_op jit(solution)/shard_map/ppermute | solution.py:189
  59.8 7.4 %shard_map.97 = (f32[96,2048]{1,0:T(8,128)S(1)}, bf16[96,2048]{1,0:T(8,128)(2,1)S(1)}) custom-call(bf16[96,2048]{1,0:T(8,128)(2,1)S(1)} %collective-permute-done.8.own, bf16[96,2048]{1,0:T(8,128)(2,1)S(1)} %collective-permute-done.9.across, bf16[2048,1024]{1,0:T(8,128)(2,1)S(1)} %bitcast.29, bf16[1024,2048]{1,0:T(8,128)(2,1)S(1)} %bitcast.34, ...), custom_call_target="tpu_custom_call" | custom-call | flops 3221225472 | bytes 16777216 | tf_op jit(solution)/shard_map/pallas_call | solution.py:121
  67.2 0.6 collective-permute-start.10
  67.8 7.4 %shard_map.98 = (f32[96,2048]{1,0:T(8,128)S(1)}, bf16[96,2048]{1,0:T(8,128)(2,1)S(1)}) custom-call(bf16[96,2048]{1,0:T(8,128)(2,1)S(1)} %collective-permute-done.12.own, bf16[96,2048]{1,0:T(8,128)(2,1)S(1)} %collective-permute-done.13.across, bf16[2048,1024]{1,0:T(8,128)(2,1)S(1)} %bitcast.30, bf16[1024,2048]{1,0:T(8,128)(2,1)S(1)} %bitcast.35, ...), custom_call_target="tpu_custom_call" | custom-call | flops 3221225472 | bytes 16777216 | tf_op jit(solution)/shard_map/pallas_call | solution.py:121
  75.2 1.6 %collective-permute-start.14 = (bf16[96,2048]{1,0:T(8,128)(2,1)S(1)}, bf16[96,2048]{1,0:T(8,128)(2,1)S(1)}, u32[]{:S(2)}, u32[]{:S(2)}) collective-permute-start(bf16[96,2048]{1,0:T(8,128)(2,1)S(1)} %get-tuple-element.25), channel_id=1, source_target_pairs={{0,1},{1,0},{2,3},{3,2},{4,5},{5,4},{6,7},{7,6},{8,9},{9,8},{10,11... | collective-permute-start | bytes 1179656 | tf_op jit(solution)/shard_map/ppermute | solution.py:189
  76.8 7.4 %shard_map.99 = (f32[96,2048]{1,0:T(8,128)S(1)}, bf16[96,2048]{1,0:T(8,128)(2,1)S(1)}) custom-call(bf16[96,2048]{1,0:T(8,128)(2,1)S(1)} %collective-permute-done.16.own, bf16[96,2048]{1,0:T(8,128)(2,1)S(1)} %collective-permute-done.17.across, bf16[2048,1024]{1,0:T(8,128)(2,1)S(1)} %bitcast.31, bf16[1024,2048]{1,0:T(8,128)(2,1)S(1)} %bitcast.36, ...), custom_call_target="tpu_custom_call" | custom-call | flops 3221225472 | bytes 16777216 | tf_op jit(solution)/shard_map/pallas_call | solution.py:121
  84.2 0.6 collective-permute-start.18
  84.8 0.1 add_convert_fusion.3
  84.9 0.7 collective-permute-start.7
  85.6 0.1 add_convert_fusion.2
  85.7 8.8 %collective-permute-start.11 = (bf16[96,2048]{1,0:T(8,128)(2,1)S(1)}, bf16[96,2048]{1,0:T(8,128)(2,1)S(1)}, u32[]{:S(2)}, u32[]{:S(2)}) collective-permute-start(bf16[96,2048]{1,0:T(8,128)(2,1)S(1)} %add_convert_fusion.2), channel_id=1, source_target_pairs={{0,4},{1,5},{2,6},{3,7},{4,0},{5,1},{6,2},{7,3},{8,12},{9,13},{10,... | collective-permute-start | bytes 1179656 | tf_op jit(solution)/shard_map/ppermute | solution.py:201
  94.6 0.1 add_convert_fusion.1
  94.6 3.0 %collective-permute-start.15 = (bf16[96,2048]{1,0:T(8,128)(2,1)S(1)}, bf16[96,2048]{1,0:T(8,128)(2,1)S(1)}, u32[]{:S(2)}, u32[]{:S(2)}) collective-permute-start(bf16[96,2048]{1,0:T(8,128)(2,1)S(1)} %add_convert_fusion.1), channel_id=1, source_target_pairs={{0,8},{1,9},{2,10},{3,11},{4,12},{5,13},{6,14},{7,15},{8,0},{9,1},... | collective-permute-start | bytes 1179656 | tf_op jit(solution)/shard_map/ppermute | solution.py:201
  97.7 0.1 add_convert_fusion
  97.8 2.4 %collective-permute-start.19 = (bf16[96,2048]{1,0:T(8,128)(2,1)S(1)}, bf16[96,2048]{1,0:T(8,128)(2,1)S(1)}, u32[]{:S(2)}, u32[]{:S(2)}) collective-permute-start(bf16[96,2048]{1,0:T(8,128)(2,1)S(1)} %add_convert_fusion), channel_id=1, source_target_pairs={{0,12},{1,13},{2,14},{3,15},{4,8},{5,9},{6,10},{7,11},{8,4},{9,5},... | collective-permute-start | bytes 1179656 | tf_op jit(solution)/shard_map/ppermute | solution.py:201
  100.1 10.6 %collective-permute-start.20 = (bf16[48,2048]{1,0:T(8,128)(2,1)S(1)}, bf16[48,2048]{1,0:T(8,128)(2,1)S(1)}, u32[]{:S(2)}, u32[]{:S(2)}) collective-permute-start(bf16[48,2048]{1,0:T(8,128)(2,1)S(1)} %slice_bitcast_fusion.3), channel_id=1, source_target_pairs={{0,16},{16,0},{1,17},{17,1},{2,18},{18,2},{3,19},{19,3},{4,20},{20... | collective-permute-start | bytes 589832 | tf_op jit(solution)/shard_map/ppermute | solution.py:186
  110.8 2.2 %collective-permute-start.21 = (bf16[48,2048]{1,0:T(8,128)(2,1)S(1)}, bf16[48,2048]{1,0:T(8,128)(2,1)S(1)}, u32[]{:S(2)}, u32[]{:S(2)}) collective-permute-start(bf16[48,2048]{1,0:T(8,128)(2,1)S(1)} %slice_bitcast_fusion.2), channel_id=1, source_target_pairs={{0,16},{16,0},{1,17},{17,1},{2,18},{18,2},{3,19},{19,3},{4,20},{20... | collective-permute-start | bytes 589832 | tf_op jit(solution)/shard_map/ppermute | solution.py:186
  112.9 15.1 %collective-permute-start.22 = (bf16[48,2048]{1,0:T(8,128)(2,1)S(1)}, bf16[48,2048]{1,0:T(8,128)(2,1)S(1)}, u32[]{:S(2)}, u32[]{:S(2)}) collective-permute-start(bf16[48,2048]{1,0:T(8,128)(2,1)S(1)} %slice_bitcast_fusion.1), channel_id=1, source_target_pairs={{0,16},{16,0},{1,17},{17,1},{2,18},{18,2},{3,19},{19,3},{4,20},{20... | collective-permute-start | bytes 589832 | tf_op jit(solution)/shard_map/ppermute | solution.py:186
  128.1 0.1 collective-permute-start.23
  128.2 0.9 collective-permute-done.22.refs_6_
  129.1 0.5 collective-permute-done.23.refs_7_
  129.6 1.9 %shard_map.100 = (bf16[128,2048]{1,0:T(8,128)(2,1)}, f32[32,128]{1,0:T(8,128)S(1)}) custom-call(bf16[96,2048]{1,0:T(8,128)(2,1)S(1)} %collective-permute-done.7.refs_0_, bf16[96,2048]{1,0:T(8,128)(2,1)S(1)} %collective-permute-done.11.refs_1_, bf16[96,2048]{1,0:T(8,128)(2,1)S(1)} %collective-permute-done.15.refs_2_, ...), custom_call_target="tpu_custom_call" | custom-call | tf_op jit(solution)/shard_map/pallas_call | solution.py:230
  131.5 16.7 %all_to_all.9 = f32[32,1,128]{2,1,0:T(1,128)S(1)} all-to-all(f32[32,1,128]{2,1,0:T(1,128)S(1)} %bitcast.47), channel_id=1, replica_groups=mesh['section'=2,'expert'=16] {'section','expert'}, dimensions={0} | all-to-all | bytes 32768 | tf_op jit(solution)/shard_map/all_to_all | solution.py:247
  148.2 0.1 slice_divide_fusion
  148.2 0.5 add_bitcast_fusion
  (38 shorter events, 0.2 us)
Async XLA Ops:
  0.6 45.3 %collective-permute-start.4 = (bf16[2048,1024]{1,0:T(8,128)(2,1)}, bf16[2048,1024]{1,0:T(8,128)(2,1)}, u32[]{:S(2)}, u32[]{:S(2)}) collective-permute-start(bf16[2048,1024]{1,0:T(8,128)(2,1)} %bitcast.27), channel_id=1, source_target_pairs={{0,16},{16,0},{1,17},{17,1},{2,18},{18,2},{3,19},{19,3},{4,20},{20... | collective-permute-start | bytes 12582920 | tf_op jit(solution)/shard_map/ppermute | solution.py:186
  1.1 44.8 %collective-permute-start.5 = (bf16[1024,2048]{1,0:T(8,128)(2,1)}, bf16[1024,2048]{1,0:T(8,128)(2,1)}, u32[]{:S(2)}, u32[]{:S(2)}) collective-permute-start(bf16[1024,2048]{1,0:T(8,128)(2,1)} %bitcast.32), channel_id=1, source_target_pairs={{0,16},{16,0},{1,17},{17,1},{2,18},{18,2},{3,19},{19,3},{4,20},{20... | collective-permute-start | bytes 12582920 | tf_op jit(solution)/shard_map/ppermute | solution.py:186
  1.2 7.8 %collective-permute-start = (bf16[128,2048]{1,0:T(8,128)(2,1)}, bf16[128,2048]{1,0:T(8,128)(2,1)S(1)}, u32[]{:S(2)}, u32[]{:S(2)}) collective-permute-start(bf16[128,2048]{1,0:T(8,128)(2,1)} %bitcast.37), channel_id=1, source_target_pairs={{0,16},{16,0},{1,17},{17,1},{2,18},{18,2},{3,19},{19,3},{4,20},{20... | collective-permute-start | bytes 1572872 | tf_op jit(solution)/shard_map/ppermute | solution.py:186
  2.4 6.3 %collective-permute-start.1 = (s32[128,2]{1,0:T(8,128)S(1)}, s32[128,2]{1,0:T(8,128)S(1)}, u32[]{:S(2)}, u32[]{:S(2)}) collective-permute-start(s32[128,2]{1,0:T(8,128)S(1)} %bitcast.45), channel_id=1, source_target_pairs={{0,16},{16,0},{1,17},{17,1},{2,18},{18,2},{3,19},{19,3},{4,20},{20... | collective-permute-start | bytes 3080 | tf_op jit(solution)/shard_map/ppermute | solution.py:186
  9.0 1.0 copy-start.4
  10.1 0.7 copy-start.7
  12.5 6.5 %collective-permute-start.2 = (bf16[96,2048]{1,0:T(8,128)(2,1)S(1)}, bf16[96,2048]{1,0:T(8,128)(2,1)S(1)}, u32[]{:S(2)}, u32[]{:S(2)}) collective-permute-start(bf16[96,2048]{1,0:T(8,128)(2,1)S(1)} %get-tuple-element.17), channel_id=1, source_target_pairs={{0,0},{1,1},{2,2},{3,3},{4,4},{5,5},{6,6},{7,7},{8,8},{9,9},{10,10... | collective-permute-start | bytes 1179656 | tf_op jit(solution)/shard_map/ppermute | solution.py:201
  13.2 17.9 %collective-permute-start.8 = (bf16[96,2048]{1,0:T(8,128)(2,1)S(1)}, bf16[96,2048]{1,0:T(8,128)(2,1)S(1)}, u32[]{:S(2)}, u32[]{:S(2)}) collective-permute-start(bf16[96,2048]{1,0:T(8,128)(2,1)S(1)} %get-tuple-element.20), channel_id=1, source_target_pairs={{0,4},{1,5},{2,6},{3,7},{4,0},{5,1},{6,2},{7,3},{8,12},{9,13},{10,... | collective-permute-start | bytes 1179656 | tf_op jit(solution)/shard_map/ppermute | solution.py:201
  16.4 17.0 %collective-permute-start.12 = (bf16[96,2048]{1,0:T(8,128)(2,1)S(1)}, bf16[96,2048]{1,0:T(8,128)(2,1)S(1)}, u32[]{:S(2)}, u32[]{:S(2)}) collective-permute-start(bf16[96,2048]{1,0:T(8,128)(2,1)S(1)} %get-tuple-element.23), channel_id=1, source_target_pairs={{0,8},{1,9},{2,10},{3,11},{4,12},{5,13},{6,14},{7,15},{8,0},{9,1},... | collective-permute-start | bytes 1179656 | tf_op jit(solution)/shard_map/ppermute | solution.py:201
  19.0 24.9 %collective-permute-start.16 = (bf16[96,2048]{1,0:T(8,128)(2,1)S(1)}, bf16[96,2048]{1,0:T(8,128)(2,1)S(1)}, u32[]{:S(2)}, u32[]{:S(2)}) collective-permute-start(bf16[96,2048]{1,0:T(8,128)(2,1)S(1)} %get-tuple-element.26), channel_id=1, source_target_pairs={{0,12},{1,13},{2,14},{3,15},{4,8},{5,9},{6,10},{7,11},{8,4},{9,5},... | collective-permute-start | bytes 1179656 | tf_op jit(solution)/shard_map/ppermute | solution.py:201
  31.1 14.3 %collective-permute-start.3 = (bf16[96,2048]{1,0:T(8,128)(2,1)S(1)}, bf16[96,2048]{1,0:T(8,128)(2,1)S(1)}, u32[]{:S(2)}, u32[]{:S(2)}) collective-permute-start(bf16[96,2048]{1,0:T(8,128)(2,1)S(1)} %collective-permute-done.2.own), channel_id=1, source_target_pairs={{0,1},{1,0},{2,3},{3,2},{4,5},{5,4},{6,7},{7,6},{8,9},{9,8},{10,11... | collective-permute-start | bytes 1179656 | tf_op jit(solution)/shard_map/ppermute | solution.py:189
  33.4 26.4 %collective-permute-start.9 = (bf16[96,2048]{1,0:T(8,128)(2,1)S(1)}, bf16[96,2048]{1,0:T(8,128)(2,1)S(1)}, u32[]{:S(2)}, u32[]{:S(2)}) collective-permute-start(bf16[96,2048]{1,0:T(8,128)(2,1)S(1)} %collective-permute-done.8.own), channel_id=1, source_target_pairs={{0,1},{1,0},{2,3},{3,2},{4,5},{5,4},{6,7},{7,6},{8,9},{9,8},{10,11... | collective-permute-start | bytes 1179656 | tf_op jit(solution)/shard_map/ppermute | solution.py:189
  43.9 23.9 %collective-permute-start.13 = (bf16[96,2048]{1,0:T(8,128)(2,1)S(1)}, bf16[96,2048]{1,0:T(8,128)(2,1)S(1)}, u32[]{:S(2)}, u32[]{:S(2)}) collective-permute-start(bf16[96,2048]{1,0:T(8,128)(2,1)S(1)} %collective-permute-done.12.own), channel_id=1, source_target_pairs={{0,1},{1,0},{2,3},{3,2},{4,5},{5,4},{6,7},{7,6},{8,9},{9,8},{10,11... | collective-permute-start | bytes 1179656 | tf_op jit(solution)/shard_map/ppermute | solution.py:189
  45.4 31.4 %collective-permute-start.17 = (bf16[96,2048]{1,0:T(8,128)(2,1)S(1)}, bf16[96,2048]{1,0:T(8,128)(2,1)S(1)}, u32[]{:S(2)}, u32[]{:S(2)}) collective-permute-start(bf16[96,2048]{1,0:T(8,128)(2,1)S(1)} %collective-permute-done.16.own), channel_id=1, source_target_pairs={{0,1},{1,0},{2,3},{3,2},{4,5},{5,4},{6,7},{7,6},{8,9},{9,8},{10,11... | collective-permute-start | bytes 1179656 | tf_op jit(solution)/shard_map/ppermute | solution.py:189
  45.9 2.2 %copy-start = (bf16[1,2048,1024]{2,1,0:T(8,128)(2,1)S(1)}, bf16[1,2048,1024]{2,1,0:T(8,128)(2,1)}, u32[]{:S(2)}) copy-start(bf16[1,2048,1024]{2,1,0:T(8,128)(2,1)} %param.12) | copy-start | bytes 12582916
  48.1 2.2 %copy-start.2 = (bf16[1,1024,2048]{2,1,0:T(8,128)(2,1)S(1)}, bf16[1,1024,2048]{2,1,0:T(8,128)(2,1)}, u32[]{:S(2)}) copy-start(bf16[1,1024,2048]{2,1,0:T(8,128)(2,1)} %param.13) | copy-start | bytes 12582916
  50.3 9.5 %copy-start.1 = (bf16[1,2048,1024]{2,1,0:T(8,128)(2,1)S(1)}, bf16[1,2048,1024]{2,1,0:T(8,128)(2,1)}, u32[]{:S(2)}) copy-start(bf16[1,2048,1024]{2,1,0:T(8,128)(2,1)} %param.12) | copy-start | bytes 12582916
  50.3 9.5 %copy-start.3 = (bf16[1,1024,2048]{2,1,0:T(8,128)(2,1)S(1)}, bf16[1,1024,2048]{2,1,0:T(8,128)(2,1)}, u32[]{:S(2)}) copy-start(bf16[1,1024,2048]{2,1,0:T(8,128)(2,1)} %param.13) | copy-start | bytes 12582916
  58.2 26.6 %collective-permute-start.6 = (bf16[96,2048]{1,0:T(8,128)(2,1)S(1)}, bf16[96,2048]{1,0:T(8,128)(2,1)S(1)}, u32[]{:S(2)}, u32[]{:S(2)}) collective-permute-start(bf16[96,2048]{1,0:T(8,128)(2,1)S(1)} %get-tuple-element.19), channel_id=1, source_target_pairs={{0,1},{1,0},{2,3},{3,2},{4,5},{5,4},{6,7},{7,6},{8,9},{9,8},{10,11... | collective-permute-start | bytes 1179656 | tf_op jit(solution)/shard_map/ppermute | solution.py:189
  67.2 18.4 %collective-permute-start.10 = (bf16[96,2048]{1,0:T(8,128)(2,1)S(1)}, bf16[96,2048]{1,0:T(8,128)(2,1)S(1)}, u32[]{:S(2)}, u32[]{:S(2)}) collective-permute-start(bf16[96,2048]{1,0:T(8,128)(2,1)S(1)} %get-tuple-element.22), channel_id=1, source_target_pairs={{0,1},{1,0},{2,3},{3,2},{4,5},{5,4},{6,7},{7,6},{8,9},{9,8},{10,11... | collective-permute-start | bytes 1179656 | tf_op jit(solution)/shard_map/ppermute | solution.py:189
  75.2 19.3 %collective-permute-start.14 = (bf16[96,2048]{1,0:T(8,128)(2,1)S(1)}, bf16[96,2048]{1,0:T(8,128)(2,1)S(1)}, u32[]{:S(2)}, u32[]{:S(2)}) collective-permute-start(bf16[96,2048]{1,0:T(8,128)(2,1)S(1)} %get-tuple-element.25), channel_id=1, source_target_pairs={{0,1},{1,0},{2,3},{3,2},{4,5},{5,4},{6,7},{7,6},{8,9},{9,8},{10,11... | collective-permute-start | bytes 1179656 | tf_op jit(solution)/shard_map/ppermute | solution.py:189
  84.2 45.4 %copy-start.5 = (bf16[1,128,2048]{2,1,0:T(8,128)(2,1)S(1)}, bf16[1,128,2048]{2,1,0:T(8,128)(2,1)}, u32[]{:S(2)}) copy-start(bf16[1,128,2048]{2,1,0:T(8,128)(2,1)} %param.8) | copy-start | bytes 1572868
  84.2 45.4 %copy-start.6 = (bf16[1,128,2048]{2,1,0:T(8,128)(2,1)S(1)}, bf16[1,128,2048]{2,1,0:T(8,128)(2,1)}, u32[]{:S(2)}) copy-start(bf16[1,128,2048]{2,1,0:T(8,128)(2,1)} %param.9) | copy-start | bytes 1572868
  84.2 45.3 %copy-start.8 = (s32[1,128]{1,0:T(1,128)S(1)}, s32[1,128]{1,0:T(1,128)}, u32[]{:S(2)}) copy-start(s32[1,128]{1,0:T(1,128)} %refs_11_.1) | copy-start | bytes 1540
  84.2 13.5 %collective-permute-start.18 = (bf16[96,2048]{1,0:T(8,128)(2,1)S(1)}, bf16[96,2048]{1,0:T(8,128)(2,1)S(1)}, u32[]{:S(2)}, u32[]{:S(2)}) collective-permute-start(bf16[96,2048]{1,0:T(8,128)(2,1)S(1)} %get-tuple-element.28), channel_id=1, source_target_pairs={{0,1},{1,0},{2,3},{3,2},{4,5},{5,4},{6,7},{7,6},{8,9},{9,8},{10,11... | collective-permute-start | bytes 1179656 | tf_op jit(solution)/shard_map/ppermute | solution.py:189
  84.9 15.2 %collective-permute-start.7 = (bf16[96,2048]{1,0:T(8,128)(2,1)S(1)}, bf16[96,2048]{1,0:T(8,128)(2,1)S(1)}, u32[]{:S(2)}, u32[]{:S(2)}) collective-permute-start(bf16[96,2048]{1,0:T(8,128)(2,1)S(1)} %add_convert_fusion.3), channel_id=1, source_target_pairs={{0,0},{1,1},{2,2},{3,3},{4,4},{5,5},{6,6},{7,7},{8,8},{9,9},{10,10... | collective-permute-start | bytes 1179656 | tf_op jit(solution)/shard_map/ppermute | solution.py:201
  85.7 25.0 %collective-permute-start.11 = (bf16[96,2048]{1,0:T(8,128)(2,1)S(1)}, bf16[96,2048]{1,0:T(8,128)(2,1)S(1)}, u32[]{:S(2)}, u32[]{:S(2)}) collective-permute-start(bf16[96,2048]{1,0:T(8,128)(2,1)S(1)} %add_convert_fusion.2), channel_id=1, source_target_pairs={{0,4},{1,5},{2,6},{3,7},{4,0},{5,1},{6,2},{7,3},{8,12},{9,13},{10,... | collective-permute-start | bytes 1179656 | tf_op jit(solution)/shard_map/ppermute | solution.py:201
  94.6 18.3 %collective-permute-start.15 = (bf16[96,2048]{1,0:T(8,128)(2,1)S(1)}, bf16[96,2048]{1,0:T(8,128)(2,1)S(1)}, u32[]{:S(2)}, u32[]{:S(2)}) collective-permute-start(bf16[96,2048]{1,0:T(8,128)(2,1)S(1)} %add_convert_fusion.1), channel_id=1, source_target_pairs={{0,8},{1,9},{2,10},{3,11},{4,12},{5,13},{6,14},{7,15},{8,0},{9,1},... | collective-permute-start | bytes 1179656 | tf_op jit(solution)/shard_map/ppermute | solution.py:201
  97.8 30.3 %collective-permute-start.19 = (bf16[96,2048]{1,0:T(8,128)(2,1)S(1)}, bf16[96,2048]{1,0:T(8,128)(2,1)S(1)}, u32[]{:S(2)}, u32[]{:S(2)}) collective-permute-start(bf16[96,2048]{1,0:T(8,128)(2,1)S(1)} %add_convert_fusion), channel_id=1, source_target_pairs={{0,12},{1,13},{2,14},{3,15},{4,8},{5,9},{6,10},{7,11},{8,4},{9,5},... | collective-permute-start | bytes 1179656 | tf_op jit(solution)/shard_map/ppermute | solution.py:201
  100.1 28.0 %collective-permute-start.20 = (bf16[48,2048]{1,0:T(8,128)(2,1)S(1)}, bf16[48,2048]{1,0:T(8,128)(2,1)S(1)}, u32[]{:S(2)}, u32[]{:S(2)}) collective-permute-start(bf16[48,2048]{1,0:T(8,128)(2,1)S(1)} %slice_bitcast_fusion.3), channel_id=1, source_target_pairs={{0,16},{16,0},{1,17},{17,1},{2,18},{18,2},{3,19},{19,3},{4,20},{20... | collective-permute-start | bytes 589832 | tf_op jit(solution)/shard_map/ppermute | solution.py:186
  110.8 17.4 %collective-permute-start.21 = (bf16[48,2048]{1,0:T(8,128)(2,1)S(1)}, bf16[48,2048]{1,0:T(8,128)(2,1)S(1)}, u32[]{:S(2)}, u32[]{:S(2)}) collective-permute-start(bf16[48,2048]{1,0:T(8,128)(2,1)S(1)} %slice_bitcast_fusion.2), channel_id=1, source_target_pairs={{0,16},{16,0},{1,17},{17,1},{2,18},{18,2},{3,19},{19,3},{4,20},{20... | collective-permute-start | bytes 589832 | tf_op jit(solution)/shard_map/ppermute | solution.py:186
  112.9 16.2 %collective-permute-start.22 = (bf16[48,2048]{1,0:T(8,128)(2,1)S(1)}, bf16[48,2048]{1,0:T(8,128)(2,1)S(1)}, u32[]{:S(2)}, u32[]{:S(2)}) collective-permute-start(bf16[48,2048]{1,0:T(8,128)(2,1)S(1)} %slice_bitcast_fusion.1), channel_id=1, source_target_pairs={{0,16},{16,0},{1,17},{17,1},{2,18},{18,2},{3,19},{19,3},{4,20},{20... | collective-permute-start | bytes 589832 | tf_op jit(solution)/shard_map/ppermute | solution.py:186
  128.1 1.5 %collective-permute-start.23 = (bf16[48,2048]{1,0:T(8,128)(2,1)S(1)}, bf16[48,2048]{1,0:T(8,128)(2,1)S(1)}, u32[]{:S(2)}, u32[]{:S(2)}) collective-permute-start(bf16[48,2048]{1,0:T(8,128)(2,1)S(1)} %slice_bitcast_fusion), channel_id=1, source_target_pairs={{0,16},{16,0},{1,17},{17,1},{2,18},{18,2},{3,19},{19,3},{4,20},{20... | collective-permute-start | bytes 589832 | tf_op jit(solution)/shard_map/ppermute | solution.py:186

commit v2 on v1

--- a/solution.py
+++ b/solution.py
@@ -24,56 +24,72 @@
     return jnp.sum(values, axis=1, keepdims=True)
 
 
-def place_body(capacity, hidden, other, gain, router, routes, other_routes, *outs):
-    sends, weights = outs[:-1], outs[-1]
-    experts = router.shape[1]
-    tok_rows = hidden.shape[0]
-    couples = experts // 2
-    slots = experts * capacity
+def column_sum(values):
+    return jnp.sum(values, axis=0, keepdims=True)
+
+
+def whole(shape):
+    return pl.BlockSpec(shape, lambda i: (0, 0))
+
+
+def after(value, *others):
+    return lax.optimization_barrier((value, *others))[0] if others else value
+
+
+def lay_out(capacity, turn, values, gain, routes):
+    tok_rows = values.shape[0]
+    experts = 3 * tok_rows // capacity
     side = lax.axis_index("section")
     group = lax.axis_index("expert") // 2
-    expert_ids = lax.broadcasted_iota(jnp.int32, (tok_rows, experts), 1)
-    before = (
+    normed = normalize(values[...].astype(jnp.float32), gain[...]).astype(jnp.bfloat16)
+    expert_ids = lax.broadcasted_iota(jnp.int32, (experts, tok_rows), 0)
+    before = jnp.where(
         lax.broadcasted_iota(jnp.int32, (tok_rows, tok_rows), 0)
-        > lax.broadcasted_iota(jnp.int32, (tok_rows, tok_rows), 1)
+        < lax.broadcasted_iota(jnp.int32, (tok_rows, tok_rows), 1),
+        1.0,
+        0.0,
     ).astype(jnp.bfloat16)
-    columns = lax.broadcasted_iota(jnp.int32, (tok_rows, slots), 1)
-    rows, placing = [], []
-    for turn, (values, chosen) in enumerate(((hidden, routes), (other, other_routes))):
-        normed = normalize(values[...].astype(jnp.float32), gain[...]).astype(jnp.bfloat16)
-        chosen = chosen[...]
-        named = [chosen[:, k : k + 1] == expert_ids for k in range(2)]
-        member = jnp.where(named[0] | named[1], 1.0, 0.0).astype(jnp.bfloat16)
-        earlier = jnp.dot(before, member, preferred_element_type=jnp.float32)
-        place = [row_sum(jnp.where(n, earlier, 0.0)).astype(jnp.int32) for n in named]
-        step = [chosen[:, k : k + 1] ^ group for k in range(2)]
-        mine = [(k & 1) == side for k in step]
-        full = [(k >> 1) * (2 * capacity) + p for k, p in zip(step, place)]
-        target = [jnp.where(m, f + turn * capacity, -1) for m, f in zip(mine, full)]
-        placing.append(
-            jnp.where((columns == target[0]) | (columns == target[1]), 1.0, 0.0).astype(jnp.bfloat16)
-        )
-        rows.append(normed)
-        if turn == 0:
-            logits = jnp.dot(normed, router[...], preferred_element_type=jnp.float32)
-            picked = [row_sum(jnp.where(n, logits, 0.0)) for n in named]
-            gates = (
-                1.0 / (1.0 + jnp.exp(picked[1] - picked[0])),
-                1.0 / (1.0 + jnp.exp(picked[0] - picked[1])),
-            )
-            wide = lax.broadcasted_iota(jnp.int32, weights.shape, 1)
-            back = [
-                jnp.where(m, f, slots + (k >> 1) * capacity + p)
-                for m, f, k, p in zip(mine, full, step, place)
-            ]
-            weights[...] = jnp.where(wide == back[0], gates[0], 0.0) + jnp.where(
-                wide == back[1], gates[1], 0.0
-            )
-    sent = lax.dot_general(
-        jnp.concatenate(placing, axis=0),
-        jnp.concatenate(rows, axis=0),
-        (((0,), (0,)), ((), ())),
-        preferred_element_type=jnp.float32,
+    chosen = [routes[k : k + 1, :] for k in range(2)]
+    named = [c == expert_ids for c in chosen]
+    member = jnp.where(named[0] | named[1], 1.0, 0.0).astype(jnp.bfloat16)
+    earlier = jnp.dot(member, before, preferred_element_type=jnp.float32)
+    place = [column_sum(jnp.where(n, earlier, 0.0)).astype(jnp.int32) for n in named]
+    step = [c ^ group for c in chosen]
+    mine = [(k & 1) == side for k in step]
+    full = [(k >> 1) * (2 * capacity) + p for k, p in zip(step, place)]
+    slots = lax.broadcasted_iota(jnp.int32, (experts * capacity, tok_rows), 0)
+    target = [jnp.where(m, f + turn * capacity, -1) for m, f in zip(mine, full)]
+    placing = jnp.where((slots == target[0]) | (slots == target[1]), 1.0, 0.0).astype(jnp.bfloat16)
+    back = [
+        jnp.where(m, f, experts * capacity + (k >> 1) * capacity + p)
+        for m, f, k, p in zip(mine, full, step, place)
+    ]
+    return normed, placing, named, back
+
+
+def own_body(capacity, hidden, gain, router, routes, rows, place, weights):
+    normed, placing, named, back = lay_out(capacity, 0, hidden, gain, routes)
+    rows[...] = normed
+    place[...] = placing
+    logits = lax.dot_general(
+        router[...], normed, (((1,), (1,)), ((), ())), preferred_element_type=jnp.float32
+    )
+    picked = [column_sum(jnp.where(n, logits, 0.0)) for n in named]
+    gates = (
+        1.0 / (1.0 + jnp.exp(picked[1] - picked[0])),
+        1.0 / (1.0 + jnp.exp(picked[0] - picked[1])),
+    )
+    wide = lax.broadcasted_iota(jnp.int32, weights.shape, 0)
+    weights[...] = jnp.where(wide == back[0], gates[0], 0.0) + jnp.where(
+        wide == back[1], gates[1], 0.0
+    )
+
+
+def place_body(capacity, rows, place, other, gain, routes, *sends):
+    normed, placing, _, _ = lay_out(capacity, 1, other, gain, routes)
+    sent = (
+        jnp.dot(place[...], rows[...], preferred_element_type=jnp.float32)
+        + jnp.dot(placing, normed, preferred_element_type=jnp.float32)
     ).astype(jnp.bfloat16)
     span = sends[0].shape[0]
     for k, ref in enumerate(sends):
@@ -111,8 +127,8 @@
         sent[...] = total[span:].astype(jnp.bfloat16)
 
 
-def expert_work(own, across, up, down, up_other, down_other):
-    span, features = own.shape
+def expert_work(span, own, across, up, down, up_other, down_other):
+    features = own[0].shape[1]
     units = up.shape[1]
     block = min(256, units)
     rows_spec = pl.BlockSpec((span, features), lambda i: (0, 0))
@@ -121,7 +137,14 @@
     return pl.pallas_call(
         expert_body,
         grid=(units // block,),
-        in_specs=[rows_spec, rows_spec, up_spec, down_spec, up_spec, down_spec],
+        in_specs=[
+            pl.BlockSpec((span, features), lambda i: (own[1], 0)),
+            pl.BlockSpec((span, features), lambda i: (across[1], 0)),
+            up_spec,
+            down_spec,
+            up_spec,
+            down_spec,
+        ],
         out_specs=[rows_spec, rows_spec],
         out_shape=[
             jax.ShapeDtypeStruct((span, features), jnp.float32),
@@ -137,7 +160,8 @@
             bytes_accessed=8 * features * units,
             transcendentals=0,
         ),
-    )(own, across, up, down, up_other, down_other)
+        name="expert",
+    )(own[0], across[0], up, down, up_other, down_other)
 
 
 def combine_body(rounds, pair_rows, *refs):
@@ -150,10 +174,10 @@
     low = (gate - high.astype(jnp.float32)).astype(jnp.bfloat16)
     total = hidden[...].astype(jnp.float32)
     rows = jnp.concatenate([r[...] for r in returned + crossed], axis=0)
-    total = total + (
-        jnp.dot(high, rows, preferred_element_type=jnp.float32)
-        + jnp.dot(low, rows, preferred_element_type=jnp.float32)
-    )
+    for part in (high, low):
+        total = total + lax.dot_general(
+            part, rows, (((0,), (0,)), ((), ())), preferred_element_type=jnp.float32
+        )
     result = total.astype(jnp.bfloat16)
     layer_out[...] = result
     score = row_sum(result.astype(jnp.float32) * target[...].astype(jnp.float32)) / math.sqrt(features)
@@ -197,36 +221,105 @@
                 for side in range(sections)
                 for i in range(chips)
             ]
-            part = value[k * 2 * capacity : (k + 1) * 2 * capacity]
+            part = value if each == 1 else value[k * 2 * capacity : (k + 1) * 2 * capacity]
             parts.append(lax.ppermute(part, both, pairs))
         return parts[0] if each == 1 else jnp.concatenate(parts, axis=0)
 
-    other_hidden = over_section(hidden_in[0])
-    other_routes = over_section(routes[0])
+    rows_in, gain, router = hidden_in[0], norm_gain[None], router_weight.T
+    chosen = routes[0].T
+    other_rows = over_section(rows_in)
+    other_routes = over_section(chosen)
+    slots = experts * capacity
+    normed, placing, weights = pl.pallas_call(
+        lambda *refs: own_body(capacity, *refs),
+        grid=(1,),
+        in_specs=[whole(a.shape) for a in (rows_in, gain, router, chosen)],
+        out_specs=[
+            whole((tok_rows, features)),
+            whole((slots, tok_rows)),
+            whole((slots * 3 // 2, tok_rows)),
+        ],
+        out_shape=[
+            jax.ShapeDtypeStruct((tok_rows, features), jnp.bfloat16),
+            jax.ShapeDtypeStruct((slots, tok_rows), jnp.bfloat16),
+            jax.ShapeDtypeStruct((slots * 3 // 2, tok_rows), jnp.float32),
+        ],
+        compiler_params=pltpu.CompilerParams(vmem_limit_bytes=16 * MIB),
+        name="own_tokens",
+    )(rows_in, gain, router, chosen)
     sends = pl.pallas_call(
         lambda *refs: place_body(capacity, *refs),
-        in_specs=[VMEM] * 6,
-        out_specs=[VMEM] * (rounds + 1),
-        out_shape=[jax.ShapeDtypeStruct((span, features), jnp.bfloat16)] * rounds
-        + [jax.ShapeDtypeStruct((tok_rows, experts * capacity * 3 // 2), jnp.float32)],
-        compiler_params=pltpu.CompilerParams(vmem_limit_bytes=32 * MIB),
-    )(hidden_in[0], other_hidden, norm_gain[None], router_weight, routes[0], other_routes)
-    sends, weights = sends[:-1], sends[-1]
+        in_specs=[VMEM] * 5,
+        out_specs=[VMEM] * rounds,
+        out_shape=[jax.ShapeDtypeStruct((span, features), jnp.bfloat16)] * rounds,
+        compiler_params=pltpu.CompilerParams(vmem_limit_bytes=16 * MIB),
+        cost_estimate=pl.CostEstimate(flops=6 * 10**9, bytes_accessed=10**6, transcendentals=0),
+        name="place_rows",
+    )(normed, placing, other_rows, gain, other_routes)
     up, down = w_up[0], w_down[0]
-    up_other, down_other = over_section(up), over_section(down)
-
-    order = list(range(rounds))
-    order = [order[k] for k in (2, 3, 1, 0)] if rounds == 4 else order[::-1]
-    arrived = {k: over_groups(sends[k], k) for k in order}
-    returned, crossed = {}, {}
-    for k in (0, 2, 1, 3) if rounds == 4 else order:
-        across = over_x(arrived[k])
-        kept, sent = expert_work(arrived[k], across, up, down, up_other, down_other)
-        summed = (kept + over_x(sent).astype(jnp.float32)).astype(jnp.bfloat16)
+    up_other = over_section(after(up, other_rows, other_routes, normed))
+    down_other = over_section(after(down, other_rows, other_routes, normed))
+
+    last = rounds - 1
+    arrived, across, kept, sent, halves, returned, crossed = {}, {}, {}, {}, {}, {}, {}
+
+    def arrive(k, *others):
+        arrived[k] = (over_groups(after(sends[k], *others), k), 0)
+
+    def arrive_across_first(k):
+        pair = jnp.concatenate([sends[k], over_x(sends[k])], axis=0)
+        if each == 1:
+            pair = over_groups(pair, k)
+            arrived[k], across[k] = (pair, 0), (pair, 1)
+        else:
+            arrived[k] = (over_groups(pair[:span], k), 0)
+            across[k] = (over_groups(pair[span:], k), 0)
+
+    def exchange(k, *others):
+        across[k] = (over_x(after(arrived[k][0], *others)), 0)
+
+    def work(k, *others):
+        own = (after(arrived[k][0], *others), arrived[k][1])
+        kept[k], sent[k] = expert_work(span, own, across[k], up, down, up_other, down_other)
+
+    def cross(k, *others):
+        halves[k] = over_x(after(sent[k], *others))
+
+    def give_back(k):
+        summed = (kept[k] + halves[k].astype(jnp.float32)).astype(jnp.bfloat16)
         returned[k] = over_groups(summed, k)
         crossed[k] = over_section(
             returned[k].reshape(each, 2, capacity, features)[:, 1].reshape(each * capacity, features)
         )
+
+    if rounds == 4:
+        arrive(2)
+        arrive(1)
+        arrive(0)
+        arrive(3)
+        exchange(0)
+        exchange(2)
+        work(0)
+        exchange(1, kept[0])
+        cross(0)
+        work(1, kept[0])
+        exchange(3, kept[1])
+        work(2, kept[1])
+        cross(2)
+        give_back(2)
+        work(3, halves[2])
+        cross(3)
+        give_back(3)
+        cross(1, halves[2])
+        give_back(1)
+        give_back(0)
+    else:
+        for k in range(rounds):
+            arrive(k)
+            exchange(k)
+            work(k)
+            cross(k)
+            give_back(k)
     layer_out, sums = pl.pallas_call(
         lambda *refs: combine_body(rounds, sections * chips, *refs),
         in_specs=[VMEM] * (2 * rounds + 4),

time: 149 us -> 121 us (0.81)
  starting transfers between devices: 59.7 us -> 49.2 us
  blocking collectives: 16.7 us -> 10.6 us
  Pallas kernels: 33.7 us -> 28.7 us
  local copies, waits for them, and re-layouts: 8 us -> 3.95 us
  waiting for transfers between devices: 28.9 us -> 26.5 us
    ppermute x8, starting transfers between devices: 29.1 us -> 15.5 us  [over_section(): return lax.ppermute(value, 'section', [(0, 1), (1, 0)])]
    ppermute x8, waiting for transfers between devices: 0.02 us -> 11.8 us  [over_x(): return lax.ppermute(value, 'expert', [(i, i ^ 1) for i in range(chips)])]
    ppermute x8, waiting for transfers between devices: 22.1 us -> 12 us  [over_groups(): parts.append(lax.ppermute(part, both, pairs))]
    ppermute x8, starting transfers between devices: 9.2 us -> 16.8 us  [over_x(): return lax.ppermute(value, 'expert', [(i, i ^ 1) for i in range(chips)])]
    all_to_all x1, blocking collectives: 16.7 us -> 10.6 us  [local(): owned = lax.all_to_all(sums, both, split_axis=0, concat_axis=0, tiled=True)]
    pallas_call x4 -> x5, Pallas kernels: 30.1 us -> 25.5 us  [the longest x4 24.8 us: expert_work(): pl.pallas_call(expert_body, grid=(units // block,), in_specs=[pl.BlockSpe...]
    ppermute x8, starting transfers between devices: 21.4 us -> 17 us  [over_groups(): parts.append(lax.ppermute(part, both, pairs))]
    ppermute x8, waiting for transfers between devices: 6.81 us -> 2.74 us  [over_section(): return lax.ppermute(value, 'section', [(0, 1), (1, 0)])]
  transfers between devices with their start and end apart: 24 -> 24, of which waited for: 6 -> 9; matrix products, arithmetic and copies ran while one was open for 1% -> 0% of each run, Pallas kernels for 21% -> 22%
where the time goes in v2:
time: 121 us
  starting transfers between devices  49.2 us (41%)
  Pallas kernels  28.7 us (24%)
  waiting for transfers between devices  26.5 us (22%)
  blocking collectives  10.6 us (9%)
  local copies, waits for them, and re-layouts  3.95 us (3%)
    pallas_call x4, Pallas kernels, expert_work(): pl.pallas_call(expert_body, grid=(units // block,), in_specs=[pl.BlockSpe...  24.8 us
    ppermute x8, starting transfers between devices, over_groups(): parts.append(lax.ppermute(part, both, pairs))  17 us
    ppermute x8, starting transfers between devices, over_x(): return lax.ppermute(value, 'expert', [(i, i ^ 1) for i in range(chips)])  16.8 us
    ppermute x8, starting transfers between devices, over_section(): return lax.ppermute(value, 'section', [(0, 1), (1, 0)])  15.5 us
    ppermute x8, waiting for transfers between devices, over_groups(): parts.append(lax.ppermute(part, both, pairs))  12 us
    ppermute x8, waiting for transfers between devices, over_x(): return lax.ppermute(value, 'expert', [(i, i ^ 1) for i in range(chips)])  11.8 us
    all_to_all x1, blocking collectives, local(): owned = lax.all_to_all(sums, both, split_axis=0, concat_axis=0, tiled=True)  10.6 us
    unnamed x20, local copies, waits for them, and re-layouts  3.9 us
  transfers between devices with their start and end apart: 24, of which 9 were waited for; matrix products, arithmetic and copies ran while one was open for 0% of the time, Pallas kernels for 22%

profile of v2, /device:TPU:0, one launch (start us, length us, event | category | flops | bytes accessed | tf_op | source)
XLA Modules:
  0.0 120.8 jit_solution(14223500266012451892)
XLA Ops:
  0.6 0.5 collective-permute-start
  1.1 0.1 collective-permute-start.1
  1.2 1.0 copy-done.2
  2.3 0.8 copy-done.5
  3.0 0.7 copy-done.6
  3.7 0.7 copy-done.8
  4.4 0.7 own_tokens.1
  5.2 0.5 collective-permute-start.4
  5.7 0.1 collective-permute-start.5
  5.7 0.7 copy-done.7
  6.4 1.3 %place_rows.1 = (bf16[96,2048]{1,0:T(8,128)(2,1)S(1)}, bf16[96,2048]{1,0:T(8,128)(2,1)S(1)}, bf16[96,2048]{1,0:T(8,128)(2,1)S(1)}, bf16[96,2048]{1,0:T(8,128)(2,1)S(1)}) custom-call(bf16[128,2048]{1,0:T(8,128)(2,1)S(1)} %get-tuple-element.26.refs_0_, bf16[384,128]{1,0:T(8,128)(2,1)S(1)} %get-tuple-element.27.refs_1_, ...), custom_call_target="tpu_custom_call" | custom-call | flops 6000000000 | bytes 1000000 | tf_op jit(solution)/shard_map/place_rows/pallas_call | solution.py:250
  7.7 0.8 collective-permute-start.2
  8.6 3.0 %collective-permute-start.3 = (bf16[96,2048]{1,0:T(8,128)(2,1)S(1)}, bf16[96,2048]{1,0:T(8,128)(2,1)S(1)}, u32[]{:S(2)}, u32[]{:S(2)}) collective-permute-start(bf16[96,2048]{1,0:T(8,128)(2,1)S(1)} %collective-permute-done.2.own), channel_id=1, source_target_pairs={{0,1},{1,0},{2,3},{3,2},{4,5},{5,4},{6,7},{7,6},{8,9},{9,8},{10,11... | collective-permute-start | bytes 1179656 | tf_op jit(solution)/shard_map/ppermute | solution.py:213
  11.6 1.6 %collective-permute-start.8 = (bf16[96,2048]{1,0:T(8,128)(2,1)S(1)}, bf16[96,2048]{1,0:T(8,128)(2,1)S(1)}, u32[]{:S(2)}, u32[]{:S(2)}) collective-permute-start(bf16[96,2048]{1,0:T(8,128)(2,1)S(1)} %get-tuple-element.33), channel_id=1, source_target_pairs={{0,4},{1,5},{2,6},{3,7},{4,0},{5,1},{6,2},{7,3},{8,12},{9,13},{10,... | collective-permute-start | bytes 1179656 | tf_op jit(solution)/shard_map/ppermute | solution.py:225
  13.1 2.6 %collective-permute-start.10 = (bf16[96,2048]{1,0:T(8,128)(2,1)S(1)}, bf16[96,2048]{1,0:T(8,128)(2,1)S(1)}, u32[]{:S(2)}, u32[]{:S(2)}) collective-permute-start(bf16[96,2048]{1,0:T(8,128)(2,1)S(1)} %get-tuple-element.37), channel_id=1, source_target_pairs={{0,8},{1,9},{2,10},{3,11},{4,12},{5,13},{6,14},{7,15},{8,0},{9,1},... | collective-permute-start | bytes 1179656 | tf_op jit(solution)/shard_map/ppermute | solution.py:225
  15.7 1.6 %collective-permute-done.3.across = bf16[96,2048]{1,0:T(8,128)(2,1)S(1)} collective-permute-done((bf16[96,2048]{1,0:T(8,128)(2,1)S(1)}, bf16[96,2048]{1,0:T(8,128)(2,1)S(1)}, u32[]{:S(2)}, u32[]{:S(2)}) %collective-permute-start.3) | collective-permute-done | bytes 393248 | tf_op jit(solution)/shard_map/ppermute | solution.py:213
  17.3 1.3 %collective-permute-done.5.down_other = bf16[1024,2048]{1,0:T(8,128)(2,1)S(1)} collective-permute-done((bf16[1024,2048]{1,0:T(8,128)(2,1)}, bf16[1024,2048]{1,0:T(8,128)(2,1)S(1)}, u32[]{:S(2)}, u32[]{:S(2)}) %collective-permute-start.5) | collective-permute-done | bytes 4194336 | tf_op jit(solution)/shard_map/ppermute | solution.py:210
  18.7 6.2 %expert.4 = (f32[96,2048]{1,0:T(8,128)S(1)}, bf16[96,2048]{1,0:T(8,128)(2,1)S(1)}) custom-call(bf16[96,2048]{1,0:T(8,128)(2,1)S(1)} %collective-permute-done.2.own, bf16[96,2048]{1,0:T(8,128)(2,1)S(1)} %collective-permute-done.3.across, bf16[2048,1024]{1,0:T(8,128)(2,1)S(1)} %bitcast.31, bf16[1024,2048]{1,0:T(8,128)(2,1)S(1)} %bitcast.36, ...), custom_call_target="tpu_custom_call" | custom-call | flops 3221225472 | bytes 16777216 | tf_op jit(solution)/shard_map/expert/pallas_call | solution.py:137
  24.9 2.9 %collective-permute-start.9 = (bf16[96,2048]{1,0:T(8,128)(2,1)S(1)}, bf16[96,2048]{1,0:T(8,128)(2,1)S(1)}, u32[]{:S(2)}, u32[]{:S(2)}) collective-permute-start(bf16[96,2048]{1,0:T(8,128)(2,1)S(1)} %collective-permute-done.8.own), channel_id=1, source_target_pairs={{0,1},{1,0},{2,3},{3,2},{4,5},{5,4},{6,7},{7,6},{8,9},{9,8},{10,11... | collective-permute-start | bytes 1179656 | tf_op jit(solution)/shard_map/ppermute | solution.py:213
  27.8 0.1 collective-permute-start.11
  27.9 4.1 %collective-permute-start.16 = (bf16[96,2048]{1,0:T(8,128)(2,1)S(1)}, bf16[96,2048]{1,0:T(8,128)(2,1)S(1)}, u32[]{:S(2)}, u32[]{:S(2)}) collective-permute-start(bf16[96,2048]{1,0:T(8,128)(2,1)S(1)} %get-tuple-element.42), channel_id=1, source_target_pairs={{0,12},{1,13},{2,14},{3,15},{4,8},{5,9},{6,10},{7,11},{8,4},{9,5},... | collective-permute-start | bytes 1179656 | tf_op jit(solution)/shard_map/ppermute | solution.py:225
  31.9 1.5 %collective-permute-start.6 = (bf16[96,2048]{1,0:T(8,128)(2,1)S(1)}, bf16[96,2048]{1,0:T(8,128)(2,1)S(1)}, u32[]{:S(2)}, u32[]{:S(2)}) collective-permute-start(bf16[96,2048]{1,0:T(8,128)(2,1)S(1)} %get-tuple-element.32), channel_id=1, source_target_pairs={{0,1},{1,0},{2,3},{3,2},{4,5},{5,4},{6,7},{7,6},{8,9},{9,8},{10,11... | collective-permute-start | bytes 1179656 | tf_op jit(solution)/shard_map/ppermute | solution.py:213
  33.4 0.1 collective-permute-done.9.across
  33.5 6.2 %expert.5 = (f32[96,2048]{1,0:T(8,128)S(1)}, bf16[96,2048]{1,0:T(8,128)(2,1)S(1)}) custom-call(bf16[96,2048]{1,0:T(8,128)(2,1)S(1)} %collective-permute-done.8.own, bf16[96,2048]{1,0:T(8,128)(2,1)S(1)} %collective-permute-done.9.across, bf16[2048,1024]{1,0:T(8,128)(2,1)S(1)} %bitcast.32, bf16[1024,2048]{1,0:T(8,128)(2,1)S(1)} %bitcast.37, ...), custom_call_target="tpu_custom_call" | custom-call | flops 3221225472 | bytes 16777216 | tf_op jit(solution)/shard_map/expert/pallas_call | solution.py:137
  39.8 1.6 %collective-permute-done.11.across = bf16[96,2048]{1,0:T(8,128)(2,1)S(1)} collective-permute-done((bf16[96,2048]{1,0:T(8,128)(2,1)S(1)}, bf16[96,2048]{1,0:T(8,128)(2,1)S(1)}, u32[]{:S(2)}, u32[]{:S(2)}) %collective-permute-start.11) | collective-permute-done | bytes 393248 | tf_op jit(solution)/shard_map/ppermute | solution.py:213
  41.4 6.2 %expert.6 = (f32[96,2048]{1,0:T(8,128)S(1)}, bf16[96,2048]{1,0:T(8,128)(2,1)S(1)}) custom-call(bf16[96,2048]{1,0:T(8,128)(2,1)S(1)} %collective-permute-done.10.own, bf16[96,2048]{1,0:T(8,128)(2,1)S(1)} %collective-permute-done.11.across, bf16[2048,1024]{1,0:T(8,128)(2,1)S(1)} %bitcast.33, bf16[1024,2048]{1,0:T(8,128)(2,1)S(1)} %bitcast.38, ...), custom_call_target="tpu_custom_call" | custom-call | flops 3221225472 | bytes 16777216 | tf_op jit(solution)/shard_map/expert/pallas_call | solution.py:137
  47.6 2.6 %collective-permute-start.12 = (bf16[96,2048]{1,0:T(8,128)(2,1)S(1)}, bf16[96,2048]{1,0:T(8,128)(2,1)S(1)}, u32[]{:S(2)}, u32[]{:S(2)}) collective-permute-start(bf16[96,2048]{1,0:T(8,128)(2,1)S(1)} %get-tuple-element.39), channel_id=1, source_target_pairs={{0,1},{1,0},{2,3},{3,2},{4,5},{5,4},{6,7},{7,6},{8,9},{9,8},{10,11... | collective-permute-start | bytes 1179656 | tf_op jit(solution)/shard_map/ppermute | solution.py:213
  50.1 0.1 add_convert_fusion.3
  50.2 0.7 collective-permute-start.7
  50.9 2.2 %collective-permute-start.17 = (bf16[96,2048]{1,0:T(8,128)(2,1)S(1)}, bf16[96,2048]{1,0:T(8,128)(2,1)S(1)}, u32[]{:S(2)}, u32[]{:S(2)}) collective-permute-start(bf16[96,2048]{1,0:T(8,128)(2,1)S(1)} %collective-permute-done.16.own), channel_id=1, source_target_pairs={{0,1},{1,0},{2,3},{3,2},{4,5},{5,4},{6,7},{7,6},{8,9},{9,8},{10,11... | collective-permute-start | bytes 1179656 | tf_op jit(solution)/shard_map/ppermute | solution.py:213
  53.1 5.7 %collective-permute-done.12 = bf16[96,2048]{1,0:T(8,128)(2,1)S(1)} collective-permute-done((bf16[96,2048]{1,0:T(8,128)(2,1)S(1)}, bf16[96,2048]{1,0:T(8,128)(2,1)S(1)}, u32[]{:S(2)}, u32[]{:S(2)}) %collective-permute-start.12) | collective-permute-done | bytes 393248 | tf_op jit(solution)/shard_map/ppermute | solution.py:213
  58.8 2.0 %collective-permute-start.13 = (bf16[96,2048]{1,0:T(8,128)(2,1)S(1)}, bf16[96,2048]{1,0:T(8,128)(2,1)S(1)}, u32[]{:S(2)}, u32[]{:S(2)}) collective-permute-start(bf16[96,2048]{1,0:T(8,128)(2,1)S(1)} %get-tuple-element.40), channel_id=1, source_target_pairs={{0,1},{1,0},{2,3},{3,2},{4,5},{5,4},{6,7},{7,6},{8,9},{9,8},{10,11... | collective-permute-start | bytes 1179656 | tf_op jit(solution)/shard_map/ppermute | solution.py:213
  60.9 2.6 %collective-permute-start.15 = (bf16[96,2048]{1,0:T(8,128)(2,1)S(1)}, bf16[96,2048]{1,0:T(8,128)(2,1)S(1)}, u32[]{:S(2)}, u32[]{:S(2)}) collective-permute-start(bf16[96,2048]{1,0:T(8,128)(2,1)S(1)} %add_convert_fusion.1), channel_id=1, source_target_pairs={{0,8},{1,9},{2,10},{3,11},{4,12},{5,13},{6,14},{7,15},{8,0},{9,1},... | collective-permute-start | bytes 1179656 | tf_op jit(solution)/shard_map/ppermute | solution.py:225
  63.6 2.8 %collective-permute-done.17.across = bf16[96,2048]{1,0:T(8,128)(2,1)S(1)} collective-permute-done((bf16[96,2048]{1,0:T(8,128)(2,1)S(1)}, bf16[96,2048]{1,0:T(8,128)(2,1)S(1)}, u32[]{:S(2)}, u32[]{:S(2)}) %collective-permute-start.17) | collective-permute-done | bytes 393248 | tf_op jit(solution)/shard_map/ppermute | solution.py:213
  66.3 6.2 %expert.7 = (f32[96,2048]{1,0:T(8,128)S(1)}, bf16[96,2048]{1,0:T(8,128)(2,1)S(1)}) custom-call(bf16[96,2048]{1,0:T(8,128)(2,1)S(1)} %collective-permute-done.16.own, bf16[96,2048]{1,0:T(8,128)(2,1)S(1)} %collective-permute-done.17.across, bf16[2048,1024]{1,0:T(8,128)(2,1)S(1)} %bitcast.34, bf16[1024,2048]{1,0:T(8,128)(2,1)S(1)} %bitcast.39, ...), custom_call_target="tpu_custom_call" | custom-call | flops 3221225472 | bytes 16777216 | tf_op jit(solution)/shard_map/expert/pallas_call | solution.py:137
  72.6 2.5 %collective-permute-start.18 = (bf16[96,2048]{1,0:T(8,128)(2,1)S(1)}, bf16[96,2048]{1,0:T(8,128)(2,1)S(1)}, u32[]{:S(2)}, u32[]{:S(2)}) collective-permute-start(bf16[96,2048]{1,0:T(8,128)(2,1)S(1)} %get-tuple-element.46), channel_id=1, source_target_pairs={{0,1},{1,0},{2,3},{3,2},{4,5},{5,4},{6,7},{7,6},{8,9},{9,8},{10,11... | collective-permute-start | bytes 1179656 | tf_op jit(solution)/shard_map/ppermute | solution.py:213
  75.1 8.5 %collective-permute-start.20 = (bf16[48,2048]{1,0:T(8,128)(2,1)S(1)}, bf16[48,2048]{1,0:T(8,128)(2,1)S(1)}, u32[]{:S(2)}, u32[]{:S(2)}) collective-permute-start(bf16[48,2048]{1,0:T(8,128)(2,1)S(1)} %slice_bitcast_fusion.3), channel_id=1, source_target_pairs={{0,16},{16,0},{1,17},{17,1},{2,18},{18,2},{3,19},{19,3},{4,20},{20... | collective-permute-start | bytes 589832 | tf_op jit(solution)/shard_map/ppermute | solution.py:210
  83.6 0.1 add_convert_fusion.2
  83.7 1.6 %collective-permute-start.14 = (bf16[96,2048]{1,0:T(8,128)(2,1)S(1)}, bf16[96,2048]{1,0:T(8,128)(2,1)S(1)}, u32[]{:S(2)}, u32[]{:S(2)}) collective-permute-start(bf16[96,2048]{1,0:T(8,128)(2,1)S(1)} %add_convert_fusion.2), channel_id=1, source_target_pairs={{0,4},{1,5},{2,6},{3,7},{4,0},{5,1},{6,2},{7,3},{8,12},{9,13},{10,... | collective-permute-start | bytes 1179656 | tf_op jit(solution)/shard_map/ppermute | solution.py:225
  85.4 3.0 %collective-permute-start.19 = (bf16[96,2048]{1,0:T(8,128)(2,1)S(1)}, bf16[96,2048]{1,0:T(8,128)(2,1)S(1)}, u32[]{:S(2)}, u32[]{:S(2)}) collective-permute-start(bf16[96,2048]{1,0:T(8,128)(2,1)S(1)} %add_convert_fusion), channel_id=1, source_target_pairs={{0,12},{1,13},{2,14},{3,15},{4,8},{5,9},{6,10},{7,11},{8,4},{9,5},... | collective-permute-start | bytes 1179656 | tf_op jit(solution)/shard_map/ppermute | solution.py:225
  88.4 5.6 %collective-permute-start.22 = (bf16[48,2048]{1,0:T(8,128)(2,1)S(1)}, bf16[48,2048]{1,0:T(8,128)(2,1)S(1)}, u32[]{:S(2)}, u32[]{:S(2)}) collective-permute-start(bf16[48,2048]{1,0:T(8,128)(2,1)S(1)} %slice_bitcast_fusion.1), channel_id=1, source_target_pairs={{0,16},{16,0},{1,17},{17,1},{2,18},{18,2},{3,19},{19,3},{4,20},{20... | collective-permute-start | bytes 589832 | tf_op jit(solution)/shard_map/ppermute | solution.py:210
  94.0 1.4 %collective-permute-done.14.refs_1_ = bf16[96,2048]{1,0:T(8,128)(2,1)S(1)} collective-permute-done((bf16[96,2048]{1,0:T(8,128)(2,1)S(1)}, bf16[96,2048]{1,0:T(8,128)(2,1)S(1)}, u32[]{:S(2)}, u32[]{:S(2)}) %collective-permute-start.14) | collective-permute-done | bytes 393248 | tf_op jit(solution)/shard_map/ppermute | solution.py:225
  95.6 10.6 %collective-permute-done.19.refs_3_ = bf16[96,2048]{1,0:T(8,128)(2,1)S(1)} collective-permute-done((bf16[96,2048]{1,0:T(8,128)(2,1)S(1)}, bf16[96,2048]{1,0:T(8,128)(2,1)S(1)}, u32[]{:S(2)}, u32[]{:S(2)}) %collective-permute-start.19) | collective-permute-done | bytes 393248 | tf_op jit(solution)/shard_map/ppermute | solution.py:225
  106.3 1.4 %collective-permute-done.23.refs_7_ = bf16[48,2048]{1,0:T(8,128)(2,1)S(1)} collective-permute-done((bf16[48,2048]{1,0:T(8,128)(2,1)S(1)}, bf16[48,2048]{1,0:T(8,128)(2,1)S(1)}, u32[]{:S(2)}, u32[]{:S(2)}) %collective-permute-start.23) | collective-permute-done | bytes 196640 | tf_op jit(solution)/shard_map/ppermute | solution.py:210
  107.7 1.9 %shard_map.95 = (bf16[128,2048]{1,0:T(8,128)(2,1)}, f32[32,128]{1,0:T(8,128)S(1)}) custom-call(bf16[96,2048]{1,0:T(8,128)(2,1)S(1)} %collective-permute-done.7.refs_0_, bf16[96,2048]{1,0:T(8,128)(2,1)S(1)} %collective-permute-done.14.refs_1_, bf16[96,2048]{1,0:T(8,128)(2,1)S(1)} %collective-permute-done.15.refs_2_, ...), custom_call_target="tpu_custom_call" | custom-call | tf_op jit(solution)/shard_map/pallas_call | solution.py:323
  109.6 10.6 %all_to_all.9 = f32[32,1,128]{2,1,0:T(1,128)S(1)} all-to-all(f32[32,1,128]{2,1,0:T(1,128)S(1)} %bitcast.49), channel_id=1, replica_groups=mesh['section'=2,'expert'=16] {'section','expert'}, dimensions={0} | all-to-all | bytes 32768 | tf_op jit(solution)/shard_map/all_to_all | solution.py:340
  120.2 0.1 slice_divide_fusion
  120.3 0.5 add_bitcast_fusion
  (39 shorter events, 0.4 us)
Async XLA Ops:
  0.6 4.5 %collective-permute-start = (bf16[128,2048]{1,0:T(8,128)(2,1)}, bf16[128,2048]{1,0:T(8,128)(2,1)S(1)}, u32[]{:S(2)}, u32[]{:S(2)}) collective-permute-start(bf16[128,2048]{1,0:T(8,128)(2,1)} %bitcast.40), channel_id=1, source_target_pairs={{0,16},{16,0},{1,17},{17,1},{2,18},{18,2},{3,19},{19,3},{4,20},{20... | collective-permute-start | bytes 1572872 | tf_op jit(solution)/shard_map/ppermute | solution.py:210
  1.1 4.0 %collective-permute-start.1 = (s32[2,128]{1,0:T(2,128)}, s32[2,128]{1,0:T(2,128)S(1)}, u32[]{:S(2)}, u32[]{:S(2)}) collective-permute-start(s32[2,128]{1,0:T(2,128)} %bitcast.52), channel_id=1, source_target_pairs={{0,16},{16,0},{1,17},{17,1},{2,18},{18,2},{3,19},{19,3},{4,20},{20... | collective-permute-start | bytes 3080 | tf_op jit(solution)/shard_map/ppermute | solution.py:210
  1.2 1.0 copy-start.2
  2.3 0.8 copy-start.5
  3.0 0.7 copy-start.6
  3.7 0.7 copy-start.8
  5.2 12.2 %collective-permute-start.4 = (bf16[2048,1024]{1,0:T(8,128)(2,1)}, bf16[2048,1024]{1,0:T(8,128)(2,1)S(1)}, u32[]{:S(2)}, u32[]{:S(2)}) collective-permute-start(bf16[2048,1024]{1,0:T(8,128)(2,1)} %bitcast.30), channel_id=1, source_target_pairs={{0,16},{16,0},{1,17},{17,1},{2,18},{18,2},{3,19},{19,3},{4,20},{20... | collective-permute-start | bytes 12582920 | tf_op jit(solution)/shard_map/ppermute | solution.py:210
  5.7 13.0 %collective-permute-start.5 = (bf16[1024,2048]{1,0:T(8,128)(2,1)}, bf16[1024,2048]{1,0:T(8,128)(2,1)S(1)}, u32[]{:S(2)}, u32[]{:S(2)}) collective-permute-start(bf16[1024,2048]{1,0:T(8,128)(2,1)} %bitcast.35), channel_id=1, source_target_pairs={{0,16},{16,0},{1,17},{17,1},{2,18},{18,2},{3,19},{19,3},{4,20},{20... | collective-permute-start | bytes 12582920 | tf_op jit(solution)/shard_map/ppermute | solution.py:210
  5.7 0.7 copy-start.7
  6.4 12.2 %copy-start = (bf16[1,2048,1024]{2,1,0:T(8,128)(2,1)S(1)}, bf16[1,2048,1024]{2,1,0:T(8,128)(2,1)}, u32[]{:S(2)}) copy-start(bf16[1,2048,1024]{2,1,0:T(8,128)(2,1)} %param.12) | copy-start | bytes 12582916
  6.4 12.2 %copy-start.1 = (bf16[1,1024,2048]{2,1,0:T(8,128)(2,1)S(1)}, bf16[1,1024,2048]{2,1,0:T(8,128)(2,1)}, u32[]{:S(2)}) copy-start(bf16[1,1024,2048]{2,1,0:T(8,128)(2,1)} %param.13) | copy-start | bytes 12582916
  7.7 0.8 collective-permute-start.2
  8.6 8.7 %collective-permute-start.3 = (bf16[96,2048]{1,0:T(8,128)(2,1)S(1)}, bf16[96,2048]{1,0:T(8,128)(2,1)S(1)}, u32[]{:S(2)}, u32[]{:S(2)}) collective-permute-start(bf16[96,2048]{1,0:T(8,128)(2,1)S(1)} %collective-permute-done.2.own), channel_id=1, source_target_pairs={{0,1},{1,0},{2,3},{3,2},{4,5},{5,4},{6,7},{7,6},{8,9},{9,8},{10,11... | collective-permute-start | bytes 1179656 | tf_op jit(solution)/shard_map/ppermute | solution.py:213
  11.6 13.3 %collective-permute-start.8 = (bf16[96,2048]{1,0:T(8,128)(2,1)S(1)}, bf16[96,2048]{1,0:T(8,128)(2,1)S(1)}, u32[]{:S(2)}, u32[]{:S(2)}) collective-permute-start(bf16[96,2048]{1,0:T(8,128)(2,1)S(1)} %get-tuple-element.33), channel_id=1, source_target_pairs={{0,4},{1,5},{2,6},{3,7},{4,0},{5,1},{6,2},{7,3},{8,12},{9,13},{10,... | collective-permute-start | bytes 1179656 | tf_op jit(solution)/shard_map/ppermute | solution.py:225
  13.1 14.7 %collective-permute-start.10 = (bf16[96,2048]{1,0:T(8,128)(2,1)S(1)}, bf16[96,2048]{1,0:T(8,128)(2,1)S(1)}, u32[]{:S(2)}, u32[]{:S(2)}) collective-permute-start(bf16[96,2048]{1,0:T(8,128)(2,1)S(1)} %get-tuple-element.37), channel_id=1, source_target_pairs={{0,8},{1,9},{2,10},{3,11},{4,12},{5,13},{6,14},{7,15},{8,0},{9,1},... | collective-permute-start | bytes 1179656 | tf_op jit(solution)/shard_map/ppermute | solution.py:225
  24.9 8.7 %collective-permute-start.9 = (bf16[96,2048]{1,0:T(8,128)(2,1)S(1)}, bf16[96,2048]{1,0:T(8,128)(2,1)S(1)}, u32[]{:S(2)}, u32[]{:S(2)}) collective-permute-start(bf16[96,2048]{1,0:T(8,128)(2,1)S(1)} %collective-permute-done.8.own), channel_id=1, source_target_pairs={{0,1},{1,0},{2,3},{3,2},{4,5},{5,4},{6,7},{7,6},{8,9},{9,8},{10,11... | collective-permute-start | bytes 1179656 | tf_op jit(solution)/shard_map/ppermute | solution.py:213
  27.8 13.6 %collective-permute-start.11 = (bf16[96,2048]{1,0:T(8,128)(2,1)S(1)}, bf16[96,2048]{1,0:T(8,128)(2,1)S(1)}, u32[]{:S(2)}, u32[]{:S(2)}) collective-permute-start(bf16[96,2048]{1,0:T(8,128)(2,1)S(1)} %collective-permute-done.10.own), channel_id=1, source_target_pairs={{0,1},{1,0},{2,3},{3,2},{4,5},{5,4},{6,7},{7,6},{8,9},{9,8},{10,11... | collective-permute-start | bytes 1179656 | tf_op jit(solution)/shard_map/ppermute | solution.py:213
  27.9 23.0 %collective-permute-start.16 = (bf16[96,2048]{1,0:T(8,128)(2,1)S(1)}, bf16[96,2048]{1,0:T(8,128)(2,1)S(1)}, u32[]{:S(2)}, u32[]{:S(2)}) collective-permute-start(bf16[96,2048]{1,0:T(8,128)(2,1)S(1)} %get-tuple-element.42), channel_id=1, source_target_pairs={{0,12},{1,13},{2,14},{3,15},{4,8},{5,9},{6,10},{7,11},{8,4},{9,5},... | collective-permute-start | bytes 1179656 | tf_op jit(solution)/shard_map/ppermute | solution.py:225
  31.9 18.2 %collective-permute-start.6 = (bf16[96,2048]{1,0:T(8,128)(2,1)S(1)}, bf16[96,2048]{1,0:T(8,128)(2,1)S(1)}, u32[]{:S(2)}, u32[]{:S(2)}) collective-permute-start(bf16[96,2048]{1,0:T(8,128)(2,1)S(1)} %get-tuple-element.32), channel_id=1, source_target_pairs={{0,1},{1,0},{2,3},{3,2},{4,5},{5,4},{6,7},{7,6},{8,9},{9,8},{10,11... | collective-permute-start | bytes 1179656 | tf_op jit(solution)/shard_map/ppermute | solution.py:213
  47.6 11.3 %collective-permute-start.12 = (bf16[96,2048]{1,0:T(8,128)(2,1)S(1)}, bf16[96,2048]{1,0:T(8,128)(2,1)S(1)}, u32[]{:S(2)}, u32[]{:S(2)}) collective-permute-start(bf16[96,2048]{1,0:T(8,128)(2,1)S(1)} %get-tuple-element.39), channel_id=1, source_target_pairs={{0,1},{1,0},{2,3},{3,2},{4,5},{5,4},{6,7},{7,6},{8,9},{9,8},{10,11... | collective-permute-start | bytes 1179656 | tf_op jit(solution)/shard_map/ppermute | solution.py:213
  50.2 24.9 %collective-permute-start.7 = (bf16[96,2048]{1,0:T(8,128)(2,1)S(1)}, bf16[96,2048]{1,0:T(8,128)(2,1)S(1)}, u32[]{:S(2)}, u32[]{:S(2)}) collective-permute-start(bf16[96,2048]{1,0:T(8,128)(2,1)S(1)} %add_convert_fusion.3), channel_id=1, source_target_pairs={{0,0},{1,1},{2,2},{3,3},{4,4},{5,5},{6,6},{7,7},{8,8},{9,9},{10,10... | collective-permute-start | bytes 1179656 | tf_op jit(solution)/shard_map/ppermute | solution.py:225
  50.9 15.4 %collective-permute-start.17 = (bf16[96,2048]{1,0:T(8,128)(2,1)S(1)}, bf16[96,2048]{1,0:T(8,128)(2,1)S(1)}, u32[]{:S(2)}, u32[]{:S(2)}) collective-permute-start(bf16[96,2048]{1,0:T(8,128)(2,1)S(1)} %collective-permute-done.16.own), channel_id=1, source_target_pairs={{0,1},{1,0},{2,3},{3,2},{4,5},{5,4},{6,7},{7,6},{8,9},{9,8},{10,11... | collective-permute-start | bytes 1179656 | tf_op jit(solution)/shard_map/ppermute | solution.py:213
  58.8 24.8 %collective-permute-start.13 = (bf16[96,2048]{1,0:T(8,128)(2,1)S(1)}, bf16[96,2048]{1,0:T(8,128)(2,1)S(1)}, u32[]{:S(2)}, u32[]{:S(2)}) collective-permute-start(bf16[96,2048]{1,0:T(8,128)(2,1)S(1)} %get-tuple-element.40), channel_id=1, source_target_pairs={{0,1},{1,0},{2,3},{3,2},{4,5},{5,4},{6,7},{7,6},{8,9},{9,8},{10,11... | collective-permute-start | bytes 1179656 | tf_op jit(solution)/shard_map/ppermute | solution.py:213
  60.9 27.5 %collective-permute-start.15 = (bf16[96,2048]{1,0:T(8,128)(2,1)S(1)}, bf16[96,2048]{1,0:T(8,128)(2,1)S(1)}, u32[]{:S(2)}, u32[]{:S(2)}) collective-permute-start(bf16[96,2048]{1,0:T(8,128)(2,1)S(1)} %add_convert_fusion.1), channel_id=1, source_target_pairs={{0,8},{1,9},{2,10},{3,11},{4,12},{5,13},{6,14},{7,15},{8,0},{9,1},... | collective-permute-start | bytes 1179656 | tf_op jit(solution)/shard_map/ppermute | solution.py:225
  72.5 35.1 %copy-start.3 = (bf16[1,128,2048]{2,1,0:T(8,128)(2,1)S(1)}, bf16[1,128,2048]{2,1,0:T(8,128)(2,1)}, u32[]{:S(2)}) copy-start(bf16[1,128,2048]{2,1,0:T(8,128)(2,1)} %param.8) | copy-start | bytes 1572868
  72.6 35.1 %copy-start.4 = (bf16[1,128,2048]{2,1,0:T(8,128)(2,1)S(1)}, bf16[1,128,2048]{2,1,0:T(8,128)(2,1)}, u32[]{:S(2)}) copy-start(bf16[1,128,2048]{2,1,0:T(8,128)(2,1)} %param.9) | copy-start | bytes 1572868
  72.6 35.1 %copy-start.9 = (s32[1,128]{1,0:T(1,128)S(1)}, s32[1,128]{1,0:T(1,128)}, u32[]{:S(2)}) copy-start(s32[1,128]{1,0:T(1,128)} %refs_11_.1) | copy-start | bytes 1540
  72.6 12.8 %collective-permute-start.18 = (bf16[96,2048]{1,0:T(8,128)(2,1)S(1)}, bf16[96,2048]{1,0:T(8,128)(2,1)S(1)}, u32[]{:S(2)}, u32[]{:S(2)}) collective-permute-start(bf16[96,2048]{1,0:T(8,128)(2,1)S(1)} %get-tuple-element.46), channel_id=1, source_target_pairs={{0,1},{1,0},{2,3},{3,2},{4,5},{5,4},{6,7},{7,6},{8,9},{9,8},{10,11... | collective-permute-start | bytes 1179656 | tf_op jit(solution)/shard_map/ppermute | solution.py:213
  75.1 31.1 %collective-permute-start.20 = (bf16[48,2048]{1,0:T(8,128)(2,1)S(1)}, bf16[48,2048]{1,0:T(8,128)(2,1)S(1)}, u32[]{:S(2)}, u32[]{:S(2)}) collective-permute-start(bf16[48,2048]{1,0:T(8,128)(2,1)S(1)} %slice_bitcast_fusion.3), channel_id=1, source_target_pairs={{0,16},{16,0},{1,17},{17,1},{2,18},{18,2},{3,19},{19,3},{4,20},{20... | collective-permute-start | bytes 589832 | tf_op jit(solution)/shard_map/ppermute | solution.py:210
  83.7 11.8 %collective-permute-start.14 = (bf16[96,2048]{1,0:T(8,128)(2,1)S(1)}, bf16[96,2048]{1,0:T(8,128)(2,1)S(1)}, u32[]{:S(2)}, u32[]{:S(2)}) collective-permute-start(bf16[96,2048]{1,0:T(8,128)(2,1)S(1)} %add_convert_fusion.2), channel_id=1, source_target_pairs={{0,4},{1,5},{2,6},{3,7},{4,0},{5,1},{6,2},{7,3},{8,12},{9,13},{10,... | collective-permute-start | bytes 1179656 | tf_op jit(solution)/shard_map/ppermute | solution.py:225
  85.4 20.7 %collective-permute-start.19 = (bf16[96,2048]{1,0:T(8,128)(2,1)S(1)}, bf16[96,2048]{1,0:T(8,128)(2,1)S(1)}, u32[]{:S(2)}, u32[]{:S(2)}) collective-permute-start(bf16[96,2048]{1,0:T(8,128)(2,1)S(1)} %add_convert_fusion), channel_id=1, source_target_pairs={{0,12},{1,13},{2,14},{3,15},{4,8},{5,9},{6,10},{7,11},{8,4},{9,5},... | collective-permute-start | bytes 1179656 | tf_op jit(solution)/shard_map/ppermute | solution.py:225
  88.4 17.9 %collective-permute-start.22 = (bf16[48,2048]{1,0:T(8,128)(2,1)S(1)}, bf16[48,2048]{1,0:T(8,128)(2,1)S(1)}, u32[]{:S(2)}, u32[]{:S(2)}) collective-permute-start(bf16[48,2048]{1,0:T(8,128)(2,1)S(1)} %slice_bitcast_fusion.1), channel_id=1, source_target_pairs={{0,16},{16,0},{1,17},{17,1},{2,18},{18,2},{3,19},{19,3},{4,20},{20... | collective-permute-start | bytes 589832 | tf_op jit(solution)/shard_map/ppermute | solution.py:210
  95.5 10.8 %collective-permute-start.21 = (bf16[48,2048]{1,0:T(8,128)(2,1)S(1)}, bf16[48,2048]{1,0:T(8,128)(2,1)S(1)}, u32[]{:S(2)}, u32[]{:S(2)}) collective-permute-start(bf16[48,2048]{1,0:T(8,128)(2,1)S(1)} %slice_bitcast_fusion.2), channel_id=1, source_target_pairs={{0,16},{16,0},{1,17},{17,1},{2,18},{18,2},{3,19},{19,3},{4,20},{20... | collective-permute-start | bytes 589832 | tf_op jit(solution)/shard_map/ppermute | solution.py:210
  106.2 1.5 %collective-permute-start.23 = (bf16[48,2048]{1,0:T(8,128)(2,1)S(1)}, bf16[48,2048]{1,0:T(8,128)(2,1)S(1)}, u32[]{:S(2)}, u32[]{:S(2)}) collective-permute-start(bf16[48,2048]{1,0:T(8,128)(2,1)S(1)} %slice_bitcast_fusion), channel_id=1, source_target_pairs={{0,16},{16,0},{1,17},{17,1},{2,18},{18,2},{3,19},{19,3},{4,20},{20... | collective-permute-start | bytes 589832 | tf_op jit(solution)/shard_map/ppermute | solution.py:210

commit v3 on v2

--- a/solution.py
+++ b/solution.py
@@ -36,23 +36,26 @@
     return lax.optimization_barrier((value, *others))[0] if others else value
 
 
-def lay_out(capacity, turn, values, gain, routes):
+def order_body(before):
+    before[...] = jnp.where(
+        lax.broadcasted_iota(jnp.int32, before.shape, 0)
+        < lax.broadcasted_iota(jnp.int32, before.shape, 1),
+        1.0,
+        0.0,
+    ).astype(jnp.bfloat16)
+
+
+def lay_out(capacity, turn, values, gain, routes, before):
     tok_rows = values.shape[0]
     experts = 3 * tok_rows // capacity
     side = lax.axis_index("section")
     group = lax.axis_index("expert") // 2
     normed = normalize(values[...].astype(jnp.float32), gain[...]).astype(jnp.bfloat16)
     expert_ids = lax.broadcasted_iota(jnp.int32, (experts, tok_rows), 0)
-    before = jnp.where(
-        lax.broadcasted_iota(jnp.int32, (tok_rows, tok_rows), 0)
-        < lax.broadcasted_iota(jnp.int32, (tok_rows, tok_rows), 1),
-        1.0,
-        0.0,
-    ).astype(jnp.bfloat16)
     chosen = [routes[k : k + 1, :] for k in range(2)]
     named = [c == expert_ids for c in chosen]
     member = jnp.where(named[0] | named[1], 1.0, 0.0).astype(jnp.bfloat16)
-    earlier = jnp.dot(member, before, preferred_element_type=jnp.float32)
+    earlier = jnp.dot(member, before[...], preferred_element_type=jnp.float32)
     place = [column_sum(jnp.where(n, earlier, 0.0)).astype(jnp.int32) for n in named]
     step = [c ^ group for c in chosen]
     mine = [(k & 1) == side for k in step]
@@ -67,8 +70,9 @@
     return normed, placing, named, back
 
 
-def own_body(capacity, hidden, gain, router, routes, rows, place, weights):
-    normed, placing, named, back = lay_out(capacity, 0, hidden, gain, routes)
+def own_body(capacity, hidden, gain, router, routes, before, rows, place, weights, gain_out):
+    gain_out[...] = gain[...]
+    normed, placing, named, back = lay_out(capacity, 0, hidden, gain, routes, before)
     rows[...] = normed
     place[...] = placing
     logits = lax.dot_general(
@@ -85,8 +89,8 @@
     )
 
 
-def place_body(capacity, rows, place, other, gain, routes, *sends):
-    normed, placing, _, _ = lay_out(capacity, 1, other, gain, routes)
+def place_body(capacity, rows, place, other, gain, routes, before, *sends):
+    normed, placing, _, _ = lay_out(capacity, 1, other, gain, routes, before)
     sent = (
         jnp.dot(place[...], rows[...], preferred_element_type=jnp.float32)
         + jnp.dot(placing, normed, preferred_element_type=jnp.float32)
@@ -130,7 +134,7 @@
 def expert_work(span, own, across, up, down, up_other, down_other):
     features = own[0].shape[1]
     units = up.shape[1]
-    block = min(256, units)
+    block = min(512, units)
     rows_spec = pl.BlockSpec((span, features), lambda i: (0, 0))
     up_spec = pl.BlockSpec((features, block), lambda i: (0, i))
     down_spec = pl.BlockSpec((block, features), lambda i: (i, 0))
@@ -164,12 +168,14 @@
     )(own[0], across[0], up, down, up_other, down_other)
 
 
-def combine_body(rounds, pair_rows, *refs):
-    returned, crossed = refs[:rounds], refs[rounds : 2 * rounds]
-    weights, hidden, target, pairs, layer_out, sums = refs[2 * rounds :]
+def combine_body(swapped, rounds, pair_rows, *refs):
+    returned, crossed = refs[:rounds], refs[rounds:-6]
+    weights, hidden, target, pairs, layer_out, sums = refs[-6:]
     features = hidden.shape[1]
-    span, half = returned[0].shape[0], crossed[0].shape[0]
-    gate = weights[...]
+    own = sum(r.shape[0] for r in returned)
+    half = own // rounds // 2
+    sources = [weights[:own]] + [weights[own + k * half : own + (k + 1) * half] for k in swapped]
+    gate = jnp.concatenate(sources, axis=0)
     high = gate.astype(jnp.bfloat16)
     low = (gate - high.astype(jnp.float32)).astype(jnp.bfloat16)
     total = hidden[...].astype(jnp.float32)
@@ -230,38 +236,44 @@
     other_rows = over_section(rows_in)
     other_routes = over_section(chosen)
     slots = experts * capacity
-    normed, placing, weights = pl.pallas_call(
+    before = pl.pallas_call(
+        order_body,
+        out_specs=VMEM,
+        out_shape=jax.ShapeDtypeStruct((tok_rows, tok_rows), jnp.bfloat16),
+        compiler_params=pltpu.CompilerParams(vmem_limit_bytes=16 * MIB),
+        cost_estimate=pl.CostEstimate(flops=2 * 10**9, bytes_accessed=10**6, transcendentals=0),
+        name="token_order",
+    )()
+    normed, placing, weights, gain = pl.pallas_call(
         lambda *refs: own_body(capacity, *refs),
-        grid=(1,),
-        in_specs=[whole(a.shape) for a in (rows_in, gain, router, chosen)],
-        out_specs=[
-            whole((tok_rows, features)),
-            whole((slots, tok_rows)),
-            whole((slots * 3 // 2, tok_rows)),
-        ],
+        in_specs=[VMEM] * 5,
+        out_specs=[VMEM] * 4,
         out_shape=[
             jax.ShapeDtypeStruct((tok_rows, features), jnp.bfloat16),
             jax.ShapeDtypeStruct((slots, tok_rows), jnp.bfloat16),
             jax.ShapeDtypeStruct((slots * 3 // 2, tok_rows), jnp.float32),
+            jax.ShapeDtypeStruct(gain.shape, jnp.float32),
         ],
         compiler_params=pltpu.CompilerParams(vmem_limit_bytes=16 * MIB),
         name="own_tokens",
-    )(rows_in, gain, router, chosen)
+    )(rows_in, gain, router, chosen, before)
     sends = pl.pallas_call(
         lambda *refs: place_body(capacity, *refs),
-        in_specs=[VMEM] * 5,
+        in_specs=[VMEM] * 6,
         out_specs=[VMEM] * rounds,
         out_shape=[jax.ShapeDtypeStruct((span, features), jnp.bfloat16)] * rounds,
         compiler_params=pltpu.CompilerParams(vmem_limit_bytes=16 * MIB),
         cost_estimate=pl.CostEstimate(flops=6 * 10**9, bytes_accessed=10**6, transcendentals=0),
         name="place_rows",
-    )(normed, placing, other_rows, gain, other_routes)
+    )(normed, placing, other_rows, gain, other_routes, before)
     up, down = w_up[0], w_down[0]
     up_other = over_section(after(up, other_rows, other_routes, normed))
+
+    last = rounds - 1
     down_other = over_section(after(down, other_rows, other_routes, normed))
 
-    last = rounds - 1
-    arrived, across, kept, sent, halves, returned, crossed = {}, {}, {}, {}, {}, {}, {}
+    arrived, across, kept, sent, halves, returned = {}, {}, {}, {}, {}, {}
+    crossed, swapped = [], []
 
     def arrive(k, *others):
         arrived[k] = (over_groups(after(sends[k], *others), k), 0)
@@ -288,9 +300,15 @@
     def give_back(k):
         summed = (kept[k] + halves[k].astype(jnp.float32)).astype(jnp.bfloat16)
         returned[k] = over_groups(summed, k)
-        crossed[k] = over_section(
+
+    def swap(ks, *others):
+        halves_out = [
             returned[k].reshape(each, 2, capacity, features)[:, 1].reshape(each * capacity, features)
-        )
+            for k in ks
+        ]
+        value = halves_out[0] if len(ks) == 1 else jnp.concatenate(halves_out, axis=0)
+        crossed.append(over_section(after(value, *others)))
+        swapped.extend(ks)
 
     if rounds == 4:
         arrive(2)
@@ -313,6 +331,10 @@
         cross(1, halves[2])
         give_back(1)
         give_back(0)
+        swap((0,), halves[1], halves[3])
+        swap((2,), halves[1], halves[3])
+        swap((3,))
+        swap((1,))
     else:
         for k in range(rounds):
             arrive(k)
@@ -320,9 +342,10 @@
             work(k)
             cross(k)
             give_back(k)
+            swap((k,))
     layer_out, sums = pl.pallas_call(
-        lambda *refs: combine_body(rounds, sections * chips, *refs),
-        in_specs=[VMEM] * (2 * rounds + 4),
+        lambda *refs: combine_body(swapped, rounds, sections * chips, *refs),
+        in_specs=[VMEM] * (rounds + len(crossed) + 4),
         out_specs=[VMEM] * 2,
         out_shape=[
             jax.ShapeDtypeStruct((tok_rows, features), jnp.bfloat16),
@@ -331,7 +354,7 @@
         compiler_params=pltpu.CompilerParams(vmem_limit_bytes=32 * MIB),
     )(
         *[returned[k] for k in range(rounds)],
-        *[crossed[k] for k in range(rounds)],
+        *crossed,
         weights,
         hidden_in[0],
         target_rows[0],

time: 121 us -> 119 us (0.983)
  Pallas kernels: 28.7 us -> 23.1 us
  blocking collectives: 10.6 us -> 15.5 us
  local copies, waits for them, and re-layouts: 3.95 us -> 0.57 us
  waiting for transfers between devices: 26.5 us -> 28.8 us
    ppermute x8, waiting for transfers between devices: 11.8 us -> 19.4 us  [over_x(): return lax.ppermute(value, 'expert', [(i, i ^ 1) for i in range(chips)])]
    ppermute x8, waiting for transfers between devices: 12 us -> 5.33 us  [over_groups(): parts.append(lax.ppermute(part, both, pairs))]
    pallas_call x4, Pallas kernels: 24.8 us -> 19.1 us  [expert_work(): pl.pallas_call(expert_body, grid=(units // block,), in_specs=[pl.BlockSpe...]
    ppermute x8, starting transfers between devices: 15.5 us -> 9.98 us  [over_section(): return lax.ppermute(value, 'section', [(0, 1), (1, 0)])]
    ppermute x8, starting transfers between devices: 17 us -> 22.3 us  [over_groups(): parts.append(lax.ppermute(part, both, pairs))]
    all_to_all x1, blocking collectives: 10.6 us -> 15.5 us  [local(): owned = lax.all_to_all(sums, both, split_axis=0, concat_axis=0, tiled=True)]
    unnamed x20 -> x16, local copies, waits for them, and re-layouts: 3.9 us -> 0.51 us
    ppermute x8, waiting for transfers between devices: 2.74 us -> 4.11 us  [over_section(): return lax.ppermute(value, 'section', [(0, 1), (1, 0)])]
  transfers between devices with their start and end apart: 24 -> 24, of which waited for: 9 -> 14; matrix products, arithmetic and copies ran while one was open for 0% -> 0% of each run, Pallas kernels for 22% -> 18%
where the time goes in v3:
time: 119 us
  starting transfers between devices  48.9 us (41%)
  waiting for transfers between devices  28.8 us (24%)
  Pallas kernels  23.1 us (19%)
  blocking collectives  15.5 us (13%)
    ppermute x8, starting transfers between devices, over_groups(): parts.append(lax.ppermute(part, both, pairs))  22.3 us
    ppermute x8, waiting for transfers between devices, over_x(): return lax.ppermute(value, 'expert', [(i, i ^ 1) for i in range(chips)])  19.4 us
    pallas_call x4, Pallas kernels, expert_work(): pl.pallas_call(expert_body, grid=(units // block,), in_specs=[pl.BlockSpe...  19.1 us
    ppermute x8, starting transfers between devices, over_x(): return lax.ppermute(value, 'expert', [(i, i ^ 1) for i in range(chips)])  16.6 us
    all_to_all x1, blocking collectives, local(): owned = lax.all_to_all(sums, both, split_axis=0, concat_axis=0, tiled=True)  15.5 us
    ppermute x8, starting transfers between devices, over_section(): return lax.ppermute(value, 'section', [(0, 1), (1, 0)])  9.98 us
    ppermute x8, waiting for transfers between devices, over_groups(): parts.append(lax.ppermute(part, both, pairs))  5.33 us
    ppermute x8, waiting for transfers between devices, over_section(): return lax.ppermute(value, 'section', [(0, 1), (1, 0)])  4.11 us
  transfers between devices with their start and end apart: 24, of which 14 were waited for; matrix products, arithmetic and copies ran while one was open for 0% of the time, Pallas kernels for 18%

profile of v3, /device:TPU:0, one launch (start us, length us, event | category | flops | bytes accessed | tf_op | source)
XLA Modules:
  0.0 118.6 jit_solution(2693921313696048322)
XLA Ops:
  0.7 0.5 collective-permute-start
  1.2 0.1 collective-permute-start.1
  1.3 0.4 copy-done.2
  1.7 0.7 own_tokens.1
  2.4 0.5 collective-permute-done.1.refs_4_
  3.0 0.1 copy-done
  3.0 0.5 collective-permute-start.4
  3.6 1.3 %place_rows.1 = (bf16[96,2048]{1,0:T(8,128)(2,1)S(1)}, bf16[96,2048]{1,0:T(8,128)(2,1)S(1)}, bf16[96,2048]{1,0:T(8,128)(2,1)S(1)}, bf16[96,2048]{1,0:T(8,128)(2,1)S(1)}) custom-call(bf16[128,2048]{1,0:T(8,128)(2,1)S(1)} %get-tuple-element.29.refs_0_, bf16[384,128]{1,0:T(8,128)(2,1)S(1)} %get-tuple-element.30.refs_1_, ...), custom_call_target="tpu_custom_call" | custom-call | flops 6000000000 | bytes 1000000 | tf_op jit(solution)/shard_map/place_rows/pallas_call | solution.py:260
  4.9 0.7 collective-permute-start.2
  5.6 3.0 %collective-permute-start.3 = (bf16[96,2048]{1,0:T(8,128)(2,1)S(1)}, bf16[96,2048]{1,0:T(8,128)(2,1)S(1)}, u32[]{:S(2)}, u32[]{:S(2)}) collective-permute-start(bf16[96,2048]{1,0:T(8,128)(2,1)S(1)} %collective-permute-done.2.own), channel_id=1, source_target_pairs={{0,1},{1,0},{2,3},{3,2},{4,5},{5,4},{6,7},{7,6},{8,9},{9,8},{10,11... | collective-permute-start | bytes 1179656 | tf_op jit(solution)/shard_map/ppermute | solution.py:219
  8.6 1.6 %collective-permute-start.8 = (bf16[96,2048]{1,0:T(8,128)(2,1)S(1)}, bf16[96,2048]{1,0:T(8,128)(2,1)S(1)}, u32[]{:S(2)}, u32[]{:S(2)}) collective-permute-start(bf16[96,2048]{1,0:T(8,128)(2,1)S(1)} %get-tuple-element.37), channel_id=1, source_target_pairs={{0,4},{1,5},{2,6},{3,7},{4,0},{5,1},{6,2},{7,3},{8,12},{9,13},{10,... | collective-permute-start | bytes 1179656 | tf_op jit(solution)/shard_map/ppermute | solution.py:231
  10.2 2.6 %collective-permute-start.10 = (bf16[96,2048]{1,0:T(8,128)(2,1)S(1)}, bf16[96,2048]{1,0:T(8,128)(2,1)S(1)}, u32[]{:S(2)}, u32[]{:S(2)}) collective-permute-start(bf16[96,2048]{1,0:T(8,128)(2,1)S(1)} %get-tuple-element.41), channel_id=1, source_target_pairs={{0,8},{1,9},{2,10},{3,11},{4,12},{5,13},{6,14},{7,15},{8,0},{9,1},... | collective-permute-start | bytes 1179656 | tf_op jit(solution)/shard_map/ppermute | solution.py:231
  12.7 1.6 %collective-permute-done.3.across = bf16[96,2048]{1,0:T(8,128)(2,1)S(1)} collective-permute-done((bf16[96,2048]{1,0:T(8,128)(2,1)S(1)}, bf16[96,2048]{1,0:T(8,128)(2,1)S(1)}, u32[]{:S(2)}, u32[]{:S(2)}) %collective-permute-start.3) | collective-permute-done | bytes 393248 | tf_op jit(solution)/shard_map/ppermute | solution.py:219
  14.3 1.4 %collective-permute-done.4.up_other = bf16[2048,1024]{1,0:T(8,128)(2,1)S(1)} collective-permute-done((bf16[2048,1024]{1,0:T(8,128)(2,1)S(1)}, bf16[2048,1024]{1,0:T(8,128)(2,1)S(1)}, u32[]{:S(2)}, u32[]{:S(2)}) %collective-permute-start.4) | collective-permute-done | bytes 4194336 | tf_op jit(solution)/shard_map/ppermute | solution.py:216
  15.7 0.8 collective-permute-done.5.down_other
  16.5 4.8 %expert.4 = (f32[96,2048]{1,0:T(8,128)S(1)}, bf16[96,2048]{1,0:T(8,128)(2,1)S(1)}) custom-call(bf16[96,2048]{1,0:T(8,128)(2,1)S(1)} %collective-permute-done.2.own, bf16[96,2048]{1,0:T(8,128)(2,1)S(1)} %collective-permute-done.3.across, bf16[2048,1024]{1,0:T(8,128)(2,1)S(1)} %bitcast.31, bf16[1024,2048]{1,0:T(8,128)(2,1)S(1)} %bitcast.36, ...), custom_call_target="tpu_custom_call" | custom-call | flops 3221225472 | bytes 16777216 | tf_op jit(solution)/shard_map/expert/pallas_call | solution.py:141
  21.3 2.9 %collective-permute-start.9 = (bf16[96,2048]{1,0:T(8,128)(2,1)S(1)}, bf16[96,2048]{1,0:T(8,128)(2,1)S(1)}, u32[]{:S(2)}, u32[]{:S(2)}) collective-permute-start(bf16[96,2048]{1,0:T(8,128)(2,1)S(1)} %collective-permute-done.8.own), channel_id=1, source_target_pairs={{0,1},{1,0},{2,3},{3,2},{4,5},{5,4},{6,7},{7,6},{8,9},{9,8},{10,11... | collective-permute-start | bytes 1179656 | tf_op jit(solution)/shard_map/ppermute | solution.py:219
  24.2 0.1 collective-permute-start.11
  24.3 4.1 %collective-permute-start.16 = (bf16[96,2048]{1,0:T(8,128)(2,1)S(1)}, bf16[96,2048]{1,0:T(8,128)(2,1)S(1)}, u32[]{:S(2)}, u32[]{:S(2)}) collective-permute-start(bf16[96,2048]{1,0:T(8,128)(2,1)S(1)} %get-tuple-element.46), channel_id=1, source_target_pairs={{0,12},{1,13},{2,14},{3,15},{4,8},{5,9},{6,10},{7,11},{8,4},{9,5},... | collective-permute-start | bytes 1179656 | tf_op jit(solution)/shard_map/ppermute | solution.py:231
  28.4 1.5 %collective-permute-start.6 = (bf16[96,2048]{1,0:T(8,128)(2,1)S(1)}, bf16[96,2048]{1,0:T(8,128)(2,1)S(1)}, u32[]{:S(2)}, u32[]{:S(2)}) collective-permute-start(bf16[96,2048]{1,0:T(8,128)(2,1)S(1)} %get-tuple-element.36), channel_id=1, source_target_pairs={{0,1},{1,0},{2,3},{3,2},{4,5},{5,4},{6,7},{7,6},{8,9},{9,8},{10,11... | collective-permute-start | bytes 1179656 | tf_op jit(solution)/shard_map/ppermute | solution.py:219
  29.8 0.1 collective-permute-done.9.across
  30.0 4.8 %expert.5 = (f32[96,2048]{1,0:T(8,128)S(1)}, bf16[96,2048]{1,0:T(8,128)(2,1)S(1)}) custom-call(bf16[96,2048]{1,0:T(8,128)(2,1)S(1)} %collective-permute-done.8.own, bf16[96,2048]{1,0:T(8,128)(2,1)S(1)} %collective-permute-done.9.across, bf16[2048,1024]{1,0:T(8,128)(2,1)S(1)} %bitcast.32, bf16[1024,2048]{1,0:T(8,128)(2,1)S(1)} %bitcast.37, ...), custom_call_target="tpu_custom_call" | custom-call | flops 3221225472 | bytes 16777216 | tf_op jit(solution)/shard_map/expert/pallas_call | solution.py:141
  34.8 2.7 %collective-permute-done.11.across = bf16[96,2048]{1,0:T(8,128)(2,1)S(1)} collective-permute-done((bf16[96,2048]{1,0:T(8,128)(2,1)S(1)}, bf16[96,2048]{1,0:T(8,128)(2,1)S(1)}, u32[]{:S(2)}, u32[]{:S(2)}) %collective-permute-start.11) | collective-permute-done | bytes 393248 | tf_op jit(solution)/shard_map/ppermute | solution.py:219
  37.4 4.8 %expert.6 = (f32[96,2048]{1,0:T(8,128)S(1)}, bf16[96,2048]{1,0:T(8,128)(2,1)S(1)}) custom-call(bf16[96,2048]{1,0:T(8,128)(2,1)S(1)} %collective-permute-done.10.own, bf16[96,2048]{1,0:T(8,128)(2,1)S(1)} %collective-permute-done.11.across, bf16[2048,1024]{1,0:T(8,128)(2,1)S(1)} %bitcast.33, bf16[1024,2048]{1,0:T(8,128)(2,1)S(1)} %bitcast.38, ...), custom_call_target="tpu_custom_call" | custom-call | flops 3221225472 | bytes 16777216 | tf_op jit(solution)/shard_map/expert/pallas_call | solution.py:141
  42.2 2.5 %collective-permute-start.12 = (bf16[96,2048]{1,0:T(8,128)(2,1)S(1)}, bf16[96,2048]{1,0:T(8,128)(2,1)S(1)}, u32[]{:S(2)}, u32[]{:S(2)}) collective-permute-start(bf16[96,2048]{1,0:T(8,128)(2,1)S(1)} %get-tuple-element.43), channel_id=1, source_target_pairs={{0,1},{1,0},{2,3},{3,2},{4,5},{5,4},{6,7},{7,6},{8,9},{9,8},{10,11... | collective-permute-start | bytes 1179656 | tf_op jit(solution)/shard_map/ppermute | solution.py:219
  44.8 1.1 collective-permute-done.6
  45.9 0.9 collective-permute-start.7
  46.8 2.5 %collective-permute-start.17 = (bf16[96,2048]{1,0:T(8,128)(2,1)S(1)}, bf16[96,2048]{1,0:T(8,128)(2,1)S(1)}, u32[]{:S(2)}, u32[]{:S(2)}) collective-permute-start(bf16[96,2048]{1,0:T(8,128)(2,1)S(1)} %collective-permute-done.16.own), channel_id=1, source_target_pairs={{0,1},{1,0},{2,3},{3,2},{4,5},{5,4},{6,7},{7,6},{8,9},{9,8},{10,11... | collective-permute-start | bytes 1179656 | tf_op jit(solution)/shard_map/ppermute | solution.py:219
  49.4 5.4 %collective-permute-done.12 = bf16[96,2048]{1,0:T(8,128)(2,1)S(1)} collective-permute-done((bf16[96,2048]{1,0:T(8,128)(2,1)S(1)}, bf16[96,2048]{1,0:T(8,128)(2,1)S(1)}, u32[]{:S(2)}, u32[]{:S(2)}) %collective-permute-start.12) | collective-permute-done | bytes 393248 | tf_op jit(solution)/shard_map/ppermute | solution.py:219
  54.8 2.0 %collective-permute-start.13 = (bf16[96,2048]{1,0:T(8,128)(2,1)S(1)}, bf16[96,2048]{1,0:T(8,128)(2,1)S(1)}, u32[]{:S(2)}, u32[]{:S(2)}) collective-permute-start(bf16[96,2048]{1,0:T(8,128)(2,1)S(1)} %get-tuple-element.44), channel_id=1, source_target_pairs={{0,1},{1,0},{2,3},{3,2},{4,5},{5,4},{6,7},{7,6},{8,9},{9,8},{10,11... | collective-permute-start | bytes 1179656 | tf_op jit(solution)/shard_map/ppermute | solution.py:219
  56.8 4.3 %collective-permute-start.15 = (bf16[96,2048]{1,0:T(8,128)(2,1)S(1)}, bf16[96,2048]{1,0:T(8,128)(2,1)S(1)}, u32[]{:S(2)}, u32[]{:S(2)}) collective-permute-start(bf16[96,2048]{1,0:T(8,128)(2,1)S(1)} %add_convert_fusion.1), channel_id=1, source_target_pairs={{0,8},{1,9},{2,10},{3,11},{4,12},{5,13},{6,14},{7,15},{8,0},{9,1},... | collective-permute-start | bytes 1179656 | tf_op jit(solution)/shard_map/ppermute | solution.py:231
  61.2 2.0 %collective-permute-done.17.across = bf16[96,2048]{1,0:T(8,128)(2,1)S(1)} collective-permute-done((bf16[96,2048]{1,0:T(8,128)(2,1)S(1)}, bf16[96,2048]{1,0:T(8,128)(2,1)S(1)}, u32[]{:S(2)}, u32[]{:S(2)}) %collective-permute-start.17) | collective-permute-done | bytes 393248 | tf_op jit(solution)/shard_map/ppermute | solution.py:219
  63.2 4.8 %expert.7 = (f32[96,2048]{1,0:T(8,128)S(1)}, bf16[96,2048]{1,0:T(8,128)(2,1)S(1)}) custom-call(bf16[96,2048]{1,0:T(8,128)(2,1)S(1)} %collective-permute-done.16.own, bf16[96,2048]{1,0:T(8,128)(2,1)S(1)} %collective-permute-done.17.across, bf16[2048,1024]{1,0:T(8,128)(2,1)S(1)} %bitcast.34, bf16[1024,2048]{1,0:T(8,128)(2,1)S(1)} %bitcast.39, ...), custom_call_target="tpu_custom_call" | custom-call | flops 3221225472 | bytes 16777216 | tf_op jit(solution)/shard_map/expert/pallas_call | solution.py:141
  68.0 2.0 %collective-permute-start.18 = (bf16[96,2048]{1,0:T(8,128)(2,1)S(1)}, bf16[96,2048]{1,0:T(8,128)(2,1)S(1)}, u32[]{:S(2)}, u32[]{:S(2)}) collective-permute-start(bf16[96,2048]{1,0:T(8,128)(2,1)S(1)} %get-tuple-element.50), channel_id=1, source_target_pairs={{0,1},{1,0},{2,3},{3,2},{4,5},{5,4},{6,7},{7,6},{8,9},{9,8},{10,11... | collective-permute-start | bytes 1179656 | tf_op jit(solution)/shard_map/ppermute | solution.py:219
  70.1 1.6 %collective-permute-done.13 = bf16[96,2048]{1,0:T(8,128)(2,1)S(1)} collective-permute-done((bf16[96,2048]{1,0:T(8,128)(2,1)S(1)}, bf16[96,2048]{1,0:T(8,128)(2,1)S(1)}, u32[]{:S(2)}, u32[]{:S(2)}) %collective-permute-start.13) | collective-permute-done | bytes 393248 | tf_op jit(solution)/shard_map/ppermute | solution.py:219
  71.7 3.5 %collective-permute-start.14 = (bf16[96,2048]{1,0:T(8,128)(2,1)S(1)}, bf16[96,2048]{1,0:T(8,128)(2,1)S(1)}, u32[]{:S(2)}, u32[]{:S(2)}) collective-permute-start(bf16[96,2048]{1,0:T(8,128)(2,1)S(1)} %add_convert_fusion.2), channel_id=1, source_target_pairs={{0,4},{1,5},{2,6},{3,7},{4,0},{5,1},{6,2},{7,3},{8,12},{9,13},{10,... | collective-permute-start | bytes 1179656 | tf_op jit(solution)/shard_map/ppermute | solution.py:231
  75.2 4.9 %collective-permute-done.18 = bf16[96,2048]{1,0:T(8,128)(2,1)S(1)} collective-permute-done((bf16[96,2048]{1,0:T(8,128)(2,1)S(1)}, bf16[96,2048]{1,0:T(8,128)(2,1)S(1)}, u32[]{:S(2)}, u32[]{:S(2)}) %collective-permute-start.18) | collective-permute-done | bytes 393248 | tf_op jit(solution)/shard_map/ppermute | solution.py:219
  80.2 4.7 %collective-permute-start.19 = (bf16[96,2048]{1,0:T(8,128)(2,1)S(1)}, bf16[96,2048]{1,0:T(8,128)(2,1)S(1)}, u32[]{:S(2)}, u32[]{:S(2)}) collective-permute-start(bf16[96,2048]{1,0:T(8,128)(2,1)S(1)} %add_convert_fusion), channel_id=1, source_target_pairs={{0,12},{1,13},{2,14},{3,15},{4,8},{5,9},{6,10},{7,11},{8,4},{9,5},... | collective-permute-start | bytes 1179656 | tf_op jit(solution)/shard_map/ppermute | solution.py:231
  84.9 4.6 %collective-permute-start.20 = (bf16[48,2048]{1,0:T(8,128)(2,1)S(1)}, bf16[48,2048]{1,0:T(8,128)(2,1)S(1)}, u32[]{:S(2)}, u32[]{:S(2)}) collective-permute-start(bf16[48,2048]{1,0:T(8,128)(2,1)S(1)} %slice_bitcast_fusion.3), channel_id=1, source_target_pairs={{0,16},{16,0},{1,17},{17,1},{2,18},{18,2},{3,19},{19,3},{4,20},{20... | collective-permute-start | bytes 589832 | tf_op jit(solution)/shard_map/ppermute | solution.py:216
  89.6 5.3 %collective-permute-done.19.refs_3_ = bf16[96,2048]{1,0:T(8,128)(2,1)S(1)} collective-permute-done((bf16[96,2048]{1,0:T(8,128)(2,1)S(1)}, bf16[96,2048]{1,0:T(8,128)(2,1)S(1)}, u32[]{:S(2)}, u32[]{:S(2)}) %collective-permute-start.19) | collective-permute-done | bytes 393248 | tf_op jit(solution)/shard_map/ppermute | solution.py:231
  94.9 4.1 %collective-permute-start.22 = (bf16[48,2048]{1,0:T(8,128)(2,1)S(1)}, bf16[48,2048]{1,0:T(8,128)(2,1)S(1)}, u32[]{:S(2)}, u32[]{:S(2)}) collective-permute-start(bf16[48,2048]{1,0:T(8,128)(2,1)S(1)} %slice_bitcast_fusion.1), channel_id=1, source_target_pairs={{0,16},{16,0},{1,17},{17,1},{2,18},{18,2},{3,19},{19,3},{4,20},{20... | collective-permute-start | bytes 589832 | tf_op jit(solution)/shard_map/ppermute | solution.py:216
  99.1 0.1 collective-permute-start.23
  99.2 0.9 collective-permute-done.22.refs_6_
  100.1 0.5 collective-permute-done.23.refs_7_
  100.6 1.9 %shard_map.95 = (bf16[128,2048]{1,0:T(8,128)(2,1)}, f32[32,128]{1,0:T(8,128)S(1)}) custom-call(bf16[96,2048]{1,0:T(8,128)(2,1)S(1)} %collective-permute-done.7.refs_0_, bf16[96,2048]{1,0:T(8,128)(2,1)S(1)} %collective-permute-done.14.refs_1_, bf16[96,2048]{1,0:T(8,128)(2,1)S(1)} %collective-permute-done.15.refs_2_, ...), custom_call_target="tpu_custom_call" | custom-call | tf_op jit(solution)/shard_map/pallas_call | solution.py:346
  102.5 15.5 %all_to_all.9 = f32[32,1,128]{2,1,0:T(1,128)S(1)} all-to-all(f32[32,1,128]{2,1,0:T(1,128)S(1)} %bitcast.49), channel_id=1, replica_groups=mesh['section'=2,'expert'=16] {'section','expert'}, dimensions={0} | all-to-all | bytes 32768 | tf_op jit(solution)/shard_map/all_to_all | solution.py:363
  118.0 0.1 slice_divide_fusion
  118.1 0.5 add_bitcast_fusion
  (36 shorter events, 0.6 us)
Async XLA Ops:
  0.6 1.0 copy-start.2
  0.6 1.0 copy-start.6
  0.7 1.0 copy-start.5
  0.7 1.0 copy-start.4
  0.7 2.4 %copy-start = (bf16[1,2048,1024]{2,1,0:T(8,128)(2,1)S(1)}, bf16[1,2048,1024]{2,1,0:T(8,128)(2,1)}, u32[]{:S(2)}) copy-start(bf16[1,2048,1024]{2,1,0:T(8,128)(2,1)} %param.12) | copy-start | bytes 12582916
  0.7 2.3 %collective-permute-start = (bf16[128,2048]{1,0:T(8,128)(2,1)}, bf16[128,2048]{1,0:T(8,128)(2,1)S(1)}, u32[]{:S(2)}, u32[]{:S(2)}) collective-permute-start(bf16[128,2048]{1,0:T(8,128)(2,1)} %bitcast.40), channel_id=1, source_target_pairs={{0,16},{16,0},{1,17},{17,1},{2,18},{18,2},{3,19},{19,3},{4,20},{20... | collective-permute-start | bytes 1572872 | tf_op jit(solution)/shard_map/ppermute | solution.py:216
  1.2 1.7 %collective-permute-start.1 = (s32[2,128]{1,0:T(2,128)}, s32[2,128]{1,0:T(2,128)S(1)}, u32[]{:S(2)}, u32[]{:S(2)}) collective-permute-start(s32[2,128]{1,0:T(2,128)} %bitcast.51), channel_id=1, source_target_pairs={{0,16},{16,0},{1,17},{17,1},{2,18},{18,2},{3,19},{19,3},{4,20},{20... | collective-permute-start | bytes 3080 | tf_op jit(solution)/shard_map/ppermute | solution.py:216
  3.0 12.7 %collective-permute-start.4 = (bf16[2048,1024]{1,0:T(8,128)(2,1)S(1)}, bf16[2048,1024]{1,0:T(8,128)(2,1)S(1)}, u32[]{:S(2)}, u32[]{:S(2)}) collective-permute-start(bf16[2048,1024]{1,0:T(8,128)(2,1)S(1)} %bitcast.30), channel_id=1, source_target_pairs={{0,16},{16,0},{1,17},{17,1},{2,18},{18,2},{3,19},{19,3},{4,20},{20... | collective-permute-start | bytes 12582920 | tf_op jit(solution)/shard_map/ppermute | solution.py:216
  3.5 13.0 %collective-permute-start.5 = (bf16[1024,2048]{1,0:T(8,128)(2,1)}, bf16[1024,2048]{1,0:T(8,128)(2,1)S(1)}, u32[]{:S(2)}, u32[]{:S(2)}) collective-permute-start(bf16[1024,2048]{1,0:T(8,128)(2,1)} %bitcast.35), channel_id=1, source_target_pairs={{0,16},{16,0},{1,17},{17,1},{2,18},{18,2},{3,19},{19,3},{4,20},{20... | collective-permute-start | bytes 12582920 | tf_op jit(solution)/shard_map/ppermute | solution.py:216
  3.6 12.9 %copy-start.1 = (bf16[1,1024,2048]{2,1,0:T(8,128)(2,1)S(1)}, bf16[1,1024,2048]{2,1,0:T(8,128)(2,1)}, u32[]{:S(2)}) copy-start(bf16[1,1024,2048]{2,1,0:T(8,128)(2,1)} %param.13) | copy-start | bytes 12582916
  4.9 0.7 collective-permute-start.2
  5.6 8.8 %collective-permute-start.3 = (bf16[96,2048]{1,0:T(8,128)(2,1)S(1)}, bf16[96,2048]{1,0:T(8,128)(2,1)S(1)}, u32[]{:S(2)}, u32[]{:S(2)}) collective-permute-start(bf16[96,2048]{1,0:T(8,128)(2,1)S(1)} %collective-permute-done.2.own), channel_id=1, source_target_pairs={{0,1},{1,0},{2,3},{3,2},{4,5},{5,4},{6,7},{7,6},{8,9},{9,8},{10,11... | collective-permute-start | bytes 1179656 | tf_op jit(solution)/shard_map/ppermute | solution.py:219
  8.6 12.7 %collective-permute-start.8 = (bf16[96,2048]{1,0:T(8,128)(2,1)S(1)}, bf16[96,2048]{1,0:T(8,128)(2,1)S(1)}, u32[]{:S(2)}, u32[]{:S(2)}) collective-permute-start(bf16[96,2048]{1,0:T(8,128)(2,1)S(1)} %get-tuple-element.37), channel_id=1, source_target_pairs={{0,4},{1,5},{2,6},{3,7},{4,0},{5,1},{6,2},{7,3},{8,12},{9,13},{10,... | collective-permute-start | bytes 1179656 | tf_op jit(solution)/shard_map/ppermute | solution.py:231
  10.2 14.1 %collective-permute-start.10 = (bf16[96,2048]{1,0:T(8,128)(2,1)S(1)}, bf16[96,2048]{1,0:T(8,128)(2,1)S(1)}, u32[]{:S(2)}, u32[]{:S(2)}) collective-permute-start(bf16[96,2048]{1,0:T(8,128)(2,1)S(1)} %get-tuple-element.41), channel_id=1, source_target_pairs={{0,8},{1,9},{2,10},{3,11},{4,12},{5,13},{6,14},{7,15},{8,0},{9,1},... | collective-permute-start | bytes 1179656 | tf_op jit(solution)/shard_map/ppermute | solution.py:231
  21.3 8.7 %collective-permute-start.9 = (bf16[96,2048]{1,0:T(8,128)(2,1)S(1)}, bf16[96,2048]{1,0:T(8,128)(2,1)S(1)}, u32[]{:S(2)}, u32[]{:S(2)}) collective-permute-start(bf16[96,2048]{1,0:T(8,128)(2,1)S(1)} %collective-permute-done.8.own), channel_id=1, source_target_pairs={{0,1},{1,0},{2,3},{3,2},{4,5},{5,4},{6,7},{7,6},{8,9},{9,8},{10,11... | collective-permute-start | bytes 1179656 | tf_op jit(solution)/shard_map/ppermute | solution.py:219
  24.2 13.2 %collective-permute-start.11 = (bf16[96,2048]{1,0:T(8,128)(2,1)S(1)}, bf16[96,2048]{1,0:T(8,128)(2,1)S(1)}, u32[]{:S(2)}, u32[]{:S(2)}) collective-permute-start(bf16[96,2048]{1,0:T(8,128)(2,1)S(1)} %collective-permute-done.10.own), channel_id=1, source_target_pairs={{0,1},{1,0},{2,3},{3,2},{4,5},{5,4},{6,7},{7,6},{8,9},{9,8},{10,11... | collective-permute-start | bytes 1179656 | tf_op jit(solution)/shard_map/ppermute | solution.py:219
  24.3 22.5 %collective-permute-start.16 = (bf16[96,2048]{1,0:T(8,128)(2,1)S(1)}, bf16[96,2048]{1,0:T(8,128)(2,1)S(1)}, u32[]{:S(2)}, u32[]{:S(2)}) collective-permute-start(bf16[96,2048]{1,0:T(8,128)(2,1)S(1)} %get-tuple-element.46), channel_id=1, source_target_pairs={{0,12},{1,13},{2,14},{3,15},{4,8},{5,9},{6,10},{7,11},{8,4},{9,5},... | collective-permute-start | bytes 1179656 | tf_op jit(solution)/shard_map/ppermute | solution.py:231
  28.4 17.5 %collective-permute-start.6 = (bf16[96,2048]{1,0:T(8,128)(2,1)S(1)}, bf16[96,2048]{1,0:T(8,128)(2,1)S(1)}, u32[]{:S(2)}, u32[]{:S(2)}) collective-permute-start(bf16[96,2048]{1,0:T(8,128)(2,1)S(1)} %get-tuple-element.36), channel_id=1, source_target_pairs={{0,1},{1,0},{2,3},{3,2},{4,5},{5,4},{6,7},{7,6},{8,9},{9,8},{10,11... | collective-permute-start | bytes 1179656 | tf_op jit(solution)/shard_map/ppermute | solution.py:219
  42.2 12.6 %collective-permute-start.12 = (bf16[96,2048]{1,0:T(8,128)(2,1)S(1)}, bf16[96,2048]{1,0:T(8,128)(2,1)S(1)}, u32[]{:S(2)}, u32[]{:S(2)}) collective-permute-start(bf16[96,2048]{1,0:T(8,128)(2,1)S(1)} %get-tuple-element.43), channel_id=1, source_target_pairs={{0,1},{1,0},{2,3},{3,2},{4,5},{5,4},{6,7},{7,6},{8,9},{9,8},{10,11... | collective-permute-start | bytes 1179656 | tf_op jit(solution)/shard_map/ppermute | solution.py:219
  45.9 24.1 %collective-permute-start.7 = (bf16[96,2048]{1,0:T(8,128)(2,1)S(1)}, bf16[96,2048]{1,0:T(8,128)(2,1)S(1)}, u32[]{:S(2)}, u32[]{:S(2)}) collective-permute-start(bf16[96,2048]{1,0:T(8,128)(2,1)S(1)} %add_convert_fusion.3), channel_id=1, source_target_pairs={{0,0},{1,1},{2,2},{3,3},{4,4},{5,5},{6,6},{7,7},{8,8},{9,9},{10,10... | collective-permute-start | bytes 1179656 | tf_op jit(solution)/shard_map/ppermute | solution.py:231
  46.8 16.4 %collective-permute-start.17 = (bf16[96,2048]{1,0:T(8,128)(2,1)S(1)}, bf16[96,2048]{1,0:T(8,128)(2,1)S(1)}, u32[]{:S(2)}, u32[]{:S(2)}) collective-permute-start(bf16[96,2048]{1,0:T(8,128)(2,1)S(1)} %collective-permute-done.16.own), channel_id=1, source_target_pairs={{0,1},{1,0},{2,3},{3,2},{4,5},{5,4},{6,7},{7,6},{8,9},{9,8},{10,11... | collective-permute-start | bytes 1179656 | tf_op jit(solution)/shard_map/ppermute | solution.py:219
  54.8 16.9 %collective-permute-start.13 = (bf16[96,2048]{1,0:T(8,128)(2,1)S(1)}, bf16[96,2048]{1,0:T(8,128)(2,1)S(1)}, u32[]{:S(2)}, u32[]{:S(2)}) collective-permute-start(bf16[96,2048]{1,0:T(8,128)(2,1)S(1)} %get-tuple-element.44), channel_id=1, source_target_pairs={{0,1},{1,0},{2,3},{3,2},{4,5},{5,4},{6,7},{7,6},{8,9},{9,8},{10,11... | collective-permute-start | bytes 1179656 | tf_op jit(solution)/shard_map/ppermute | solution.py:219
  56.8 32.7 %collective-permute-start.15 = (bf16[96,2048]{1,0:T(8,128)(2,1)S(1)}, bf16[96,2048]{1,0:T(8,128)(2,1)S(1)}, u32[]{:S(2)}, u32[]{:S(2)}) collective-permute-start(bf16[96,2048]{1,0:T(8,128)(2,1)S(1)} %add_convert_fusion.1), channel_id=1, source_target_pairs={{0,8},{1,9},{2,10},{3,11},{4,12},{5,13},{6,14},{7,15},{8,0},{9,1},... | collective-permute-start | bytes 1179656 | tf_op jit(solution)/shard_map/ppermute | solution.py:231
  68.0 32.6 %copy-start.3 = (bf16[1,128,2048]{2,1,0:T(8,128)(2,1)S(1)}, bf16[1,128,2048]{2,1,0:T(8,128)(2,1)}, u32[]{:S(2)}) copy-start(bf16[1,128,2048]{2,1,0:T(8,128)(2,1)} %param.9) | copy-start | bytes 1572868
  68.0 32.6 %copy-start.7 = (s32[1,128]{1,0:T(1,128)S(1)}, s32[1,128]{1,0:T(1,128)}, u32[]{:S(2)}) copy-start(s32[1,128]{1,0:T(1,128)} %refs_11_.1) | copy-start | bytes 1540
  68.0 12.1 %collective-permute-start.18 = (bf16[96,2048]{1,0:T(8,128)(2,1)S(1)}, bf16[96,2048]{1,0:T(8,128)(2,1)S(1)}, u32[]{:S(2)}, u32[]{:S(2)}) collective-permute-start(bf16[96,2048]{1,0:T(8,128)(2,1)S(1)} %get-tuple-element.50), channel_id=1, source_target_pairs={{0,1},{1,0},{2,3},{3,2},{4,5},{5,4},{6,7},{7,6},{8,9},{9,8},{10,11... | collective-permute-start | bytes 1179656 | tf_op jit(solution)/shard_map/ppermute | solution.py:219
  71.7 27.3 %collective-permute-start.14 = (bf16[96,2048]{1,0:T(8,128)(2,1)S(1)}, bf16[96,2048]{1,0:T(8,128)(2,1)S(1)}, u32[]{:S(2)}, u32[]{:S(2)}) collective-permute-start(bf16[96,2048]{1,0:T(8,128)(2,1)S(1)} %add_convert_fusion.2), channel_id=1, source_target_pairs={{0,4},{1,5},{2,6},{3,7},{4,0},{5,1},{6,2},{7,3},{8,12},{9,13},{10,... | collective-permute-start | bytes 1179656 | tf_op jit(solution)/shard_map/ppermute | solution.py:231
  80.2 14.7 %collective-permute-start.19 = (bf16[96,2048]{1,0:T(8,128)(2,1)S(1)}, bf16[96,2048]{1,0:T(8,128)(2,1)S(1)}, u32[]{:S(2)}, u32[]{:S(2)}) collective-permute-start(bf16[96,2048]{1,0:T(8,128)(2,1)S(1)} %add_convert_fusion), channel_id=1, source_target_pairs={{0,12},{1,13},{2,14},{3,15},{4,8},{5,9},{6,10},{7,11},{8,4},{9,5},... | collective-permute-start | bytes 1179656 | tf_op jit(solution)/shard_map/ppermute | solution.py:231
  84.9 14.3 %collective-permute-start.20 = (bf16[48,2048]{1,0:T(8,128)(2,1)S(1)}, bf16[48,2048]{1,0:T(8,128)(2,1)S(1)}, u32[]{:S(2)}, u32[]{:S(2)}) collective-permute-start(bf16[48,2048]{1,0:T(8,128)(2,1)S(1)} %slice_bitcast_fusion.3), channel_id=1, source_target_pairs={{0,16},{16,0},{1,17},{17,1},{2,18},{18,2},{3,19},{19,3},{4,20},{20... | collective-permute-start | bytes 589832 | tf_op jit(solution)/shard_map/ppermute | solution.py:216
  89.5 9.6 %collective-permute-start.21 = (bf16[48,2048]{1,0:T(8,128)(2,1)S(1)}, bf16[48,2048]{1,0:T(8,128)(2,1)S(1)}, u32[]{:S(2)}, u32[]{:S(2)}) collective-permute-start(bf16[48,2048]{1,0:T(8,128)(2,1)S(1)} %slice_bitcast_fusion.2), channel_id=1, source_target_pairs={{0,16},{16,0},{1,17},{17,1},{2,18},{18,2},{3,19},{19,3},{4,20},{20... | collective-permute-start | bytes 589832 | tf_op jit(solution)/shard_map/ppermute | solution.py:216
  94.9 5.2 %collective-permute-start.22 = (bf16[48,2048]{1,0:T(8,128)(2,1)S(1)}, bf16[48,2048]{1,0:T(8,128)(2,1)S(1)}, u32[]{:S(2)}, u32[]{:S(2)}) collective-permute-start(bf16[48,2048]{1,0:T(8,128)(2,1)S(1)} %slice_bitcast_fusion.1), channel_id=1, source_target_pairs={{0,16},{16,0},{1,17},{17,1},{2,18},{18,2},{3,19},{19,3},{4,20},{20... | collective-permute-start | bytes 589832 | tf_op jit(solution)/shard_map/ppermute | solution.py:216
  99.1 1.5 %collective-permute-start.23 = (bf16[48,2048]{1,0:T(8,128)(2,1)S(1)}, bf16[48,2048]{1,0:T(8,128)(2,1)S(1)}, u32[]{:S(2)}, u32[]{:S(2)}) collective-permute-start(bf16[48,2048]{1,0:T(8,128)(2,1)S(1)} %slice_bitcast_fusion), channel_id=1, source_target_pairs={{0,16},{16,0},{1,17},{17,1},{2,18},{18,2},{3,19},{19,3},{4,20},{20... | collective-permute-start | bytes 589832 | tf_op jit(solution)/shard_map/ppermute | solution.py:216

commit v4 on v3

--- a/solution.py
+++ b/solution.py
@@ -218,12 +218,12 @@
     def over_x(value):
         return lax.ppermute(value, "expert", [(i, i ^ 1) for i in range(chips)])
 
-    def over_groups(value, index):
+    def over_groups(value, index, flip=0):
         parts = []
         for k in range(each):
             couple = index * each + k
             pairs = [
-                (side * chips + i, side * chips + (i ^ (2 * (2 * couple + side))))
+                (side * chips + i, side * chips + (i ^ (2 * (2 * couple + side)) ^ flip))
                 for side in range(sections)
                 for i in range(chips)
             ]
@@ -278,14 +278,8 @@
     def arrive(k, *others):
         arrived[k] = (over_groups(after(sends[k], *others), k), 0)
 
-    def arrive_across_first(k):
-        pair = jnp.concatenate([sends[k], over_x(sends[k])], axis=0)
-        if each == 1:
-            pair = over_groups(pair, k)
-            arrived[k], across[k] = (pair, 0), (pair, 1)
-        else:
-            arrived[k] = (over_groups(pair[:span], k), 0)
-            across[k] = (over_groups(pair[span:], k), 0)
+    def arrive_across(k, *others):
+        across[k] = (over_groups(after(sends[k], *others), k, flip=1), 0)
 
     def exchange(k, *others):
         across[k] = (over_x(after(arrived[k][0], *others)), 0)
@@ -296,6 +290,11 @@
 
     def cross(k, *others):
         halves[k] = over_x(after(sent[k], *others))
+
+    def give_back_straight(k, *others):
+        near = over_groups(after(kept[k].astype(jnp.bfloat16), *others), k)
+        far = over_groups(after(sent[k], *others), k, flip=1)
+        returned[k] = (near.astype(jnp.float32) + far.astype(jnp.float32)).astype(jnp.bfloat16)
 
     def give_back(k):
         summed = (kept[k] + halves[k].astype(jnp.float32)).astype(jnp.bfloat16)
@@ -314,12 +313,12 @@
         arrive(2)
         arrive(1)
         arrive(0)
+        arrive_across(0)
         arrive(3)
-        exchange(0)
         exchange(2)
         work(0)
         exchange(1, kept[0])
-        cross(0)
+        give_back_straight(0)
         work(1, kept[0])
         exchange(3, kept[1])
         work(2, kept[1])
@@ -330,11 +329,10 @@
         give_back(3)
         cross(1, halves[2])
         give_back(1)
-        give_back(0)
-        swap((0,), halves[1], halves[3])
-        swap((2,), halves[1], halves[3])
+        swap((0,), halves[3])
+        swap((2,), halves[3])
+        swap((1,), halves[3])
         swap((3,))
-        swap((1,))
     else:
         for k in range(rounds):
             arrive(k)

time: 119 us -> 115 us (0.966)
  waiting for transfers between devices: 28.8 us -> 22.3 us
  starting transfers between devices: 48.9 us -> 55.3 us
  blocking collectives: 15.5 us -> 11.9 us
    ppermute x8 -> x6, starting transfers between devices: 16.6 us -> 5.7 us  [over_x(): return lax.ppermute(value, 'expert', [(i, i ^ 1) for i in range(chips)])]
    ppermute x8, starting transfers between devices: 9.98 us -> 19.1 us  [over_section(): return lax.ppermute(value, 'section', [(0, 1), (1, 0)])]
    ppermute x8 -> x10, starting transfers between devices: 22.3 us -> 30.5 us  [over_groups(): parts.append(lax.ppermute(part, both, pairs))]
    ppermute x8 -> x6, waiting for transfers between devices: 19.4 us -> 15.2 us  [over_x(): return lax.ppermute(value, 'expert', [(i, i ^ 1) for i in range(chips)])]
    all_to_all x1, blocking collectives: 15.5 us -> 11.9 us  [local(): owned = lax.all_to_all(sums, both, split_axis=0, concat_axis=0, tiled=True)]
    ppermute x8, waiting for transfers between devices: 4.11 us -> 1.61 us  [over_section(): return lax.ppermute(value, 'section', [(0, 1), (1, 0)])]
    ppermute x8 -> x10, waiting for transfers between devices: 5.33 us -> 5.54 us  [over_groups(): parts.append(lax.ppermute(part, both, pairs))]
  transfers between devices with their start and end apart: 24 -> 24, of which waited for: 14 -> 9; matrix products, arithmetic and copies ran while one was open for 0% -> 0% of each run, Pallas kernels for 18% -> 18%
where the time goes in v4:
time: 115 us
  starting transfers between devices  55.3 us (48%)
  Pallas kernels  23.1 us (20%)
  waiting for transfers between devices  22.3 us (19%)
  blocking collectives  11.9 us (10%)
    ppermute x10, starting transfers between devices, over_groups(): parts.append(lax.ppermute(part, both, pairs))  30.5 us
    pallas_call x4, Pallas kernels, expert_work(): pl.pallas_call(expert_body, grid=(units // block,), in_specs=[pl.BlockSpe...  19.2 us
    ppermute x8, starting transfers between devices, over_section(): return lax.ppermute(value, 'section', [(0, 1), (1, 0)])  19.1 us
    ppermute x6, waiting for transfers between devices, over_x(): return lax.ppermute(value, 'expert', [(i, i ^ 1) for i in range(chips)])  15.2 us
    all_to_all x1, blocking collectives, local(): owned = lax.all_to_all(sums, both, split_axis=0, concat_axis=0, tiled=True)  11.9 us
    ppermute x6, starting transfers between devices, over_x(): return lax.ppermute(value, 'expert', [(i, i ^ 1) for i in range(chips)])  5.7 us
    ppermute x10, waiting for transfers between devices, over_groups(): parts.append(lax.ppermute(part, both, pairs))  5.54 us
  transfers between devices with their start and end apart: 24, of which 9 were waited for; matrix products, arithmetic and copies ran while one was open for 0% of the time, Pallas kernels for 18%

profile of v4, /device:TPU:0, one launch (start us, length us, event | category | flops | bytes accessed | tf_op | source)
XLA Modules:
  0.0 115.1 jit_solution(12967420365689130531)
XLA Ops:
  0.7 0.5 collective-permute-start
  1.2 0.1 collective-permute-start.1
  1.3 0.4 copy-done.2
  1.7 0.7 own_tokens.1
  2.4 0.5 collective-permute-done.1.refs_4_
  3.0 0.1 copy-done
  3.0 0.5 collective-permute-start.4
  3.6 1.3 %place_rows.1 = (bf16[96,2048]{1,0:T(8,128)(2,1)S(1)}, bf16[96,2048]{1,0:T(8,128)(2,1)S(1)}, bf16[96,2048]{1,0:T(8,128)(2,1)S(1)}, bf16[96,2048]{1,0:T(8,128)(2,1)S(1)}) custom-call(bf16[128,2048]{1,0:T(8,128)(2,1)S(1)} %get-tuple-element.30.refs_0_, bf16[384,128]{1,0:T(8,128)(2,1)S(1)} %get-tuple-element.31.refs_1_, ...), custom_call_target="tpu_custom_call" | custom-call | flops 6000000000 | bytes 1000000 | tf_op jit(solution)/shard_map/place_rows/pallas_call | solution.py:260
  4.9 0.7 collective-permute-start.2
  5.6 3.0 %collective-permute-start.3 = (bf16[96,2048]{1,0:T(8,128)(2,1)S(1)}, bf16[96,2048]{1,0:T(8,128)(2,1)S(1)}, u32[]{:S(2)}, u32[]{:S(2)}) collective-permute-start(bf16[96,2048]{1,0:T(8,128)(2,1)S(1)} %get-tuple-element.33), channel_id=1, source_target_pairs={{0,1},{1,0},{2,3},{3,2},{4,5},{5,4},{6,7},{7,6},{8,9},{9,8},{10,11... | collective-permute-start | bytes 1179656 | tf_op jit(solution)/shard_map/ppermute | solution.py:231
  8.6 1.6 %collective-permute-start.8 = (bf16[96,2048]{1,0:T(8,128)(2,1)S(1)}, bf16[96,2048]{1,0:T(8,128)(2,1)S(1)}, u32[]{:S(2)}, u32[]{:S(2)}) collective-permute-start(bf16[96,2048]{1,0:T(8,128)(2,1)S(1)} %get-tuple-element.38), channel_id=1, source_target_pairs={{0,4},{1,5},{2,6},{3,7},{4,0},{5,1},{6,2},{7,3},{8,12},{9,13},{10,... | collective-permute-start | bytes 1179656 | tf_op jit(solution)/shard_map/ppermute | solution.py:231
  10.2 2.6 %collective-permute-start.10 = (bf16[96,2048]{1,0:T(8,128)(2,1)S(1)}, bf16[96,2048]{1,0:T(8,128)(2,1)S(1)}, u32[]{:S(2)}, u32[]{:S(2)}) collective-permute-start(bf16[96,2048]{1,0:T(8,128)(2,1)S(1)} %get-tuple-element.42), channel_id=1, source_target_pairs={{0,8},{1,9},{2,10},{3,11},{4,12},{5,13},{6,14},{7,15},{8,0},{9,1},... | collective-permute-start | bytes 1179656 | tf_op jit(solution)/shard_map/ppermute | solution.py:231
  12.7 4.0 %collective-permute-done.3.across = bf16[96,2048]{1,0:T(8,128)(2,1)S(1)} collective-permute-done((bf16[96,2048]{1,0:T(8,128)(2,1)S(1)}, bf16[96,2048]{1,0:T(8,128)(2,1)S(1)}, u32[]{:S(2)}, u32[]{:S(2)}) %collective-permute-start.3) | collective-permute-done | bytes 393248 | tf_op jit(solution)/shard_map/ppermute | solution.py:231
  16.7 4.8 %expert.4 = (f32[96,2048]{1,0:T(8,128)S(1)}, bf16[96,2048]{1,0:T(8,128)(2,1)S(1)}) custom-call(bf16[96,2048]{1,0:T(8,128)(2,1)S(1)} %collective-permute-done.2.own, bf16[96,2048]{1,0:T(8,128)(2,1)S(1)} %collective-permute-done.3.across, bf16[2048,1024]{1,0:T(8,128)(2,1)S(1)} %bitcast.31, bf16[1024,2048]{1,0:T(8,128)(2,1)S(1)} %bitcast.36, ...), custom_call_target="tpu_custom_call" | custom-call | flops 3221225472 | bytes 16777216 | tf_op jit(solution)/shard_map/expert/pallas_call | solution.py:141
  21.5 1.1 collective-permute-done.8.own
  22.6 1.6 %collective-permute-start.9 = (bf16[96,2048]{1,0:T(8,128)(2,1)S(1)}, bf16[96,2048]{1,0:T(8,128)(2,1)S(1)}, u32[]{:S(2)}, u32[]{:S(2)}) collective-permute-start(bf16[96,2048]{1,0:T(8,128)(2,1)S(1)} %collective-permute-done.8.own), channel_id=1, source_target_pairs={{0,1},{1,0},{2,3},{3,2},{4,5},{5,4},{6,7},{7,6},{8,9},{9,8},{10,11... | collective-permute-start | bytes 1179656 | tf_op jit(solution)/shard_map/ppermute | solution.py:219
  24.2 0.4 collective-permute-start.11
  24.6 4.3 %collective-permute-start.16 = (bf16[96,2048]{1,0:T(8,128)(2,1)S(1)}, bf16[96,2048]{1,0:T(8,128)(2,1)S(1)}, u32[]{:S(2)}, u32[]{:S(2)}) collective-permute-start(bf16[96,2048]{1,0:T(8,128)(2,1)S(1)} %get-tuple-element.47), channel_id=1, source_target_pairs={{0,12},{1,13},{2,14},{3,15},{4,8},{5,9},{6,10},{7,11},{8,4},{9,5},... | collective-permute-start | bytes 1179656 | tf_op jit(solution)/shard_map/ppermute | solution.py:231
  28.9 1.0 collective-permute-start.7
  30.0 0.9 collective-permute-start.6
  30.8 4.8 %expert.5 = (f32[96,2048]{1,0:T(8,128)S(1)}, bf16[96,2048]{1,0:T(8,128)(2,1)S(1)}) custom-call(bf16[96,2048]{1,0:T(8,128)(2,1)S(1)} %collective-permute-done.8.own, bf16[96,2048]{1,0:T(8,128)(2,1)S(1)} %collective-permute-done.9.across, bf16[2048,1024]{1,0:T(8,128)(2,1)S(1)} %bitcast.32, bf16[1024,2048]{1,0:T(8,128)(2,1)S(1)} %bitcast.37, ...), custom_call_target="tpu_custom_call" | custom-call | flops 3221225472 | bytes 16777216 | tf_op jit(solution)/shard_map/expert/pallas_call | solution.py:141
  35.7 4.8 %expert.6 = (f32[96,2048]{1,0:T(8,128)S(1)}, bf16[96,2048]{1,0:T(8,128)(2,1)S(1)}) custom-call(bf16[96,2048]{1,0:T(8,128)(2,1)S(1)} %collective-permute-done.10.own, bf16[96,2048]{1,0:T(8,128)(2,1)S(1)} %collective-permute-done.11.across, bf16[2048,1024]{1,0:T(8,128)(2,1)S(1)} %bitcast.33, bf16[1024,2048]{1,0:T(8,128)(2,1)S(1)} %bitcast.38, ...), custom_call_target="tpu_custom_call" | custom-call | flops 3221225472 | bytes 16777216 | tf_op jit(solution)/shard_map/expert/pallas_call | solution.py:141
  40.5 1.2 %collective-permute-start.12 = (bf16[96,2048]{1,0:T(8,128)(2,1)S(1)}, bf16[96,2048]{1,0:T(8,128)(2,1)S(1)}, u32[]{:S(2)}, u32[]{:S(2)}) collective-permute-start(bf16[96,2048]{1,0:T(8,128)(2,1)S(1)} %get-tuple-element.44), channel_id=1, source_target_pairs={{0,1},{1,0},{2,3},{3,2},{4,5},{5,4},{6,7},{7,6},{8,9},{9,8},{10,11... | collective-permute-start | bytes 1179656 | tf_op jit(solution)/shard_map/ppermute | solution.py:219
  41.7 0.9 collective-permute-start.17
  42.6 0.5 collective-permute-done.7
  43.0 0.1 add_convert_fusion.3.refs_0_
  43.1 7.3 %collective-permute-done.12 = bf16[96,2048]{1,0:T(8,128)(2,1)S(1)} collective-permute-done((bf16[96,2048]{1,0:T(8,128)(2,1)S(1)}, bf16[96,2048]{1,0:T(8,128)(2,1)S(1)}, u32[]{:S(2)}, u32[]{:S(2)}) %collective-permute-start.12) | collective-permute-done | bytes 393248 | tf_op jit(solution)/shard_map/ppermute | solution.py:219
  50.5 0.8 collective-permute-start.13
  51.2 0.1 add_convert_fusion.1
  51.3 7.4 %collective-permute-start.15 = (bf16[96,2048]{1,0:T(8,128)(2,1)S(1)}, bf16[96,2048]{1,0:T(8,128)(2,1)S(1)}, u32[]{:S(2)}, u32[]{:S(2)}) collective-permute-start(bf16[96,2048]{1,0:T(8,128)(2,1)S(1)} %add_convert_fusion.1), channel_id=1, source_target_pairs={{0,8},{1,9},{2,10},{3,11},{4,12},{5,13},{6,14},{7,15},{8,0},{9,1},... | collective-permute-start | bytes 1179656 | tf_op jit(solution)/shard_map/ppermute | solution.py:231
  58.7 0.2 collective-permute-done.17.across
  58.9 4.8 %expert.7 = (f32[96,2048]{1,0:T(8,128)S(1)}, bf16[96,2048]{1,0:T(8,128)(2,1)S(1)}) custom-call(bf16[96,2048]{1,0:T(8,128)(2,1)S(1)} %collective-permute-done.16.own, bf16[96,2048]{1,0:T(8,128)(2,1)S(1)} %collective-permute-done.17.across, bf16[2048,1024]{1,0:T(8,128)(2,1)S(1)} %bitcast.34, bf16[1024,2048]{1,0:T(8,128)(2,1)S(1)} %bitcast.39, ...), custom_call_target="tpu_custom_call" | custom-call | flops 3221225472 | bytes 16777216 | tf_op jit(solution)/shard_map/expert/pallas_call | solution.py:141
  63.7 0.8 collective-permute-start.18
  64.5 2.8 %collective-permute-done.13 = bf16[96,2048]{1,0:T(8,128)(2,1)S(1)} collective-permute-done((bf16[96,2048]{1,0:T(8,128)(2,1)S(1)}, bf16[96,2048]{1,0:T(8,128)(2,1)S(1)}, u32[]{:S(2)}, u32[]{:S(2)}) %collective-permute-start.13) | collective-permute-done | bytes 393248 | tf_op jit(solution)/shard_map/ppermute | solution.py:219
  67.3 0.1 add_convert_fusion.2
  67.4 3.5 %collective-permute-start.14 = (bf16[96,2048]{1,0:T(8,128)(2,1)S(1)}, bf16[96,2048]{1,0:T(8,128)(2,1)S(1)}, u32[]{:S(2)}, u32[]{:S(2)}) collective-permute-start(bf16[96,2048]{1,0:T(8,128)(2,1)S(1)} %add_convert_fusion.2), channel_id=1, source_target_pairs={{0,4},{1,5},{2,6},{3,7},{4,0},{5,1},{6,2},{7,3},{8,12},{9,13},{10,... | collective-permute-start | bytes 1179656 | tf_op jit(solution)/shard_map/ppermute | solution.py:231
  70.9 4.9 %collective-permute-done.18 = bf16[96,2048]{1,0:T(8,128)(2,1)S(1)} collective-permute-done((bf16[96,2048]{1,0:T(8,128)(2,1)S(1)}, bf16[96,2048]{1,0:T(8,128)(2,1)S(1)}, u32[]{:S(2)}, u32[]{:S(2)}) %collective-permute-start.18) | collective-permute-done | bytes 393248 | tf_op jit(solution)/shard_map/ppermute | solution.py:219
  75.8 0.1 add_convert_fusion
  75.9 5.6 %collective-permute-start.19 = (bf16[96,2048]{1,0:T(8,128)(2,1)S(1)}, bf16[96,2048]{1,0:T(8,128)(2,1)S(1)}, u32[]{:S(2)}, u32[]{:S(2)}) collective-permute-start(bf16[96,2048]{1,0:T(8,128)(2,1)S(1)} %add_convert_fusion), channel_id=1, source_target_pairs={{0,12},{1,13},{2,14},{3,15},{4,8},{5,9},{6,10},{7,11},{8,4},{9,5},... | collective-permute-start | bytes 1179656 | tf_op jit(solution)/shard_map/ppermute | solution.py:231
  81.5 12.1 %collective-permute-start.20 = (bf16[48,2048]{1,0:T(8,128)(2,1)S(1)}, bf16[48,2048]{1,0:T(8,128)(2,1)S(1)}, u32[]{:S(2)}, u32[]{:S(2)}) collective-permute-start(bf16[48,2048]{1,0:T(8,128)(2,1)S(1)} %slice_bitcast_fusion.3), channel_id=1, source_target_pairs={{0,16},{16,0},{1,17},{17,1},{2,18},{18,2},{3,19},{19,3},{4,20},{20... | collective-permute-start | bytes 589832 | tf_op jit(solution)/shard_map/ppermute | solution.py:216
  93.7 0.1 collective-permute-start.21
  93.8 0.9 collective-permute-start.22
  94.8 4.8 %collective-permute-start.23 = (bf16[48,2048]{1,0:T(8,128)(2,1)S(1)}, bf16[48,2048]{1,0:T(8,128)(2,1)S(1)}, u32[]{:S(2)}, u32[]{:S(2)}) collective-permute-start(bf16[48,2048]{1,0:T(8,128)(2,1)S(1)} %slice_bitcast_fusion), channel_id=1, source_target_pairs={{0,16},{16,0},{1,17},{17,1},{2,18},{18,2},{3,19},{19,3},{4,20},{20... | collective-permute-start | bytes 589832 | tf_op jit(solution)/shard_map/ppermute | solution.py:216
  99.6 1.1 collective-permute-done.23.refs_7_
  100.7 1.9 %shard_map.95 = (bf16[128,2048]{1,0:T(8,128)(2,1)}, f32[32,128]{1,0:T(8,128)S(1)}) custom-call(bf16[96,2048]{1,0:T(8,128)(2,1)S(1)} %add_convert_fusion.3.refs_0_, bf16[96,2048]{1,0:T(8,128)(2,1)S(1)} %collective-permute-done.14.refs_1_, bf16[96,2048]{1,0:T(8,128)(2,1)S(1)} %collective-permute-done.15.refs_2_, ...), custom_call_target="tpu_custom_call" | custom-call | tf_op jit(solution)/shard_map/pallas_call | solution.py:344
  102.6 11.9 %all_to_all.9 = f32[32,1,128]{2,1,0:T(1,128)S(1)} all-to-all(f32[32,1,128]{2,1,0:T(1,128)S(1)} %bitcast.49), channel_id=1, replica_groups=mesh['section'=2,'expert'=16] {'section','expert'}, dimensions={0} | all-to-all | bytes 32768 | tf_op jit(solution)/shard_map/all_to_all | solution.py:361
  114.5 0.1 slice_divide_fusion
  114.6 0.5 add_bitcast_fusion
  (37 shorter events, 0.3 us)
Async XLA Ops:
  0.6 1.0 copy-start.2
  0.6 1.0 copy-start.6
  0.7 1.0 copy-start.5
  0.7 1.0 copy-start.4
  0.7 2.4 %copy-start = (bf16[1,2048,1024]{2,1,0:T(8,128)(2,1)S(1)}, bf16[1,2048,1024]{2,1,0:T(8,128)(2,1)}, u32[]{:S(2)}) copy-start(bf16[1,2048,1024]{2,1,0:T(8,128)(2,1)} %param.12) | copy-start | bytes 12582916
  0.7 2.3 %collective-permute-start = (bf16[128,2048]{1,0:T(8,128)(2,1)}, bf16[128,2048]{1,0:T(8,128)(2,1)S(1)}, u32[]{:S(2)}, u32[]{:S(2)}) collective-permute-start(bf16[128,2048]{1,0:T(8,128)(2,1)} %bitcast.41), channel_id=1, source_target_pairs={{0,16},{16,0},{1,17},{17,1},{2,18},{18,2},{3,19},{19,3},{4,20},{20... | collective-permute-start | bytes 1572872 | tf_op jit(solution)/shard_map/ppermute | solution.py:216
  1.2 1.7 %collective-permute-start.1 = (s32[2,128]{1,0:T(2,128)}, s32[2,128]{1,0:T(2,128)S(1)}, u32[]{:S(2)}, u32[]{:S(2)}) collective-permute-start(s32[2,128]{1,0:T(2,128)} %bitcast.51), channel_id=1, source_target_pairs={{0,16},{16,0},{1,17},{17,1},{2,18},{18,2},{3,19},{19,3},{4,20},{20... | collective-permute-start | bytes 3080 | tf_op jit(solution)/shard_map/ppermute | solution.py:216
  3.0 13.7 %collective-permute-start.4 = (bf16[2048,1024]{1,0:T(8,128)(2,1)S(1)}, bf16[2048,1024]{1,0:T(8,128)(2,1)S(1)}, u32[]{:S(2)}, u32[]{:S(2)}) collective-permute-start(bf16[2048,1024]{1,0:T(8,128)(2,1)S(1)} %bitcast.30), channel_id=1, source_target_pairs={{0,16},{16,0},{1,17},{17,1},{2,18},{18,2},{3,19},{19,3},{4,20},{20... | collective-permute-start | bytes 12582920 | tf_op jit(solution)/shard_map/ppermute | solution.py:216
  3.5 13.2 %collective-permute-start.5 = (bf16[1024,2048]{1,0:T(8,128)(2,1)}, bf16[1024,2048]{1,0:T(8,128)(2,1)S(1)}, u32[]{:S(2)}, u32[]{:S(2)}) collective-permute-start(bf16[1024,2048]{1,0:T(8,128)(2,1)} %bitcast.35), channel_id=1, source_target_pairs={{0,16},{16,0},{1,17},{17,1},{2,18},{18,2},{3,19},{19,3},{4,20},{20... | collective-permute-start | bytes 12582920 | tf_op jit(solution)/shard_map/ppermute | solution.py:216
  3.6 13.2 %copy-start.1 = (bf16[1,1024,2048]{2,1,0:T(8,128)(2,1)S(1)}, bf16[1,1024,2048]{2,1,0:T(8,128)(2,1)}, u32[]{:S(2)}) copy-start(bf16[1,1024,2048]{2,1,0:T(8,128)(2,1)} %param.13) | copy-start | bytes 12582916
  4.9 5.3 %collective-permute-start.2 = (bf16[96,2048]{1,0:T(8,128)(2,1)S(1)}, bf16[96,2048]{1,0:T(8,128)(2,1)S(1)}, u32[]{:S(2)}, u32[]{:S(2)}) collective-permute-start(bf16[96,2048]{1,0:T(8,128)(2,1)S(1)} %get-tuple-element.33), channel_id=1, source_target_pairs={{0,0},{1,1},{2,2},{3,3},{4,4},{5,5},{6,6},{7,7},{8,8},{9,9},{10,10... | collective-permute-start | bytes 1179656 | tf_op jit(solution)/shard_map/ppermute | solution.py:231
  5.6 11.1 %collective-permute-start.3 = (bf16[96,2048]{1,0:T(8,128)(2,1)S(1)}, bf16[96,2048]{1,0:T(8,128)(2,1)S(1)}, u32[]{:S(2)}, u32[]{:S(2)}) collective-permute-start(bf16[96,2048]{1,0:T(8,128)(2,1)S(1)} %get-tuple-element.33), channel_id=1, source_target_pairs={{0,1},{1,0},{2,3},{3,2},{4,5},{5,4},{6,7},{7,6},{8,9},{9,8},{10,11... | collective-permute-start | bytes 1179656 | tf_op jit(solution)/shard_map/ppermute | solution.py:231
  8.6 14.0 %collective-permute-start.8 = (bf16[96,2048]{1,0:T(8,128)(2,1)S(1)}, bf16[96,2048]{1,0:T(8,128)(2,1)S(1)}, u32[]{:S(2)}, u32[]{:S(2)}) collective-permute-start(bf16[96,2048]{1,0:T(8,128)(2,1)S(1)} %get-tuple-element.38), channel_id=1, source_target_pairs={{0,4},{1,5},{2,6},{3,7},{4,0},{5,1},{6,2},{7,3},{8,12},{9,13},{10,... | collective-permute-start | bytes 1179656 | tf_op jit(solution)/shard_map/ppermute | solution.py:231
  10.2 14.1 %collective-permute-start.10 = (bf16[96,2048]{1,0:T(8,128)(2,1)S(1)}, bf16[96,2048]{1,0:T(8,128)(2,1)S(1)}, u32[]{:S(2)}, u32[]{:S(2)}) collective-permute-start(bf16[96,2048]{1,0:T(8,128)(2,1)S(1)} %get-tuple-element.42), channel_id=1, source_target_pairs={{0,8},{1,9},{2,10},{3,11},{4,12},{5,13},{6,14},{7,15},{8,0},{9,1},... | collective-permute-start | bytes 1179656 | tf_op jit(solution)/shard_map/ppermute | solution.py:231
  22.6 8.2 %collective-permute-start.9 = (bf16[96,2048]{1,0:T(8,128)(2,1)S(1)}, bf16[96,2048]{1,0:T(8,128)(2,1)S(1)}, u32[]{:S(2)}, u32[]{:S(2)}) collective-permute-start(bf16[96,2048]{1,0:T(8,128)(2,1)S(1)} %collective-permute-done.8.own), channel_id=1, source_target_pairs={{0,1},{1,0},{2,3},{3,2},{4,5},{5,4},{6,7},{7,6},{8,9},{9,8},{10,11... | collective-permute-start | bytes 1179656 | tf_op jit(solution)/shard_map/ppermute | solution.py:219
  24.2 11.4 %collective-permute-start.11 = (bf16[96,2048]{1,0:T(8,128)(2,1)S(1)}, bf16[96,2048]{1,0:T(8,128)(2,1)S(1)}, u32[]{:S(2)}, u32[]{:S(2)}) collective-permute-start(bf16[96,2048]{1,0:T(8,128)(2,1)S(1)} %collective-permute-done.10.own), channel_id=1, source_target_pairs={{0,1},{1,0},{2,3},{3,2},{4,5},{5,4},{6,7},{7,6},{8,9},{9,8},{10,11... | collective-permute-start | bytes 1179656 | tf_op jit(solution)/shard_map/ppermute | solution.py:219
  24.6 17.0 %collective-permute-start.16 = (bf16[96,2048]{1,0:T(8,128)(2,1)S(1)}, bf16[96,2048]{1,0:T(8,128)(2,1)S(1)}, u32[]{:S(2)}, u32[]{:S(2)}) collective-permute-start(bf16[96,2048]{1,0:T(8,128)(2,1)S(1)} %get-tuple-element.47), channel_id=1, source_target_pairs={{0,12},{1,13},{2,14},{3,15},{4,8},{5,9},{6,10},{7,11},{8,4},{9,5},... | collective-permute-start | bytes 1179656 | tf_op jit(solution)/shard_map/ppermute | solution.py:231
  28.9 14.1 %collective-permute-start.7 = (bf16[96,2048]{1,0:T(8,128)(2,1)S(1)}, bf16[96,2048]{1,0:T(8,128)(2,1)S(1)}, u32[]{:S(2)}, u32[]{:S(2)}) collective-permute-start(bf16[96,2048]{1,0:T(8,128)(2,1)S(1)} %get-tuple-element.37), channel_id=1, source_target_pairs={{0,1},{1,0},{2,3},{3,2},{4,5},{5,4},{6,7},{7,6},{8,9},{9,8},{10,11... | collective-permute-start | bytes 1179656 | tf_op jit(solution)/shard_map/ppermute | solution.py:231
  30.0 13.1 %collective-permute-start.6 = (bf16[96,2048]{1,0:T(8,128)(2,1)S(1)}, bf16[96,2048]{1,0:T(8,128)(2,1)S(1)}, u32[]{:S(2)}, u32[]{:S(2)}) collective-permute-start(bf16[96,2048]{1,0:T(8,128)(2,1)S(1)} %convert_element_type.30), channel_id=1, source_target_pairs={{0,0},{1,1},{2,2},{3,3},{4,4},{5,5},{6,6},{7,7},{8,8},{9,9},{10,10... | collective-permute-start | bytes 1179656 | tf_op jit(solution)/shard_map/ppermute | solution.py:231
  40.5 10.0 %collective-permute-start.12 = (bf16[96,2048]{1,0:T(8,128)(2,1)S(1)}, bf16[96,2048]{1,0:T(8,128)(2,1)S(1)}, u32[]{:S(2)}, u32[]{:S(2)}) collective-permute-start(bf16[96,2048]{1,0:T(8,128)(2,1)S(1)} %get-tuple-element.44), channel_id=1, source_target_pairs={{0,1},{1,0},{2,3},{3,2},{4,5},{5,4},{6,7},{7,6},{8,9},{9,8},{10,11... | collective-permute-start | bytes 1179656 | tf_op jit(solution)/shard_map/ppermute | solution.py:219
  41.7 17.2 %collective-permute-start.17 = (bf16[96,2048]{1,0:T(8,128)(2,1)S(1)}, bf16[96,2048]{1,0:T(8,128)(2,1)S(1)}, u32[]{:S(2)}, u32[]{:S(2)}) collective-permute-start(bf16[96,2048]{1,0:T(8,128)(2,1)S(1)} %collective-permute-done.16.own), channel_id=1, source_target_pairs={{0,1},{1,0},{2,3},{3,2},{4,5},{5,4},{6,7},{7,6},{8,9},{9,8},{10,11... | collective-permute-start | bytes 1179656 | tf_op jit(solution)/shard_map/ppermute | solution.py:219
  50.5 16.9 %collective-permute-start.13 = (bf16[96,2048]{1,0:T(8,128)(2,1)S(1)}, bf16[96,2048]{1,0:T(8,128)(2,1)S(1)}, u32[]{:S(2)}, u32[]{:S(2)}) collective-permute-start(bf16[96,2048]{1,0:T(8,128)(2,1)S(1)} %get-tuple-element.45), channel_id=1, source_target_pairs={{0,1},{1,0},{2,3},{3,2},{4,5},{5,4},{6,7},{7,6},{8,9},{9,8},{10,11... | collective-permute-start | bytes 1179656 | tf_op jit(solution)/shard_map/ppermute | solution.py:219
  51.3 42.3 %collective-permute-start.15 = (bf16[96,2048]{1,0:T(8,128)(2,1)S(1)}, bf16[96,2048]{1,0:T(8,128)(2,1)S(1)}, u32[]{:S(2)}, u32[]{:S(2)}) collective-permute-start(bf16[96,2048]{1,0:T(8,128)(2,1)S(1)} %add_convert_fusion.1), channel_id=1, source_target_pairs={{0,8},{1,9},{2,10},{3,11},{4,12},{5,13},{6,14},{7,15},{8,0},{9,1},... | collective-permute-start | bytes 1179656 | tf_op jit(solution)/shard_map/ppermute | solution.py:231
  63.7 37.0 %copy-start.3 = (bf16[1,128,2048]{2,1,0:T(8,128)(2,1)S(1)}, bf16[1,128,2048]{2,1,0:T(8,128)(2,1)}, u32[]{:S(2)}) copy-start(bf16[1,128,2048]{2,1,0:T(8,128)(2,1)} %param.9) | copy-start | bytes 1572868
  63.7 37.0 %copy-start.7 = (s32[1,128]{1,0:T(1,128)S(1)}, s32[1,128]{1,0:T(1,128)}, u32[]{:S(2)}) copy-start(s32[1,128]{1,0:T(1,128)} %refs_11_.1) | copy-start | bytes 1540
  63.7 12.1 %collective-permute-start.18 = (bf16[96,2048]{1,0:T(8,128)(2,1)S(1)}, bf16[96,2048]{1,0:T(8,128)(2,1)S(1)}, u32[]{:S(2)}, u32[]{:S(2)}) collective-permute-start(bf16[96,2048]{1,0:T(8,128)(2,1)S(1)} %get-tuple-element.51), channel_id=1, source_target_pairs={{0,1},{1,0},{2,3},{3,2},{4,5},{5,4},{6,7},{7,6},{8,9},{9,8},{10,11... | collective-permute-start | bytes 1179656 | tf_op jit(solution)/shard_map/ppermute | solution.py:219
  67.4 26.4 %collective-permute-start.14 = (bf16[96,2048]{1,0:T(8,128)(2,1)S(1)}, bf16[96,2048]{1,0:T(8,128)(2,1)S(1)}, u32[]{:S(2)}, u32[]{:S(2)}) collective-permute-start(bf16[96,2048]{1,0:T(8,128)(2,1)S(1)} %add_convert_fusion.2), channel_id=1, source_target_pairs={{0,4},{1,5},{2,6},{3,7},{4,0},{5,1},{6,2},{7,3},{8,12},{9,13},{10,... | collective-permute-start | bytes 1179656 | tf_op jit(solution)/shard_map/ppermute | solution.py:231
  75.9 18.8 %collective-permute-start.19 = (bf16[96,2048]{1,0:T(8,128)(2,1)S(1)}, bf16[96,2048]{1,0:T(8,128)(2,1)S(1)}, u32[]{:S(2)}, u32[]{:S(2)}) collective-permute-start(bf16[96,2048]{1,0:T(8,128)(2,1)S(1)} %add_convert_fusion), channel_id=1, source_target_pairs={{0,12},{1,13},{2,14},{3,15},{4,8},{5,9},{6,10},{7,11},{8,4},{9,5},... | collective-permute-start | bytes 1179656 | tf_op jit(solution)/shard_map/ppermute | solution.py:231
  81.5 18.1 %collective-permute-start.20 = (bf16[48,2048]{1,0:T(8,128)(2,1)S(1)}, bf16[48,2048]{1,0:T(8,128)(2,1)S(1)}, u32[]{:S(2)}, u32[]{:S(2)}) collective-permute-start(bf16[48,2048]{1,0:T(8,128)(2,1)S(1)} %slice_bitcast_fusion.3), channel_id=1, source_target_pairs={{0,16},{16,0},{1,17},{17,1},{2,18},{18,2},{3,19},{19,3},{4,20},{20... | collective-permute-start | bytes 589832 | tf_op jit(solution)/shard_map/ppermute | solution.py:216
  93.7 5.9 %collective-permute-start.21 = (bf16[48,2048]{1,0:T(8,128)(2,1)S(1)}, bf16[48,2048]{1,0:T(8,128)(2,1)S(1)}, u32[]{:S(2)}, u32[]{:S(2)}) collective-permute-start(bf16[48,2048]{1,0:T(8,128)(2,1)S(1)} %slice_bitcast_fusion.2), channel_id=1, source_target_pairs={{0,16},{16,0},{1,17},{17,1},{2,18},{18,2},{3,19},{19,3},{4,20},{20... | collective-permute-start | bytes 589832 | tf_op jit(solution)/shard_map/ppermute | solution.py:216
  93.8 5.8 %collective-permute-start.22 = (bf16[48,2048]{1,0:T(8,128)(2,1)S(1)}, bf16[48,2048]{1,0:T(8,128)(2,1)S(1)}, u32[]{:S(2)}, u32[]{:S(2)}) collective-permute-start(bf16[48,2048]{1,0:T(8,128)(2,1)S(1)} %slice_bitcast_fusion.1), channel_id=1, source_target_pairs={{0,16},{16,0},{1,17},{17,1},{2,18},{18,2},{3,19},{19,3},{4,20},{20... | collective-permute-start | bytes 589832 | tf_op jit(solution)/shard_map/ppermute | solution.py:216
  94.8 5.9 %collective-permute-start.23 = (bf16[48,2048]{1,0:T(8,128)(2,1)S(1)}, bf16[48,2048]{1,0:T(8,128)(2,1)S(1)}, u32[]{:S(2)}, u32[]{:S(2)}) collective-permute-start(bf16[48,2048]{1,0:T(8,128)(2,1)S(1)} %slice_bitcast_fusion), channel_id=1, source_target_pairs={{0,16},{16,0},{1,17},{17,1},{2,18},{18,2},{3,19},{19,3},{4,20},{20... | collective-permute-start | bytes 589832 | tf_op jit(solution)/shard_map/ppermute | solution.py:216
